TPU v7x, 512 devices: a whole 4x8x8 slice. The times are simulated.
512 devices in a mesh: dp: 8 (over z), tensor: 8 (over y), factor: 8 (over x, core).
Axes of the slice: x: 4, y: 8, z: 8, core: 2. Of those that a mesh axis runs over, the one named last changes fastest.
Arguments:
- resid: bfloat16 [4096, 8192], P('dp', ('tensor', 'factor')), may hold values from -60 to 60
- norm_gain: bfloat16 [8192], P(('tensor', 'factor')), may hold values from 0.5 to 1.5
- cotangent: bfloat16 [4096, 2, 64], P('dp'), may hold values from -0.059814453 to 0.059814453
- segment_ids: int32 [8, 512], P('dp'), may hold values from 0 to 1, never falling along the last dimension, each value on 1 to 511 neighbouring positions
- query_grads: bfloat16 [16, 2, 64, 8192], P('dp', None, None, ('tensor', 'factor')), may hold values from -0.011962891 to 0.011962891
- input_basis: bfloat16 [2, 8192, 8192], P(None, 'tensor', ('dp', 'factor')), may hold values from -0.0625 to 0.0625
- output_basis: bfloat16 [2, 64, 64], replicated, may hold values from -0.75 to 0.75
- eigenvalues: float32 [2, 64, 8192], P(None, None, ('dp', 'factor')), may hold values from 0.003 to 3
Outputs:
- scores: float32 [16, 16], replicated
Inputs may be any that keep to these rules, and one draw needn't show every extreme that they name: `segment_ids`: in each row ids never fall and every id appears; a candidate has at most 511 tokens.
All inputs are finite; a program needn't handle non-finite values.
Results may differ from a plain program's by a relative error of at most 0.005.
Values may be sent and summed in bfloat16 or wider, within the bound.
No kernel may reach another device: no remote copies, remote signals or barrier semaphores. Data moves between devices by JAX's collectives and lax.ppermute only.
A program may use at most 64 MiB of HBM per device.

v0:
```python
import jax
import jax.numpy as jnp
from jax import lax
from jax.sharding import PartitionSpec as P

D = 8192
R = 64
CAND_DEV = 2
Q_DEV = 2


def combine_rows(rotated, denominator, output_float):
    summed = lax.psum(rotated, "tensor")
    turned = jnp.einsum("mba,dnmbj->dnmaj", output_float, summed, precision=lax.Precision.HIGHEST)
    return (turned, denominator)


def body(
    resid, norm_gain, cotangent, segment_ids, query_grads, input_basis, output_basis, eigenvalues
):
    n_dp = lax.axis_size("dp")
    values = resid.astype(jnp.float32)
    squares = jnp.sum(values * values, axis=1)
    totals = lax.psum(squares, ("tensor", "factor"))
    normed = (
        values * lax.rsqrt(totals / D + 1e-05)[:, None] * norm_gain.astype(jnp.float32)
    ).astype(jnp.bfloat16)
    members = segment_ids[0]
    onehot = (members[None, :] == jnp.arange(CAND_DEV, dtype=jnp.int32)[:, None]).astype(
        jnp.bfloat16
    )
    weighted = onehot[:, :, None, None] * cotangent[None]
    grads = jnp.einsum(
        "stmb,ti->smbi", weighted, normed, preferred_element_type=jnp.float32
    ).astype(jnp.bfloat16)
    local_stack = jnp.concatenate([grads, query_grads], axis=0)
    eigen_sums = jnp.sum(eigenvalues, axis=(1, 2))
    eigen_total = lax.psum(eigen_sums, ("dp", "factor"))
    damping = 0.1 * eigen_total / (R * D)
    output_float = output_basis.astype(jnp.float32)
    block_rows = lax.all_gather(local_stack, "factor", axis=3, tiled=True)
    denominator = eigenvalues + damping[:, None, None]
    rotated = jnp.einsum(
        "unmbi,mij->unmbj",
        lax.all_gather(block_rows[None], "dp", axis=0, tiled=True),
        input_basis,
        preferred_element_type=jnp.float32,
    )
    turned, local_den = combine_rows(rotated, denominator, output_float)
    rank_rows = turned.shape[3]
    columns = turned.shape[4]
    candidates = turned[:, :CAND_DEV].reshape(n_dp * CAND_DEV, 2, rank_rows, columns)
    queries = turned[:, CAND_DEV:].reshape(n_dp * Q_DEV, 2, rank_rows, columns)
    weights = candidates / local_den[None]
    partial_scores = jnp.einsum("smaj,qmaj->sq", weights, queries, precision=lax.Precision.HIGHEST)
    scores = lax.psum(partial_scores, ("dp", "factor"))
    return scores


def solution(mesh):
    placed = (
        P("dp", ("tensor", "factor")),
        P(("tensor", "factor")),
        P("dp", None, None),
        P("dp", None),
        P("dp", None, None, ("tensor", "factor")),
        P(None, "tensor", ("dp", "factor")),
        P(),
        P(None, None, ("dp", "factor")),
    )
    return jax.shard_map(body, mesh=mesh, in_specs=placed, out_specs=P(), check_vma=False)
```

profile of v0, /device:TPU:1, one launch (start us, length us, event | category | flops | bytes accessed | tf_op | source)
XLA Modules:
  0.0 544.4 jit_solution(4920589733729840385)
XLA Ops:
  6.5 1.1 fusion.8
  7.7 130.3 %psum.28 = f32[512]{0:T(512)S(1)} all-reduce(f32[512]{0:T(512)S(1)} %fusion.8), channel_id=1, replica_groups=mesh['dp'=8,'tensor'=8,'factor'=8] {'tensor','factor'}, use_global_device_ids=true, to_apply=%region_1.0 | all-reduce | flops 512 | bytes 4096 | tf_op jit(solution)/shard_map/psum | solution.py:24
  137.9 0.7 compare_convert_fusion
  138.6 0.7 convert_element_type.22
  139.3 1.3 convolution_convert_fusion
  140.6 1.5 pad_maximum_fusion
  142.1 0.0 all-gather.4.cloned.1.call-update
  142.1 0.0 all-gather.6.cloned.1.call-start
  142.2 28.1 %all-gather.4.cloned.1.call-done = bf16[4,2,64,1024]{3,2,1,0:T(8,128)(2,1)} async-done(((bf16[4,2,64,128]{3,2,1,0:T(8,128)(2,1)}), bf16[4,2,64,1024]{3,2,1,0:T(8,128)(2,1)}) %all-gather.4.cloned.1.call-update) | async-done | bytes 1048592 | tf_op jit(solution)/shard_map/all_gather | solution.py:41
  170.2 0.0 all-gather.6.cloned.1.call-update
  170.2 0.0 all-reduce.2.cloned.1.call-start
  170.3 100.3 %all-gather.6.cloned.1.call-done = bf16[32,2,64,1024]{3,2,1,0:T(8,128)(2,1)} async-done(((bf16[4,2,64,1024]{3,2,1,0:T(8,128)(2,1)}), bf16[32,2,64,1024]{3,2,1,0:T(8,128)(2,1)}) %all-gather.6.cloned.1.call-update) | async-done | bytes 8388624 | tf_op jit(solution)/shard_map/all_gather | solution.py:45
  270.6 7.1 %fusion.2 = f32[8,4,2,64,128]{4,3,1,0,2:T(8,128)} fusion(bf16[8,4,2,64,1024]{4,3,2,1,0:T(8,128)(2,1)} %bitcast.31, bf16[2,1024,128]{2,1,0:T(8,128)(2,1)S(1)} %copy-done), kind=kOutput, calls=%fused_computation.3 | convolution fusion | flops 1073741824 | bytes 11010048 | tf_op jit(solution)/shard_map/unmbi,mij->unmbj/dot_general | solution.py:43
  277.7 0.0 all-reduce.2.cloned.1.call-update
  277.7 0.8 copy-done.1
  278.5 0.1 reduce_sum.19
  278.6 124.1 %psum.30 = f32[2]{0:T(128)S(1)} all-reduce(f32[2]{0:T(128)S(1)} %reduce_sum.19), channel_id=1, replica_groups=mesh['dp'=8,'tensor'=8,'factor'=8] {'dp','factor'}, use_global_device_ids=true, to_apply=%region_4.0 | all-reduce | flops 2 | bytes 16 | tf_op jit(solution)/shard_map/psum | solution.py:38
  402.7 0.1 broadcast_add_fusion
  402.8 0.1 copy.14
  402.8 0.0 all-reduce.2.cloned.1.call-done
  402.9 2.7 convolution_bitcast_fusion
  405.6 0.2 fusion.19
  405.8 2.6 convolution_bitcast_fusion.1
  408.4 129.5 %psum.31 = f32[16,16]{1,0:T(8,128)} all-reduce(f32[16,16]{1,0:T(8,128)S(1)} %convolution_bitcast_fusion.1), channel_id=1, replica_groups=mesh['dp'=8,'tensor'=8,'factor'=8] {'dp','factor'}, use_global_device_ids=true, to_apply=%region_5.0 | all-reduce | flops 256 | bytes 2048 | tf_op jit(solution)/shard_map/psum | solution.py:56
  (8 shorter events, 0.0 us)
Async XLA Ops:
  6.5 264.0 %copy-start = (bf16[2,1024,128]{2,1,0:T(8,128)(2,1)S(1)}, bf16[2,1024,128]{2,1,0:T(8,128)(2,1)}, u32[]{:S(2)}) copy-start(bf16[2,1024,128]{2,1,0:T(8,128)(2,1)} %param.13) | copy-start | bytes 1572868
  6.5 163.7 %all-gather.4.cloned.1.call-start = ((), (), s32[]{:S(2)}) async-start(), calls=%async_computation | async-start | bytes 1179648 | tf_op jit(solution)/shard_map/all_gather | solution.py:41
  142.1 128.4 %all-gather.6.cloned.1.call-start = ((), (), s32[]{:S(2)}) async-start(), calls=%async_computation.2 | async-start | bytes 9437184 | tf_op jit(solution)/shard_map/all_gather | solution.py:45
  170.2 232.6 %all-reduce.2.cloned.1.call-start = ((), (), s32[]{:S(2)}) async-start(), calls=%async_computation.1 | async-start | bytes 4194304 | tf_op jit(solution)/shard_map/psum | solution.py:13
  277.7 0.8 copy-start.1
  277.7 125.2 %copy-start.2 = (bf16[2,64,64]{2,1,0:T(8,128)(2,1)S(1)}, bf16[2,64,64]{2,1,0:T(8,128)(2,1)}, u32[]{:S(2)}) copy-start(bf16[2,64,64]{2,1,0:T(8,128)(2,1)} %param.14) | copy-start | bytes 49156
Sparse Core Ops, SparseCore 0:
  142.2 27.9 all-gather.3
  172.3 98.2 all-gather.5
  277.8 82.3 all-reduce.1
where the time goes:
time: 545 us; the launch traced here: 544 us
  blocking collectives  384 us (70%)
  waiting for transfers between devices  128 us (23%)
  matrix products  13.7 us (3%)
  between operations  13.2 us (2%)
    psum x1, blocking collectives, body(): totals = lax.psum(squares, ('tensor', 'factor'))  130 us
    psum x1, blocking collectives, body(): scores = lax.psum(partial_scores, ('dp', 'factor'))  129 us
    psum x1, blocking collectives, body(): eigen_total = lax.psum(eigen_sums, ('dp', 'factor'))  124 us
    all_gather x1, waiting for transfers between devices, body(): lax.all_gather(block_rows[None], 'dp', axis=0, tiled=True)  100 us
    all_gather x1, waiting for transfers between devices, body(): block_rows = lax.all_gather(local_stack, 'factor', axis=3, tiled=True)  28.1 us
  transfers between devices with their start and end apart: 3, of which 2 were waited for; matrix products, arithmetic and copies ran while one was open for 0% of the time, Pallas kernels for 0%

commit v1 on v0

v1 whole, which is shorter than its diff:
```python
import jax
import jax.numpy as jnp
from jax import lax
from jax.sharding import Mesh, PartitionSpec as P

D = 8192
R = 64
MODULES = 2
CAND_DEV = 2
Q_DEV = 2
STACK = CAND_DEV + Q_DEV
FACTOR = ("x", "core")
GROUPS = 8
A_ROWS = MODULES * R // GROUPS


def split_three(value):
    high = value.astype(jnp.bfloat16)
    rest = value - high.astype(jnp.float32)
    middle = rest.astype(jnp.bfloat16)
    low = (rest - middle.astype(jnp.float32)).astype(jnp.bfloat16)
    return jnp.stack([high, middle, low])


def body(
    resid, norm_gain, cotangent, segment_ids, query_grads, input_basis, output_basis, eigenvalues
):
    n_dp = lax.axis_size("dp")
    n_t = lax.axis_size("tensor")
    t = lax.axis_index("tensor")
    group = lax.axis_index(FACTOR)
    tokens, width = resid.shape

    basis = lax.all_gather(input_basis, FACTOR, axis=0)

    values = resid.astype(jnp.float32)
    squares = jnp.sum(values * values, axis=1)
    per_t = A_ROWS // n_t
    eigen_part = lax.dynamic_index_in_dim(
        eigenvalues.reshape(GROUPS, n_t, per_t * width), t, axis=1, keepdims=False
    )
    parcel = jnp.concatenate(
        [
            jnp.broadcast_to(squares, (n_t, GROUPS, tokens)),
            jnp.broadcast_to(eigen_part, (n_t, GROUPS, per_t * width)),
        ],
        axis=2,
    ).reshape(n_t * GROUPS, 1, tokens + per_t * width)
    parcel = lax.all_to_all(parcel, ("tensor",) + FACTOR, 0, 0, tiled=True)
    totals = jnp.sum(parcel[:, 0, :tokens], axis=0)
    eigen = lax.dynamic_index_in_dim(
        parcel.reshape(n_t, GROUPS, tokens + per_t * width)[:, :, tokens:], t, axis=1, keepdims=False
    ).reshape(A_ROWS, width)

    normed = (
        values * lax.rsqrt(totals / D + 1e-05)[:, None] * norm_gain.astype(jnp.float32)
    ).astype(jnp.bfloat16)
    onehot = (
        segment_ids[0][None, :] == jnp.arange(CAND_DEV, dtype=jnp.int32)[:, None]
    ).astype(jnp.bfloat16)
    weighted = onehot[:, :, None, None] * cotangent[None]
    grads = jnp.einsum(
        "stmb,ti->smbi", weighted, normed, preferred_element_type=jnp.float32
    ).astype(jnp.bfloat16)
    stack = jnp.concatenate([grads, query_grads], axis=0)
    turned = jnp.einsum(
        "mba,nmbi->mani", output_basis, stack, preferred_element_type=jnp.float32
    ).astype(jnp.bfloat16)
    turned = turned.reshape(GROUPS, A_ROWS * STACK, width)
    eigen_sums = split_three(jnp.sum(eigenvalues, axis=(1, 2)))
    extra = jnp.zeros((8, width), jnp.bfloat16).at[:3, :MODULES].set(eigen_sums)
    rows = jnp.concatenate(
        [turned, jnp.broadcast_to(extra, (GROUPS, 8, width))], axis=1
    )
    rows = jnp.broadcast_to(rows, (n_dp,) + rows.shape).reshape((n_dp * GROUPS,) + rows.shape[1:])
    rows = lax.all_to_all(rows, ("dp",) + FACTOR, 0, 0, tiled=True)
    sums = jnp.sum(rows[:, A_ROWS * STACK : A_ROWS * STACK + 3, :MODULES].astype(jnp.float32), axis=(0, 1))
    damping = 0.1 * sums / (R * D)
    rows = rows[:, : A_ROWS * STACK].reshape(n_dp, GROUPS, A_ROWS * STACK, width)

    module = group // (GROUPS // MODULES)
    mine = lax.dynamic_index_in_dim(basis, module, axis=1, keepdims=False)
    mine = mine.reshape(GROUPS, GROUPS, width, mine.shape[-1])
    partial = jnp.einsum(
        "dfrk,hfkj->hdrj", rows, mine, preferred_element_type=jnp.float32
    ).astype(jnp.bfloat16)
    columns = partial.shape[-1]
    partial = partial.reshape(GROUPS, n_dp * A_ROWS * STACK, columns)
    partial = lax.all_to_all(partial, "tensor", 0, 0, tiled=True)
    rotated = jnp.sum(partial.astype(jnp.float32), axis=0)
    rotated = rotated.reshape(n_dp, A_ROWS, STACK, columns)

    weight = 1.0 / (eigen + lax.dynamic_index_in_dim(damping, module, keepdims=False))
    candidates = rotated[:, :, :CAND_DEV] * weight[None, :, None, :]
    queries = rotated[:, :, CAND_DEV:]
    scores = jnp.einsum(
        "dasj,eaqj->dseq", candidates, queries, precision=lax.Precision.HIGHEST
    ).reshape(2, -1)
    scores = lax.psum(scores, "core")
    peers = n_dp * n_t * lax.axis_size("x")
    scores = jnp.broadcast_to(scores, (peers,) + scores.shape)
    scores = lax.all_to_all(scores, ("dp", "tensor", "x"), 0, 0, tiled=True)
    return jnp.sum(scores, axis=0).reshape(n_dp * CAND_DEV, n_dp * Q_DEV)


def solution(mesh):
    n_dp, n_t, n_f = (mesh.shape[name] for name in ("dp", "tensor", "factor"))
    fine = Mesh(mesh.devices.reshape(n_dp, n_t, n_f // 2, 2), ("dp", "tensor", "x", "core"))
    placed = (
        P("dp", ("tensor", "x", "core")),
        P(("tensor", "x", "core")),
        P("dp", None, None),
        P("dp", None),
        P("dp", None, None, ("tensor", "x", "core")),
        P(None, "tensor", ("dp", "x", "core")),
        P(),
        P(None, None, ("dp", "x", "core")),
    )
    return jax.shard_map(body, mesh=fine, in_specs=placed, out_specs=P(), check_vma=False)
```

time: 545 us -> 151 us (0.28)
  blocking collectives: 384 us -> 25.6 us
  waiting for transfers between devices: 128 us -> 68.7 us
  starting transfers between devices: 0.08 us -> 27.5 us
  matrix products: 13.7 us -> 3.79 us
  local copies, waits for them, and re-layouts: 1.11 us -> 6.62 us
    psum x3 -> x1, blocking collectives: 384 us -> 2.62 us  [body(): scores = lax.psum(scores, 'core')]
    all_gather x2 -> x1, waiting for transfers between devices: 128 us -> 0.02 us  [body(): basis = lax.all_gather(input_basis, FACTOR, axis=0)]
    all_to_all x0 -> x3, waiting for transfers between devices: none -> 68 us  [the longest x1 30.6 us: body(): rows = lax.all_to_all(rows, ('dp',) + FACTOR, 0, 0, tiled=True)]
    all_to_all x0 -> x3, starting transfers between devices: none -> 27.4 us  [the longest x1 12.3 us: body(): rows = lax.all_to_all(rows, ('dp',) + FACTOR, 0, 0, tiled=True)]
    all_to_all x0 -> x1, blocking collectives: none -> 23 us  [body(): scores = lax.all_to_all(scores, ('dp', 'tensor', 'x'), 0, 0, tiled=True)]
    dot_general x3, matrix products: 12.4 us -> 3.46 us  [the longest x1 2.25 us: body(): jnp.einsum('dfrk,hfkj->hdrj', rows, mine, preferred_element_type=jnp.floa...]
  transfers between devices with their start and end apart: 3 -> 4, of which waited for: 2 -> 3; matrix products, arithmetic and copies ran while one was open for 0% -> 6% of each run, Pallas kernels for 0% -> 0%
where the time goes in v1:
time: 151 us
  waiting for transfers between devices  68.7 us (45%)
  starting transfers between devices  27.5 us (18%)
  blocking collectives  25.6 us (17%)
  between operations  13.6 us (9%)
  local copies, waits for them, and re-layouts  6.62 us (4%)
  other arithmetic  4.82 us (3%)
  matrix products  3.79 us (3%)
    all_to_all x1, waiting for transfers between devices, body(): rows = lax.all_to_all(rows, ('dp',) + FACTOR, 0, 0, tiled=True)  30.6 us
    all_to_all x1, waiting for transfers between devices, body(): partial = lax.all_to_all(partial, 'tensor', 0, 0, tiled=True)  27.7 us
    all_to_all x1, blocking collectives, body(): scores = lax.all_to_all(scores, ('dp', 'tensor', 'x'), 0, 0, tiled=True)  23 us
    all_to_all x1, starting transfers between devices, body(): rows = lax.all_to_all(rows, ('dp',) + FACTOR, 0, 0, tiled=True)  12.3 us
    all_to_all x1, starting transfers between devices, body(): parcel = lax.all_to_all(parcel, ('tensor',) + FACTOR, 0, 0, tiled=True)  11.6 us
    all_to_all x1, waiting for transfers between devices, body(): parcel = lax.all_to_all(parcel, ('tensor',) + FACTOR, 0, 0, tiled=True)  9.71 us
    all_to_all x1, starting transfers between devices, body(): partial = lax.all_to_all(partial, 'tensor', 0, 0, tiled=True)  3.56 us
  transfers between devices with their start and end apart: 4, of which 3 were waited for; matrix products, arithmetic and copies ran while one was open for 6% of the time, Pallas kernels for 0%

profile of v1, /device:TPU:1, one launch (start us, length us, event | category | flops | bytes accessed | tf_op | source)
XLA Modules:
  0.0 150.6 jit_solution(325591531411314985)
XLA Ops:
  6.6 0.7 all-gather.3.cloned.1.call-update
  7.3 0.9 reshape.139
  8.2 1.1 fusion.1
  9.3 0.9 reshape.140
  10.2 11.6 %all-to-all-start = ((f32[64,1,768]{2,1,0:T(1,128)}), f32[64,1,768]{2,1,0:T(1,128)S(1)}, u32[]{:S(2)}, u32[]{:S(2)}) async-start(f32[64,1,768]{2,1,0:T(1,128)} %reshape.140), calls=%async_computation | async-start | bytes 393216 | tf_op jit(solution)/shard_map/all_to_all | solution.py:49
  21.8 0.9 reduce_sum.58
  22.7 0.7 convert_element_type.105
  23.4 0.7 compare_convert_fusion
  24.1 9.7 %all-to-all-done = f32[64,1,768]{2,1,0:T(1,128)S(1)} async-done(((f32[64,1,768]{2,1,0:T(1,128)}), f32[64,1,768]{2,1,0:T(1,128)S(1)}, u32[]{:S(2)}, u32[]{:S(2)}) %all-to-all-start) | async-done | bytes 196640 | tf_op jit(solution)/shard_map/all_to_all | solution.py:49
  33.9 0.3 convolution_convert_fusion.1
  34.7 1.2 broadcast_in_dim.25
  35.8 12.3 %all-to-all-start.1 = ((bf16[64,72,128]{2,1,0:T(8,128)(2,1)}), bf16[64,72,128]{2,1,0:T(8,128)(2,1)S(1)}, u32[]{:S(2)}, u32[]{:S(2)}) async-start(bf16[64,72,128]{2,1,0:T(8,128)(2,1)} %bitcast.10), calls=%async_computation.1 | async-start | bytes 2359296 | tf_op jit(solution)/shard_map/all_to_all | solution.py:76
  48.1 30.6 %all-to-all-done.1 = bf16[64,72,128]{2,1,0:T(8,128)(2,1)S(1)} async-done(((bf16[64,72,128]{2,1,0:T(8,128)(2,1)}), bf16[64,72,128]{2,1,0:T(8,128)(2,1)S(1)}, u32[]{:S(2)}, u32[]{:S(2)}) %all-to-all-start.1) | async-done | bytes 1179680 | tf_op jit(solution)/shard_map/all_to_all | solution.py:76
  78.9 1.8 %constant_dynamic-slice_fusion.1 = bf16[8,1,1024,128]{3,2,1,0:T(8,128)(2,1)S(1)} fusion(bf16[8,2,1024,128]{3,2,1,0:T(8,128)(2,1)} %bitcast.66, s32[]{:T(128)S(6)} %select_n.17), kind=kLoop, calls=%fused_computation.46 | loop fusion | bytes 4194308 | tf_op jit(solution)/shard_map/jit(dynamic_index_in_dim)/dynamic_slice | solution.py:82
  80.6 2.3 %bitcast_convert_fusion = bf16[8,128,8,64]{1,3,2,0:T(8,128)(2,1)} fusion(bf16[8,8,128,128,1]{3,2,1,4,0:T(8,128)(2,1)S(1)} %bitcast.64, bf16[8,8,64,128,1]{3,2,1,0,4:T(8,128)(2,1)S(1)} %bitcast.67), kind=kOutput, calls=%fused_computation | convolution fusion | flops 1074266112 | bytes 4194304 | tf_op jit(solution)/shard_map/dfrk,hfkj->hdrj/dot_general | solution.py:84
  82.9 3.6 %all-to-all-start.2 = ((bf16[8,512,128]{2,1,0:T(8,128)(2,1)}), bf16[8,512,128]{2,1,0:T(8,128)(2,1)S(1)}, u32[]{:S(2)}, u32[]{:S(2)}) async-start(bf16[8,512,128]{2,1,0:T(8,128)(2,1)} %bitcast.16), calls=%async_computation.2 | async-start | bytes 2097152 | tf_op jit(solution)/shard_map/all_to_all | solution.py:89
  86.6 0.6 dynamic_slice.18
  87.2 0.7 add_divide_fusion
  87.8 27.7 %all-to-all-done.2 = bf16[8,512,128]{2,1,0:T(8,128)(2,1)S(1)} async-done(((bf16[8,512,128]{2,1,0:T(8,128)(2,1)}), bf16[8,512,128]{2,1,0:T(8,128)(2,1)S(1)}, u32[]{:S(2)}, u32[]{:S(2)}) %all-to-all-start.2) | async-done | bytes 1048608 | tf_op jit(solution)/shard_map/all_to_all | solution.py:89
  115.8 1.0 convolution_bitcast_fusion
  117.1 2.6 %psum.7 = f32[2,128]{1,0:T(2,128)S(1)} all-reduce(f32[2,128]{1,0:T(2,128)S(1)} %reshape.147), channel_id=1, replica_groups=mesh['dp'=8,'tensor'=8,'x'=4,'core'=2] {'core'}, use_global_device_ids=true, to_apply=%region_5.6 | all-reduce | flops 256 | bytes 2048 | tf_op jit(solution)/shard_map/psum | solution.py:99
  119.8 23.0 %all_to_all.20 = f32[256,2,128]{2,1,0:T(2,128)S(1)} all-to-all(f32[256,2,128]{2,1,0:T(2,128)S(1)} %broadcast_in_dim.26), channel_id=1, replica_groups=mesh['dp'=8,'tensor'=8,'x'=4,'core'=2] {'dp','tensor','x'}, dimensions={0} | all-to-all | bytes 524288 | tf_op jit(solution)/shard_map/all_to_all | solution.py:102
  142.8 0.3 reduce_sum.62
  143.1 0.7 reshape.148
  (34 shorter events, 1.5 us)
Async XLA Ops:
  6.5 27.7 %copy-start = (bf16[2,64,64]{2,1,0:T(8,128)(2,1)S(1)}, bf16[2,64,64]{2,1,0:T(8,128)(2,1)}, u32[]{:S(2)}) copy-start(bf16[2,64,64]{2,1,0:T(8,128)(2,1)} %param.16) | copy-start | bytes 49156
  6.5 27.4 %copy-start.1 = (bf16[512,128]{1,0:T(8,128)(2,1)S(1)}, bf16[512,128]{1,0:T(8,128)(2,1)}, u32[]{:S(2)}) copy-start(bf16[512,128]{1,0:T(8,128)(2,1)} %param.10) | copy-start | bytes 393220
  6.5 27.4 %copy-start.2 = (bf16[512,2,64]{0,2,1:T(8,128)(2,1)S(1)}, bf16[512,2,64]{0,2,1:T(8,128)(2,1)}, u32[]{:S(2)}) copy-start(bf16[512,2,64]{0,2,1:T(8,128)(2,1)} %param.12) | copy-start | bytes 393220
  6.5 27.8 %copy-start.3 = (bf16[2,2,64,128]{3,2,1,0:T(8,128)(2,1)S(1)}, bf16[2,2,64,128]{3,2,1,0:T(8,128)(2,1)}, u32[]{:S(2)}) copy-start(bf16[2,2,64,128]{3,2,1,0:T(8,128)(2,1)} %param.14) | copy-start | bytes 196612
  6.5 72.3 %all-gather.3.cloned.1.call-start = ((), (), s32[]{:S(2)}) async-start(), calls=%async_computation.4 | async-start | bytes 4718592 | tf_op jit(solution)/shard_map/all_gather | solution.py:34
  10.2 23.7 %all-to-all-start = ((f32[64,1,768]{2,1,0:T(1,128)}), f32[64,1,768]{2,1,0:T(1,128)S(1)}, u32[]{:S(2)}, u32[]{:S(2)}) async-start(f32[64,1,768]{2,1,0:T(1,128)} %reshape.140), calls=%async_computation | async-start | bytes 393216 | tf_op jit(solution)/shard_map/all_to_all | solution.py:49
  35.8 42.9 %all-to-all-start.1 = ((bf16[64,72,128]{2,1,0:T(8,128)(2,1)}), bf16[64,72,128]{2,1,0:T(8,128)(2,1)S(1)}, u32[]{:S(2)}, u32[]{:S(2)}) async-start(bf16[64,72,128]{2,1,0:T(8,128)(2,1)} %bitcast.10), calls=%async_computation.1 | async-start | bytes 2359296 | tf_op jit(solution)/shard_map/all_to_all | solution.py:76
  82.9 32.7 %all-to-all-start.2 = ((bf16[8,512,128]{2,1,0:T(8,128)(2,1)}), bf16[8,512,128]{2,1,0:T(8,128)(2,1)S(1)}, u32[]{:S(2)}, u32[]{:S(2)}) async-start(bf16[8,512,128]{2,1,0:T(8,128)(2,1)} %bitcast.16), calls=%async_computation.2 | async-start | bytes 2097152 | tf_op jit(solution)/shard_map/all_to_all | solution.py:89
Sparse Core Ops, SparseCore 0:
  9.5 43.3 all-gather.2

commit v2 on v1

v2 whole, which is shorter than its diff:
```python
import jax
import jax.numpy as jnp
from jax import lax
from jax.sharding import Mesh, PartitionSpec as P

D = 8192
R = 64
MODULES = 2
CAND_DEV = 2
DP = ("zh", "zl")
FACTOR = ("x", "core")


def split_three(value):
    high = value.astype(jnp.bfloat16)
    rest = value - high.astype(jnp.float32)
    middle = rest.astype(jnp.bfloat16)
    low = (rest - middle.astype(jnp.float32)).astype(jnp.bfloat16)
    return jnp.stack([high, middle, low])


def everywhere(value, axes):
    peers = 1
    for axis in axes:
        peers *= lax.axis_size(axis)
    terms = jnp.broadcast_to(value, (peers,) + value.shape)
    return jnp.sum(lax.all_to_all(terms, axes, 0, 0, tiled=True), axis=0)


def body(
    resid, norm_gain, cotangent, segment_ids, query_grads, input_basis, output_basis, eigenvalues
):
    n_zh, n_zl = lax.axis_size("zh"), lax.axis_size("zl")
    n_t, n_x, n_c = lax.axis_size("tensor"), lax.axis_size("x"), lax.axis_size("core")
    n_dp, n_f = n_zh * n_zl, n_x * n_c
    module = lax.axis_index("zl")
    t = lax.axis_index("tensor")
    core = lax.axis_index("core")
    tokens, width = resid.shape
    a_rows = R // n_x
    rows_dev = a_rows * CAND_DEV

    basis = lax.all_gather(input_basis, ("zl", "x"), axis=0)

    swap = []
    for zl in range(n_zl):
        for tt in range(n_t):
            for x in range(n_x):
                source = ((tt // n_x) * n_t + zl * n_x + x) * n_x + tt % n_x
                swap.append((source, (zl * n_t + tt) * n_x + x))
    eigen_part = lax.dynamic_index_in_dim(
        eigenvalues.reshape(n_t, a_rows, width), t, axis=0, keepdims=False
    )
    eigen = lax.ppermute(eigen_part, ("zl", "tensor", "x"), swap)

    values = resid.astype(jnp.float32)
    squares = jnp.sum(values * values, axis=1)
    totals = everywhere(squares.reshape(-1, 128), ("tensor",) + FACTOR).reshape(-1)

    normed = (
        values * lax.rsqrt(totals / D + 1e-05)[:, None] * norm_gain.astype(jnp.float32)
    ).astype(jnp.bfloat16)
    onehot = (
        segment_ids[0][None, :] == jnp.arange(CAND_DEV, dtype=jnp.int32)[:, None]
    ).astype(jnp.bfloat16)
    weighted = onehot[:, :, None, None] * cotangent[None]
    grads = jnp.einsum(
        "stmb,ti->smbi", weighted, normed, preferred_element_type=jnp.float32
    ).astype(jnp.bfloat16)
    stack = jnp.stack([grads, query_grads])
    turned = jnp.einsum(
        "mbxa,hnmbi->mxhnai",
        output_basis.reshape(MODULES, R, n_x, a_rows),
        stack,
        preferred_element_type=jnp.float32,
    ).astype(jnp.bfloat16)
    turned = turned.reshape(MODULES, n_x, n_c, rows_dev, width)
    eigen_sums = split_three(jnp.sum(eigenvalues, axis=(1, 2)))
    extra = jnp.zeros((8, width), jnp.bfloat16).at[:3, :MODULES].set(eigen_sums)
    parcel = jnp.concatenate(
        [turned, jnp.broadcast_to(extra, (MODULES, n_x, n_c) + extra.shape)], axis=3
    )
    parcel = jnp.broadcast_to(parcel, (n_zh,) + parcel.shape)
    parcel = parcel.reshape((n_dp * n_f,) + parcel.shape[-2:])
    parcel = lax.all_to_all(parcel, DP + FACTOR, 0, 0, tiled=True)
    sums = jnp.sum(parcel[:, rows_dev : rows_dev + 3, :MODULES].astype(jnp.float32), axis=(0, 1))
    damping = 0.1 * sums / (R * D)

    mine = parcel[:, :rows_dev]
    other = lax.ppermute(mine, "core", [(0, 1), (1, 0)])
    blocks = lax.dynamic_index_in_dim(basis, module, axis=1, keepdims=False)
    blocks = blocks.reshape(n_t, n_f, width, blocks.shape[-1])

    def rotate(rows):
        return jnp.einsum(
            "dfrk,hfkj->hdrj",
            rows.reshape(n_dp, n_f, rows_dev, width),
            blocks,
            preferred_element_type=jnp.float32,
        ).astype(jnp.bfloat16)

    partial = jnp.stack([rotate(mine), rotate(other)], axis=1)
    partial = partial.reshape(n_t, 2 * n_dp * rows_dev, -1)
    partial = lax.all_to_all(partial, "tensor", 0, 0, tiled=True)
    rotated = jnp.sum(partial.astype(jnp.float32), axis=0)
    rotated = rotated.reshape(2, n_dp * CAND_DEV, a_rows, -1)

    weight = 1.0 / (eigen + lax.dynamic_index_in_dim(damping, module, keepdims=False))
    scores = jnp.einsum(
        "naj,kaj->nk", rotated[0] * weight, rotated[1], precision=lax.Precision.HIGHEST
    )
    shape = scores.shape
    scores = jnp.where(core == 0, scores, scores.T).reshape(2, -1)
    scores = lax.psum(scores, "core")
    scores = everywhere(scores, ("tensor", "x"))
    return everywhere(scores, DP).reshape(shape)


def solution(mesh):
    n_dp, n_t, n_f = (mesh.shape[name] for name in ("dp", "tensor", "factor"))
    fine = Mesh(
        mesh.devices.reshape(n_dp // 2, 2, n_t, n_f // 2, 2), DP + ("tensor",) + FACTOR
    )
    features = ("tensor",) + FACTOR
    columns = DP + FACTOR
    placed = (
        P(DP, features),
        P(features),
        P(DP, None, None),
        P(DP, None),
        P(DP, None, None, features),
        P(None, "tensor", columns),
        P(),
        P(None, None, columns),
    )
    return jax.shard_map(body, mesh=fine, in_specs=placed, out_specs=P(), check_vma=False)
```

time: 151 us -> 167 us (1.11)
  blocking collectives: 25.6 us -> 68.4 us
  waiting for transfers between devices: 68.7 us -> 46.2 us
  starting transfers between devices: 27.5 us -> 21.9 us
    all_to_all x1 -> x3, blocking collectives: 23 us -> 65.7 us  [the longest x1 38.5 us: body(): parcel = lax.all_to_all(parcel, DP + FACTOR, 0, 0, tiled=True)]
    all_to_all x2 -> x1, waiting for transfers between devices: 40.3 us -> 7.94 us  [everywhere(): return jnp.sum(lax.all_to_all(terms, axes, 0, 0, tiled=True), axis=0)]
    all_to_all x2 -> x1, starting transfers between devices: 23.9 us -> 11.6 us  [everywhere(): return jnp.sum(lax.all_to_all(terms, axes, 0, 0, tiled=True), axis=0)]
    all_gather x1, waiting for transfers between devices: 0.02 us -> 11 us  [body(): basis = lax.all_gather(input_basis, ('zl', 'x'), axis=0)]
    ppermute x0 -> x2, starting transfers between devices: none -> 3.83 us  [the longest x1 3.19 us: body(): other = lax.ppermute(mine, 'core', [(0, 1), (1, 0)])]
    all_to_all x1, starting transfers between devices: 3.56 us -> 6.46 us  [body(): partial = lax.all_to_all(partial, 'tensor', 0, 0, tiled=True)]
    reshape x4 -> x2, local copies, waits for them, and re-layouts: 2.56 us -> 0.82 us  [the longest x1 0.68 us: body(): return everywhere(scores, DP).reshape(shape)]
    dot_general x3 -> x4, matrix products: 3.46 us -> 2.71 us  [the longest x2 1.42 us: rotate(): jnp.einsum('dfrk,hfkj->hdrj', rows.reshape(n_dp, n_f, rows_dev, width), b...]
  transfers between devices with their start and end apart: 4 -> 5, of which waited for: 3 -> 3; matrix products, arithmetic and copies ran while one was open for 6% -> 7% of each run, Pallas kernels for 0% -> 0%
where the time goes in v2:
time: 167 us; the launch traced here: 165 us
  blocking collectives  68.4 us (41%)
  waiting for transfers between devices  46.2 us (28%)
  starting transfers between devices  21.9 us (13%)
  between operations  13.6 us (8%)
  local copies, waits for them, and re-layouts  6.68 us (4%)
  other arithmetic  4.55 us (3%)
  matrix products  4.01 us (2%)
    all_to_all x1, blocking collectives, body(): parcel = lax.all_to_all(parcel, DP + FACTOR, 0, 0, tiled=True)  38.5 us
    all_to_all x2, blocking collectives, everywhere(): return jnp.sum(lax.all_to_all(terms, axes, 0, 0, tiled=True), axis=0)  27.1 us
    all_to_all x1, waiting for transfers between devices, body(): partial = lax.all_to_all(partial, 'tensor', 0, 0, tiled=True)  26.5 us
    all_to_all x1, starting transfers between devices, everywhere(): return jnp.sum(lax.all_to_all(terms, axes, 0, 0, tiled=True), axis=0)  11.6 us
    all_gather x1, waiting for transfers between devices, body(): basis = lax.all_gather(input_basis, ('zl', 'x'), axis=0)  11 us
    all_to_all x1, waiting for transfers between devices, everywhere(): return jnp.sum(lax.all_to_all(terms, axes, 0, 0, tiled=True), axis=0)  7.94 us
    all_to_all x1, starting transfers between devices, body(): partial = lax.all_to_all(partial, 'tensor', 0, 0, tiled=True)  6.46 us
  transfers between devices with their start and end apart: 5, of which 3 were waited for; matrix products, arithmetic and copies ran while one was open for 7% of the time, Pallas kernels for 0%

profile of v2, /device:TPU:1, one launch (start us, length us, event | category | flops | bytes accessed | tf_op | source)
XLA Modules:
  0.0 165.2 jit_solution(5532744196477046408)
XLA Ops:
  6.5 0.7 all-gather.3.cloned.1.call-update
  7.3 1.1 fusion.6
  8.3 0.7 broadcast_in_dim.10
  9.0 11.6 %all-to-all-start = ((f32[64,4,128]{2,1,0:T(4,128)}), f32[64,4,128]{2,1,0:T(4,128)S(1)}, u32[]{:S(2)}, u32[]{:S(2)}) async-start(f32[64,4,128]{2,1,0:T(4,128)} %broadcast_in_dim.10), calls=%async_computation | async-start | bytes 262144 | tf_op jit(solution)/shard_map/all_to_all | solution.py:27
  20.6 0.9 reduce_sum.67
  22.2 0.8 copy.39
  23.1 0.7 compare_convert_fusion
  23.8 7.9 %all-to-all-done = f32[64,4,128]{2,1,0:T(4,128)S(1)} async-done(((f32[64,4,128]{2,1,0:T(4,128)}), f32[64,4,128]{2,1,0:T(4,128)S(1)}, u32[]{:S(2)}, u32[]{:S(2)}) %all-to-all-start) | async-done | bytes 131104 | tf_op jit(solution)/shard_map/all_to_all | solution.py:27
  31.8 1.3 fusion.5
  33.1 1.0 fusion.4
  34.3 38.5 %all_to_all.25 = bf16[64,40,128]{2,1,0:T(8,128)(2,1)S(1)} all-to-all(bf16[64,40,128]{2,1,0:T(8,128)(2,1)S(1)} %bitcast.92), channel_id=1, replica_groups=mesh['zh'=4,'zl'=2,'tensor'=8,'x'=4,'core'=2] {'zh','zl','x','core'}, dimensions={0} | all-to-all | bytes 1310720 | tf_op jit(solution)/shard_map/all_to_all | solution.py:85
  72.9 3.2 %collective-permute-start = (bf16[64,32,128]{2,1,0:T(8,128)(2,1)S(1)}, bf16[64,32,128]{2,1,0:T(8,128)(2,1)S(1)}, u32[]{:S(2)}, u32[]{:S(2)}) collective-permute-start(bf16[64,32,128]{2,1,0:T(8,128)(2,1)S(1)} %slice.38), channel_id=1, source_target_pairs={{0,1},{1,0},{2,3},{3,2},{4,5},{5,4},{6,7},{7,6},{8,9},{9,8},{10,11... | collective-permute-start | bytes 1572872 | tf_op jit(solution)/shard_map/ppermute | solution.py:90
  76.1 11.0 %all-gather.3.cloned.1.call-done = bf16[16,1024,128]{2,1,0:T(8,128)(2,1)} async-done(((bf16[2,1024,128]{2,1,0:T(8,128)(2,1)}), bf16[16,1024,128]{2,1,0:T(8,128)(2,1)}) %all-gather.3.cloned.1.call-update) | async-done | bytes 4194320 | tf_op jit(solution)/shard_map/all_gather | solution.py:43
  87.1 1.7 %constant_dynamic-slice_fusion = bf16[8,1,1024,128]{3,2,1,0:T(8,128)(2,1)S(1)} fusion(bf16[8,2,1024,128]{3,2,1,0:T(8,128)(2,1)} %bitcast.95, s32[]{:T(128)S(6)} %select_n.19), kind=kLoop, calls=%fused_computation.50 | loop fusion | bytes 4194308 | tf_op jit(solution)/shard_map/jit(dynamic_index_in_dim)/dynamic_slice | solution.py:91
  88.8 0.7 fusion.2
  89.6 0.7 fusion.3
  90.4 1.1 copy.42
  91.5 6.5 %all-to-all-start.2 = ((bf16[8,512,128]{2,1,0:T(8,128)(2,1)}), bf16[8,512,128]{2,1,0:T(8,128)(2,1)S(1)}, u32[]{:S(2)}, u32[]{:S(2)}) async-start(bf16[8,512,128]{2,1,0:T(8,128)(2,1)} %bitcast.33), calls=%async_computation.2 | async-start | bytes 2097152 | tf_op jit(solution)/shard_map/all_to_all | solution.py:104
  97.9 0.7 dynamic-slice_bitcast_fusion
  100.6 26.5 %all-to-all-done.2 = bf16[8,512,128]{2,1,0:T(8,128)(2,1)S(1)} async-done(((bf16[8,512,128]{2,1,0:T(8,128)(2,1)}), bf16[8,512,128]{2,1,0:T(8,128)(2,1)S(1)}, u32[]{:S(2)}, u32[]{:S(2)}) %all-to-all-start.2) | async-done | bytes 1048608 | tf_op jit(solution)/shard_map/all_to_all | solution.py:104
  127.8 2.7 %psum.7 = f32[2,128]{1,0:T(2,128)S(1)} all-reduce(f32[2,128]{1,0:T(2,128)S(1)} %reshape.151), channel_id=1, replica_groups=mesh['zh'=4,'zl'=2,'tensor'=8,'x'=4,'core'=2] {'core'}, use_global_device_ids=true, to_apply=%region_5.6 | all-reduce | flops 256 | bytes 2048 | tf_op jit(solution)/shard_map/psum | solution.py:114
  130.5 13.7 %all_to_all.26 = f32[32,2,128]{2,1,0:T(2,128)S(1)} all-to-all(f32[32,2,128]{2,1,0:T(2,128)S(1)} %broadcast_in_dim.25), channel_id=1, replica_groups=mesh['zh'=4,'zl'=2,'tensor'=8,'x'=4,'core'=2] {'tensor','x'}, dimensions={0} | all-to-all | bytes 65536 | tf_op jit(solution)/shard_map/all_to_all | solution.py:27
  144.2 13.5 %all_to_all.27 = f32[8,2,128]{2,1,0:T(2,128)S(1)} all-to-all(f32[8,2,128]{2,1,0:T(2,128)S(1)} %broadcast_in_dim.26), channel_id=1, replica_groups=mesh['zh'=4,'zl'=2,'tensor'=8,'x'=4,'core'=2] {'zh','zl'}, dimensions={0} | all-to-all | bytes 16384 | tf_op jit(solution)/shard_map/all_to_all | solution.py:27
  157.7 0.7 reshape.152
  (30 shorter events, 3.8 us)
Async XLA Ops:
  6.5 80.5 %all-gather.3.cloned.1.call-start = ((), (), s32[]{:S(2)}) async-start(), calls=%async_computation.5 | async-start | bytes 4718592 | tf_op jit(solution)/shard_map/all_gather | solution.py:43
  9.0 22.7 %all-to-all-start = ((f32[64,4,128]{2,1,0:T(4,128)}), f32[64,4,128]{2,1,0:T(4,128)S(1)}, u32[]{:S(2)}, u32[]{:S(2)}) async-start(f32[64,4,128]{2,1,0:T(4,128)} %broadcast_in_dim.10), calls=%async_computation | async-start | bytes 262144 | tf_op jit(solution)/shard_map/all_to_all | solution.py:27
  72.9 16.0 %collective-permute-start = (bf16[64,32,128]{2,1,0:T(8,128)(2,1)S(1)}, bf16[64,32,128]{2,1,0:T(8,128)(2,1)S(1)}, u32[]{:S(2)}, u32[]{:S(2)}) collective-permute-start(bf16[64,32,128]{2,1,0:T(8,128)(2,1)S(1)} %slice.38), channel_id=1, source_target_pairs={{0,1},{1,0},{2,3},{3,2},{4,5},{5,4},{6,7},{7,6},{8,9},{9,8},{10,11... | collective-permute-start | bytes 1572872 | tf_op jit(solution)/shard_map/ppermute | solution.py:90
  91.5 35.7 %all-to-all-start.2 = ((bf16[8,512,128]{2,1,0:T(8,128)(2,1)}), bf16[8,512,128]{2,1,0:T(8,128)(2,1)S(1)}, u32[]{:S(2)}, u32[]{:S(2)}) async-start(bf16[8,512,128]{2,1,0:T(8,128)(2,1)} %bitcast.33), calls=%async_computation.2 | async-start | bytes 2097152 | tf_op jit(solution)/shard_map/all_to_all | solution.py:104
  98.6 1.3 collective-permute-start.1
Sparse Core Ops, SparseCore 0:
  9.4 77.5 all-gather.2

commit v3 on v2

--- a/solution.py
+++ b/solution.py
@@ -1,6 +1,8 @@
 import jax
 import jax.numpy as jnp
 from jax import lax
+from jax.experimental import pallas as pl
+from jax.experimental.pallas import tpu as pltpu
 from jax.sharding import Mesh, PartitionSpec as P
 
 D = 8192
@@ -27,6 +29,23 @@
     return jnp.sum(lax.all_to_all(terms, axes, 0, 0, tiled=True), axis=0)
 
 
+def rotate_kernel(mine_ref, other_ref, *refs):
+    *block_refs, out_ref, rows_ref = refs
+    sources, height, width = mine_ref.shape
+    across = rows_ref.shape[1] // width
+    for half, ref in enumerate((mine_ref, other_ref)):
+        for source in range(sources):
+            top = (half * (sources // across) + source // across) * height
+            left = (source % across) * width
+            rows_ref[top : top + height, left : left + width] = ref[source]
+    shifts = len(block_refs)
+    for shift, ref in enumerate(block_refs):
+        columns = jnp.concatenate([ref[0], ref[1]], axis=1)
+        product = jnp.dot(rows_ref[...], columns, preferred_element_type=jnp.float32)
+        out_ref[shift] = product[:, :width].astype(jnp.bfloat16)
+        out_ref[shifts + shift] = product[:, width:].astype(jnp.bfloat16)
+
+
 def body(
     resid, norm_gain, cotangent, segment_ids, query_grads, input_basis, output_basis, eigenvalues
 ):
@@ -40,22 +59,34 @@
     a_rows = R // n_x
     rows_dev = a_rows * CAND_DEV
 
-    basis = lax.all_gather(input_basis, ("zl", "x"), axis=0)
-
-    swap = []
+    own = lax.dynamic_index_in_dim(input_basis, module, axis=0, keepdims=False)
+    got = lax.ppermute(
+        lax.dynamic_index_in_dim(input_basis, 1 - module, axis=0, keepdims=False),
+        "zl",
+        [(0, 1), (1, 0)],
+    )
+    pair = jnp.stack([own, got])
+    moves = []
     for zl in range(n_zl):
-        for tt in range(n_t):
+        for h in range(n_t):
             for x in range(n_x):
-                source = ((tt // n_x) * n_t + zl * n_x + x) * n_x + tt % n_x
-                swap.append((source, (zl * n_t + tt) * n_x + x))
+                source = ((zl ^ (h // n_x)) * n_t + h) * n_x + (x + h % n_x) % n_x
+                moves.append((source, (zl * n_t + h) * n_x + x))
+    wanted = jnp.bitwise_xor(module, t // n_x) * n_x + (lax.axis_index("x") - t % n_x) % n_x
     eigen_part = lax.dynamic_index_in_dim(
-        eigenvalues.reshape(n_t, a_rows, width), t, axis=0, keepdims=False
+        eigenvalues.reshape(MODULES * n_x, a_rows, width), wanted, axis=0, keepdims=False
     )
-    eigen = lax.ppermute(eigen_part, ("zl", "tensor", "x"), swap)
+    eigen = lax.ppermute(eigen_part, ("zl", "tensor", "x"), moves)
 
     values = resid.astype(jnp.float32)
     squares = jnp.sum(values * values, axis=1)
     totals = everywhere(squares.reshape(-1, 128), ("tensor",) + FACTOR).reshape(-1)
+
+    totals, pair = lax.optimization_barrier((totals, pair))
+    blocks = [pair] + [
+        lax.ppermute(pair, "x", [((x + step) % n_x, x) for x in range(n_x)])
+        for step in range(1, n_x)
+    ]
 
     normed = (
         values * lax.rsqrt(totals / D + 1e-05)[:, None] * norm_gain.astype(jnp.float32)
@@ -88,19 +119,15 @@
 
     mine = parcel[:, :rows_dev]
     other = lax.ppermute(mine, "core", [(0, 1), (1, 0)])
-    blocks = lax.dynamic_index_in_dim(basis, module, axis=1, keepdims=False)
-    blocks = blocks.reshape(n_t, n_f, width, blocks.shape[-1])
-
-    def rotate(rows):
-        return jnp.einsum(
-            "dfrk,hfkj->hdrj",
-            rows.reshape(n_dp, n_f, rows_dev, width),
-            blocks,
-            preferred_element_type=jnp.float32,
-        ).astype(jnp.bfloat16)
-
-    partial = jnp.stack([rotate(mine), rotate(other)], axis=1)
-    partial = partial.reshape(n_t, 2 * n_dp * rows_dev, -1)
+    partial = pl.pallas_call(
+        rotate_kernel,
+        out_shape=jax.ShapeDtypeStruct((n_t, 2 * n_dp * rows_dev, 128), jnp.bfloat16),
+        in_specs=[pl.BlockSpec(memory_space=pltpu.VMEM)] * (2 + n_x),
+        out_specs=pl.BlockSpec(memory_space=pltpu.VMEM),
+        scratch_shapes=[pltpu.VMEM((2 * n_dp * rows_dev, n_f * width), jnp.bfloat16)],
+        compiler_params=pltpu.CompilerParams(vmem_limit_bytes=32 << 20),
+        name="rotate",
+    )(mine, other, *blocks)
     partial = lax.all_to_all(partial, "tensor", 0, 0, tiled=True)
     rotated = jnp.sum(partial.astype(jnp.float32), axis=0)
     rotated = rotated.reshape(2, n_dp * CAND_DEV, a_rows, -1)
@@ -112,8 +139,7 @@
     shape = scores.shape
     scores = jnp.where(core == 0, scores, scores.T).reshape(2, -1)
     scores = lax.psum(scores, "core")
-    scores = everywhere(scores, ("tensor", "x"))
-    return everywhere(scores, DP).reshape(shape)
+    return everywhere(scores, DP + ("tensor", "x")).reshape(shape)
 
 
 def solution(mesh):

time: 167 us -> 144 us (0.86)
  blocking collectives: 68.4 us -> 28.6 us
  starting transfers between devices: 21.9 us -> 49.9 us
  between operations: 13.6 us -> 0.3 us
  waiting for transfers between devices: 46.2 us -> 54.5 us
  matrix products: 4.01 us -> 0.79 us
  Pallas kernels: 0 us -> 2.25 us
  local copies, waits for them, and re-layouts: 6.68 us -> 4.43 us
  other arithmetic: 4.55 us -> 2.59 us
    all_to_all x1 -> x0, blocking collectives: 38.5 us -> none  [body(): parcel = lax.all_to_all(parcel, DP + FACTOR, 0, 0, tiled=True)]
    ppermute x1 -> x5, starting transfers between devices: 0.65 us -> 15.5 us  [the longest x3 10.7 us: body(): lax.ppermute(pair, 'x', [((x + step) % n_x, x) for x in range(n_x)])]
    all_to_all x0 -> x1, starting transfers between devices: none -> 13.8 us  [body(): parcel = lax.all_to_all(parcel, DP + FACTOR, 0, 0, tiled=True)]
    ppermute x1 -> x5, waiting for transfers between devices: 0.01 us -> 12.2 us  [the longest x3 11.8 us: body(): lax.ppermute(pair, 'x', [((x + step) % n_x, x) for x in range(n_x)])]
    all_gather x1 -> x0, waiting for transfers between devices: 11 us -> none  [body(): basis = lax.all_gather(input_basis, ('zl', 'x'), axis=0)]
    all_to_all x0 -> x1, waiting for transfers between devices: none -> 9.66 us  [body(): parcel = lax.all_to_all(parcel, DP + FACTOR, 0, 0, tiled=True)]
    all_to_all x1, waiting for transfers between devices: 7.94 us -> 5.52 us  [everywhere(): return jnp.sum(lax.all_to_all(terms, axes, 0, 0, tiled=True), axis=0)]
    pallas_call x0 -> x1, Pallas kernels: none -> 2.25 us  [body(): pl.pallas_call(rotate_kernel, out_shape=jax.ShapeDtypeStruct((n_t, 2 * n_...]
  transfers between devices with their start and end apart: 5 -> 9, of which waited for: 3 -> 5; matrix products, arithmetic and copies ran while one was open for 7% -> 2% of each run, Pallas kernels for 0% -> 0%
where the time goes in v3:
time: 144 us; the launch traced here: 143 us
  waiting for transfers between devices  54.5 us (38%)
  starting transfers between devices  49.9 us (35%)
  blocking collectives  28.6 us (20%)
  local copies, waits for them, and re-layouts  4.43 us (3%)
  other arithmetic  2.59 us (2%)
  Pallas kernels  2.25 us (2%)
    all_to_all x1, waiting for transfers between devices, body(): partial = lax.all_to_all(partial, 'tensor', 0, 0, tiled=True)  27.2 us
    all_to_all x1, blocking collectives, everywhere(): return jnp.sum(lax.all_to_all(terms, axes, 0, 0, tiled=True), axis=0)  25.9 us
    all_to_all x1, starting transfers between devices, body(): parcel = lax.all_to_all(parcel, DP + FACTOR, 0, 0, tiled=True)  13.8 us
    ppermute x3, waiting for transfers between devices, body(): lax.ppermute(pair, 'x', [((x + step) % n_x, x) for x in range(n_x)])  11.8 us
    all_to_all x1, starting transfers between devices, everywhere(): return jnp.sum(lax.all_to_all(terms, axes, 0, 0, tiled=True), axis=0)  11.6 us
    ppermute x3, starting transfers between devices, body(): lax.ppermute(pair, 'x', [((x + step) % n_x, x) for x in range(n_x)])  10.7 us
    all_to_all x1, waiting for transfers between devices, body(): parcel = lax.all_to_all(parcel, DP + FACTOR, 0, 0, tiled=True)  9.66 us
    all_to_all x1, starting transfers between devices, body(): partial = lax.all_to_all(partial, 'tensor', 0, 0, tiled=True)  6.49 us
  transfers between devices with their start and end apart: 9, of which 5 were waited for; matrix products, arithmetic and copies ran while one was open for 2% of the time, Pallas kernels for 0%

profile of v3, /device:TPU:1, one launch (start us, length us, event | category | flops | bytes accessed | tf_op | source)
XLA Modules:
  0.0 143.3 jit_solution(9330779146351903508)
XLA Ops:
  0.0 1.1 fusion.2
  1.1 0.7 broadcast_in_dim.8
  1.8 11.6 %all-to-all-start = ((f32[64,4,128]{2,1,0:T(4,128)}), f32[64,4,128]{2,1,0:T(4,128)S(1)}, u32[]{:S(2)}, u32[]{:S(2)}) async-start(f32[64,4,128]{2,1,0:T(4,128)} %broadcast_in_dim.8), calls=%async_computation | async-start | bytes 262144 | tf_op jit(solution)/shard_map/all_to_all | solution.py:29
  13.4 1.1 constant_dynamic-slice_fusion
  14.6 4.1 %collective-permute-start = (bf16[1024,128]{1,0:T(8,128)(2,1)S(1)}, bf16[1024,128]{1,0:T(8,128)(2,1)S(1)}, u32[]{:S(2)}, u32[]{:S(2)}) collective-permute-start(bf16[1024,128]{1,0:T(8,128)(2,1)S(1)} %get-tuple-element.22), channel_id=1, source_target_pairs={{0,64},{64,0},{1,65},{65,1},{2,66},{66,2},{3,67},{67,3},{4,68},{68... | collective-permute-start | bytes 786440 | tf_op jit(solution)/shard_map/ppermute | solution.py:63
  19.0 5.5 %all-to-all-done = f32[64,4,128]{2,1,0:T(4,128)S(1)} async-done(((f32[64,4,128]{2,1,0:T(4,128)}), f32[64,4,128]{2,1,0:T(4,128)S(1)}, u32[]{:S(2)}, u32[]{:S(2)}) %all-to-all-start) | async-done | bytes 131104 | tf_op jit(solution)/shard_map/all_to_all | solution.py:29
  24.6 0.4 collective-permute-done
  25.7 0.9 broadcast_in_dim.10
  26.6 13.8 %all-to-all-start.1 = ((bf16[64,40,128]{2,1,0:T(8,128)(2,1)}), bf16[64,40,128]{2,1,0:T(8,128)(2,1)S(1)}, u32[]{:S(2)}, u32[]{:S(2)}) async-start(bf16[64,40,128]{2,1,0:T(8,128)(2,1)} %bitcast.16), calls=%async_computation.1 | async-start | bytes 1310720 | tf_op jit(solution)/shard_map/all_to_all | solution.py:116
  40.4 3.3 %collective-permute-start.4 = (bf16[2,1024,128]{2,1,0:T(8,128)(2,1)S(1)}, bf16[2,1024,128]{2,1,0:T(8,128)(2,1)S(1)}, u32[]{:S(2)}, u32[]{:S(2)}) collective-permute-start(bf16[2,1024,128]{2,1,0:T(8,128)(2,1)S(1)} %pad_maximum_fusion.refs_0_), channel_id=1, source_target_pairs={{6,0},{0,2},{2,4},{4,6},{7,1},{1,3},{3,5},{5,7},{14,8},{8,10},{10,... | collective-permute-start | bytes 1572872 | tf_op jit(solution)/shard_map/ppermute | solution.py:87
  43.7 4.3 %collective-permute-start.3 = (bf16[2,1024,128]{2,1,0:T(8,128)(2,1)S(1)}, bf16[2,1024,128]{2,1,0:T(8,128)(2,1)S(1)}, u32[]{:S(2)}, u32[]{:S(2)}) collective-permute-start(bf16[2,1024,128]{2,1,0:T(8,128)(2,1)S(1)} %pad_maximum_fusion.refs_0_), channel_id=1, source_target_pairs={{4,0},{6,2},{0,4},{2,6},{5,1},{7,3},{1,5},{3,7},{12,8},{14,10},{8,... | collective-permute-start | bytes 1572872 | tf_op jit(solution)/shard_map/ppermute | solution.py:87
  48.0 3.1 %collective-permute-start.2 = (bf16[2,1024,128]{2,1,0:T(8,128)(2,1)S(1)}, bf16[2,1024,128]{2,1,0:T(8,128)(2,1)S(1)}, u32[]{:S(2)}, u32[]{:S(2)}) collective-permute-start(bf16[2,1024,128]{2,1,0:T(8,128)(2,1)S(1)} %pad_maximum_fusion.refs_0_), channel_id=1, source_target_pairs={{2,0},{4,2},{6,4},{0,6},{3,1},{5,3},{7,5},{1,7},{10,8},{12,10},{14... | collective-permute-start | bytes 1572872 | tf_op jit(solution)/shard_map/ppermute | solution.py:87
  51.1 9.7 %all-to-all-done.1 = bf16[64,40,128]{2,1,0:T(8,128)(2,1)S(1)} async-done(((bf16[64,40,128]{2,1,0:T(8,128)(2,1)}), bf16[64,40,128]{2,1,0:T(8,128)(2,1)S(1)}, u32[]{:S(2)}, u32[]{:S(2)}) %all-to-all-start.1) | async-done | bytes 655392 | tf_op jit(solution)/shard_map/all_to_all | solution.py:116
  60.8 2.5 %collective-permute-start.1 = (bf16[64,32,128]{2,1,0:T(8,128)(2,1)S(1)}, bf16[64,32,128]{2,1,0:T(8,128)(2,1)S(1)}, u32[]{:S(2)}, u32[]{:S(2)}) collective-permute-start(bf16[64,32,128]{2,1,0:T(8,128)(2,1)S(1)} %slice.38.mine_ref), channel_id=1, source_target_pairs={{0,1},{1,0},{2,3},{3,2},{4,5},{5,4},{6,7},{7,6},{8,9},{9,8},{10,11... | collective-permute-start | bytes 1572872 | tf_op jit(solution)/shard_map/ppermute | solution.py:121
  63.3 11.8 %collective-permute-done.3.refs_2_ = bf16[2,1024,128]{2,1,0:T(8,128)(2,1)S(1)} collective-permute-done((bf16[2,1024,128]{2,1,0:T(8,128)(2,1)S(1)}, bf16[2,1024,128]{2,1,0:T(8,128)(2,1)S(1)}, u32[]{:S(2)}, u32[]{:S(2)}) %collective-permute-start.3) | collective-permute-done | bytes 524320 | tf_op jit(solution)/shard_map/ppermute | solution.py:87
  75.1 2.2 %rotate.1 = bf16[8,512,128]{2,1,0:T(8,128)(2,1)} custom-call(bf16[64,32,128]{2,1,0:T(8,128)(2,1)S(1)} %slice.38.mine_ref, bf16[64,32,128]{2,1,0:T(8,128)(2,1)S(1)} %collective-permute-done.1.other_ref, bf16[2,1024,128]{2,1,0:T(8,128)(2,1)S(1)} %pad_maximum_fusion.refs_0_, bf16[2,1024,128]{2,1,0:T(8,128)(2,1)S(1)} %collective-permute-done.2.refs_1_, ...), custom_call_target="tpu_custom_call" | custom-call | tf_op jit(solution)/shard_map/rotate/pallas_call | solution.py:122
  77.3 6.5 %all-to-all-start.2 = ((bf16[8,512,128]{2,1,0:T(8,128)(2,1)}), bf16[8,512,128]{2,1,0:T(8,128)(2,1)S(1)}, u32[]{:S(2)}, u32[]{:S(2)}) async-start(bf16[8,512,128]{2,1,0:T(8,128)(2,1)} %rotate.1), calls=%async_computation.2 | async-start | bytes 2097152 | tf_op jit(solution)/shard_map/all_to_all | solution.py:131
  83.8 0.7 collective-permute-start.5
  84.6 0.6 dynamic_slice.18
  85.2 0.7 add_divide_fusion
  85.8 27.2 %all-to-all-done.2 = bf16[8,512,128]{2,1,0:T(8,128)(2,1)S(1)} async-done(((bf16[8,512,128]{2,1,0:T(8,128)(2,1)}), bf16[8,512,128]{2,1,0:T(8,128)(2,1)S(1)}, u32[]{:S(2)}, u32[]{:S(2)}) %all-to-all-start.2) | async-done | bytes 1048608 | tf_op jit(solution)/shard_map/all_to_all | solution.py:131
  113.7 2.6 %psum.7 = f32[2,128]{1,0:T(2,128)S(1)} all-reduce(f32[2,128]{1,0:T(2,128)S(1)} %reshape.126), channel_id=1, replica_groups=mesh['zh'=4,'zl'=2,'tensor'=8,'x'=4,'core'=2] {'core'}, use_global_device_ids=true, to_apply=%region_5.6 | all-reduce | flops 256 | bytes 2048 | tf_op jit(solution)/shard_map/psum | solution.py:141
  116.4 25.9 %all_to_all.20 = f32[256,2,128]{2,1,0:T(2,128)S(1)} all-to-all(f32[256,2,128]{2,1,0:T(2,128)S(1)} %broadcast_in_dim.22), channel_id=1, replica_groups=mesh['zh'=4,'zl'=2,'tensor'=8,'x'=4,'core'=2] {'zh','zl','tensor','x'}, dimensions={0} | all-to-all | bytes 524288 | tf_op jit(solution)/shard_map/all_to_all | solution.py:29
  142.6 0.7 reshape.127
  (45 shorter events, 2.1 us)
Async XLA Ops:
  0.0 18.7 %copy-start.1 = (f32[2,64,128]{2,1,0:T(8,128)S(1)}, f32[2,64,128]{2,1,0:T(8,128)}, u32[]{:S(2)}) copy-start(f32[2,64,128]{2,1,0:T(8,128)} %param.17) | copy-start | bytes 196612
  0.0 18.9 %copy-start.6 = (bf16[128]{0:T(256)(128)(2,1)S(1)}, bf16[128]{0:T(256)(128)(2,1)}, u32[]{:S(2)}) copy-start(bf16[128]{0:T(256)(128)(2,1)} %param.11) | copy-start | bytes 772
  0.0 18.9 %copy-start.2 = (bf16[2,64,64]{2,1,0:T(8,128)(2,1)S(1)}, bf16[2,64,64]{2,1,0:T(8,128)(2,1)}, u32[]{:S(2)}) copy-start(bf16[2,64,64]{2,1,0:T(8,128)(2,1)} %param.16) | copy-start | bytes 49156
  0.0 19.0 %copy-start.3 = (s32[1,512]{1,0:T(1,128)S(1)}, s32[1,512]{1,0:T(1,128)}, u32[]{:S(2)}) copy-start(s32[1,512]{1,0:T(1,128)} %param.13) | copy-start | bytes 6148
  1.8 22.7 %all-to-all-start = ((f32[64,4,128]{2,1,0:T(4,128)}), f32[64,4,128]{2,1,0:T(4,128)S(1)}, u32[]{:S(2)}, u32[]{:S(2)}) async-start(f32[64,4,128]{2,1,0:T(4,128)} %broadcast_in_dim.8), calls=%async_computation | async-start | bytes 262144 | tf_op jit(solution)/shard_map/all_to_all | solution.py:29
  13.4 11.6 %copy-start = (bf16[512,128]{1,0:T(8,128)(2,1)S(1)}, bf16[512,128]{1,0:T(8,128)(2,1)}, u32[]{:S(2)}) copy-start(bf16[512,128]{1,0:T(8,128)(2,1)} %param.10) | copy-start | bytes 393220
  13.4 11.6 %copy-start.4 = (bf16[512,2,64]{0,2,1:T(8,128)(2,1)S(1)}, bf16[512,2,64]{0,2,1:T(8,128)(2,1)}, u32[]{:S(2)}) copy-start(bf16[512,2,64]{0,2,1:T(8,128)(2,1)} %param.12) | copy-start | bytes 393220
  14.6 10.9 %copy-start.5 = (bf16[2,2,64,128]{3,2,1,0:T(8,128)(2,1)S(1)}, bf16[2,2,64,128]{3,2,1,0:T(8,128)(2,1)}, u32[]{:S(2)}) copy-start(bf16[2,2,64,128]{3,2,1,0:T(8,128)(2,1)} %param.14) | copy-start | bytes 196612
  14.6 10.4 %collective-permute-start = (bf16[1024,128]{1,0:T(8,128)(2,1)S(1)}, bf16[1024,128]{1,0:T(8,128)(2,1)S(1)}, u32[]{:S(2)}, u32[]{:S(2)}) collective-permute-start(bf16[1024,128]{1,0:T(8,128)(2,1)S(1)} %get-tuple-element.22), channel_id=1, source_target_pairs={{0,64},{64,0},{1,65},{65,1},{2,66},{66,2},{3,67},{67,3},{4,68},{68... | collective-permute-start | bytes 786440 | tf_op jit(solution)/shard_map/ppermute | solution.py:63
  26.6 34.2 %all-to-all-start.1 = ((bf16[64,40,128]{2,1,0:T(8,128)(2,1)}), bf16[64,40,128]{2,1,0:T(8,128)(2,1)S(1)}, u32[]{:S(2)}, u32[]{:S(2)}) async-start(bf16[64,40,128]{2,1,0:T(8,128)(2,1)} %bitcast.16), calls=%async_computation.1 | async-start | bytes 1310720 | tf_op jit(solution)/shard_map/all_to_all | solution.py:116
  40.4 22.9 %collective-permute-start.4 = (bf16[2,1024,128]{2,1,0:T(8,128)(2,1)S(1)}, bf16[2,1024,128]{2,1,0:T(8,128)(2,1)S(1)}, u32[]{:S(2)}, u32[]{:S(2)}) collective-permute-start(bf16[2,1024,128]{2,1,0:T(8,128)(2,1)S(1)} %pad_maximum_fusion.refs_0_), channel_id=1, source_target_pairs={{6,0},{0,2},{2,4},{4,6},{7,1},{1,3},{3,5},{5,7},{14,8},{8,10},{10,... | collective-permute-start | bytes 1572872 | tf_op jit(solution)/shard_map/ppermute | solution.py:87
  43.7 31.4 %collective-permute-start.3 = (bf16[2,1024,128]{2,1,0:T(8,128)(2,1)S(1)}, bf16[2,1024,128]{2,1,0:T(8,128)(2,1)S(1)}, u32[]{:S(2)}, u32[]{:S(2)}) collective-permute-start(bf16[2,1024,128]{2,1,0:T(8,128)(2,1)S(1)} %pad_maximum_fusion.refs_0_), channel_id=1, source_target_pairs={{4,0},{6,2},{0,4},{2,6},{5,1},{7,3},{1,5},{3,7},{12,8},{14,10},{8,... | collective-permute-start | bytes 1572872 | tf_op jit(solution)/shard_map/ppermute | solution.py:87
  48.0 27.0 %collective-permute-start.2 = (bf16[2,1024,128]{2,1,0:T(8,128)(2,1)S(1)}, bf16[2,1024,128]{2,1,0:T(8,128)(2,1)S(1)}, u32[]{:S(2)}, u32[]{:S(2)}) collective-permute-start(bf16[2,1024,128]{2,1,0:T(8,128)(2,1)S(1)} %pad_maximum_fusion.refs_0_), channel_id=1, source_target_pairs={{2,0},{4,2},{6,4},{0,6},{3,1},{5,3},{7,5},{1,7},{10,8},{12,10},{14... | collective-permute-start | bytes 1572872 | tf_op jit(solution)/shard_map/ppermute | solution.py:87
  60.8 14.3 %collective-permute-start.1 = (bf16[64,32,128]{2,1,0:T(8,128)(2,1)S(1)}, bf16[64,32,128]{2,1,0:T(8,128)(2,1)S(1)}, u32[]{:S(2)}, u32[]{:S(2)}) collective-permute-start(bf16[64,32,128]{2,1,0:T(8,128)(2,1)S(1)} %slice.38.mine_ref), channel_id=1, source_target_pairs={{0,1},{1,0},{2,3},{3,2},{4,5},{5,4},{6,7},{7,6},{8,9},{9,8},{10,11... | collective-permute-start | bytes 1572872 | tf_op jit(solution)/shard_map/ppermute | solution.py:121
  77.3 35.7 %all-to-all-start.2 = ((bf16[8,512,128]{2,1,0:T(8,128)(2,1)}), bf16[8,512,128]{2,1,0:T(8,128)(2,1)S(1)}, u32[]{:S(2)}, u32[]{:S(2)}) async-start(bf16[8,512,128]{2,1,0:T(8,128)(2,1)} %rotate.1), calls=%async_computation.2 | async-start | bytes 2097152 | tf_op jit(solution)/shard_map/all_to_all | solution.py:131
  83.8 1.4 collective-permute-start.5

commit v4 on v3

--- a/solution.py
+++ b/solution.py
@@ -33,17 +33,20 @@
     *block_refs, out_ref, rows_ref = refs
     sources, height, width = mine_ref.shape
     across = rows_ref.shape[1] // width
+    count = sources // across * height
     for half, ref in enumerate((mine_ref, other_ref)):
         for source in range(sources):
-            top = (half * (sources // across) + source // across) * height
+            top = half * count + source // across * height
             left = (source % across) * width
             rows_ref[top : top + height, left : left + width] = ref[source]
     shifts = len(block_refs)
     for shift, ref in enumerate(block_refs):
         columns = jnp.concatenate([ref[0], ref[1]], axis=1)
         product = jnp.dot(rows_ref[...], columns, preferred_element_type=jnp.float32)
-        out_ref[shift] = product[:, :width].astype(jnp.bfloat16)
-        out_ref[shifts + shift] = product[:, width:].astype(jnp.bfloat16)
+        for near in range(2):
+            part = product[:, near * width : (near + 1) * width].astype(jnp.bfloat16)
+            out_ref[near * shifts + shift, :, :width] = part[:count]
+            out_ref[near * shifts + shift, :, width:] = part[count:]
 
 
 def body(
@@ -65,7 +68,14 @@
         "zl",
         [(0, 1), (1, 0)],
     )
+    values = resid.astype(jnp.float32)
+    squares = jnp.sum(values * values, axis=1)
+    squares, got = lax.optimization_barrier((squares, got))
     pair = jnp.stack([own, got])
+    blocks = [pair] + [
+        lax.ppermute(pair, "x", [((x + step) % n_x, x) for x in range(n_x)])
+        for step in range(1, n_x)
+    ]
     moves = []
     for zl in range(n_zl):
         for h in range(n_t):
@@ -78,15 +88,7 @@
     )
     eigen = lax.ppermute(eigen_part, ("zl", "tensor", "x"), moves)
 
-    values = resid.astype(jnp.float32)
-    squares = jnp.sum(values * values, axis=1)
     totals = everywhere(squares.reshape(-1, 128), ("tensor",) + FACTOR).reshape(-1)
-
-    totals, pair = lax.optimization_barrier((totals, pair))
-    blocks = [pair] + [
-        lax.ppermute(pair, "x", [((x + step) % n_x, x) for x in range(n_x)])
-        for step in range(1, n_x)
-    ]
 
     normed = (
         values * lax.rsqrt(totals / D + 1e-05)[:, None] * norm_gain.astype(jnp.float32)
@@ -113,6 +115,7 @@
     )
     parcel = jnp.broadcast_to(parcel, (n_zh,) + parcel.shape)
     parcel = parcel.reshape((n_dp * n_f,) + parcel.shape[-2:])
+    parcel, blocks[1] = lax.optimization_barrier((parcel, blocks[1]))
     parcel = lax.all_to_all(parcel, DP + FACTOR, 0, 0, tiled=True)
     sums = jnp.sum(parcel[:, rows_dev : rows_dev + 3, :MODULES].astype(jnp.float32), axis=(0, 1))
     damping = 0.1 * sums / (R * D)
@@ -121,7 +124,7 @@
     other = lax.ppermute(mine, "core", [(0, 1), (1, 0)])
     partial = pl.pallas_call(
         rotate_kernel,
-        out_shape=jax.ShapeDtypeStruct((n_t, 2 * n_dp * rows_dev, 128), jnp.bfloat16),
+        out_shape=jax.ShapeDtypeStruct((n_t, n_dp * rows_dev, 2 * width), jnp.bfloat16),
         in_specs=[pl.BlockSpec(memory_space=pltpu.VMEM)] * (2 + n_x),
         out_specs=pl.BlockSpec(memory_space=pltpu.VMEM),
         scratch_shapes=[pltpu.VMEM((2 * n_dp * rows_dev, n_f * width), jnp.bfloat16)],
@@ -130,11 +133,13 @@
     )(mine, other, *blocks)
     partial = lax.all_to_all(partial, "tensor", 0, 0, tiled=True)
     rotated = jnp.sum(partial.astype(jnp.float32), axis=0)
-    rotated = rotated.reshape(2, n_dp * CAND_DEV, a_rows, -1)
+    halves = (n_dp * CAND_DEV, a_rows, width)
+    first = rotated[:, :width].reshape(halves)
+    second = rotated[:, width:].reshape(halves)
 
     weight = 1.0 / (eigen + lax.dynamic_index_in_dim(damping, module, keepdims=False))
     scores = jnp.einsum(
-        "naj,kaj->nk", rotated[0] * weight, rotated[1], precision=lax.Precision.HIGHEST
+        "naj,kaj->nk", first * weight, second, precision=lax.Precision.HIGHEST
     )
     shape = scores.shape
     scores = jnp.where(core == 0, scores, scores.T).reshape(2, -1)

time: 144 us -> 157 us (1.090)
  waiting for transfers between devices: 54.5 us -> 66.2 us
  starting transfers between devices: 49.9 us -> 54.1 us
  blocking collectives: 28.6 us -> 26.2 us
    ppermute x3, waiting for transfers between devices: 11.8 us -> 16.5 us  [body(): lax.ppermute(pair, 'x', [((x + step) % n_x, x) for x in range(n_x)])]
    all_to_all x1, waiting for transfers between devices: 9.66 us -> 12.8 us  [body(): parcel = lax.all_to_all(parcel, DP + FACTOR, 0, 0, tiled=True)]
    ppermute x1, waiting for transfers between devices: 0.37 us -> 3.44 us  [body(): lax.ppermute(lax.dynamic_index_in_dim(input_basis, 1 - module, axis=0, ke...]
    all_to_all x1, blocking collectives: 25.9 us -> 23.6 us  [everywhere(): return jnp.sum(lax.all_to_all(terms, axes, 0, 0, tiled=True), axis=0)]
    all_to_all x1, starting transfers between devices: 11.6 us -> 13.7 us  [everywhere(): return jnp.sum(lax.all_to_all(terms, axes, 0, 0, tiled=True), axis=0)]
  transfers between devices with their start and end apart: 9 -> 9, of which waited for: 5 -> 6; matrix products, arithmetic and copies ran while one was open for 2% -> 2% of each run, Pallas kernels for 0% -> 0%
where the time goes in v4:
time: 157 us; the launch traced here: 156 us
  waiting for transfers between devices  66.2 us (42%)
  starting transfers between devices  54.1 us (34%)
  blocking collectives  26.2 us (17%)
  local copies, waits for them, and re-layouts  4.47 us (3%)
  Pallas kernels  2.25 us (1%)
  other arithmetic  1.63 us (1%)
    all_to_all x1, waiting for transfers between devices, body(): partial = lax.all_to_all(partial, 'tensor', 0, 0, tiled=True)  27.2 us
    all_to_all x1, blocking collectives, everywhere(): return jnp.sum(lax.all_to_all(terms, axes, 0, 0, tiled=True), axis=0)  23.6 us
    ppermute x3, waiting for transfers between devices, body(): lax.ppermute(pair, 'x', [((x + step) % n_x, x) for x in range(n_x)])  16.5 us
    all_to_all x1, starting transfers between devices, body(): parcel = lax.all_to_all(parcel, DP + FACTOR, 0, 0, tiled=True)  14.1 us
    all_to_all x1, starting transfers between devices, everywhere(): return jnp.sum(lax.all_to_all(terms, axes, 0, 0, tiled=True), axis=0)  13.7 us
    all_to_all x1, waiting for transfers between devices, body(): parcel = lax.all_to_all(parcel, DP + FACTOR, 0, 0, tiled=True)  12.8 us
    ppermute x3, starting transfers between devices, body(): lax.ppermute(pair, 'x', [((x + step) % n_x, x) for x in range(n_x)])  12.1 us
    all_to_all x1, waiting for transfers between devices, everywhere(): return jnp.sum(lax.all_to_all(terms, axes, 0, 0, tiled=True), axis=0)  6.38 us
  transfers between devices with their start and end apart: 9, of which 6 were waited for; matrix products, arithmetic and copies ran while one was open for 2% of the time, Pallas kernels for 0%

profile of v4, /device:TPU:1, one launch (start us, length us, event | category | flops | bytes accessed | tf_op | source)
XLA Modules:
  0.0 156.0 jit_solution(12068097358524596540)
XLA Ops:
  0.0 1.2 constant_dynamic-slice_fusion
  1.2 5.0 %collective-permute-start = (bf16[1024,128]{1,0:T(8,128)(2,1)S(1)}, bf16[1024,128]{1,0:T(8,128)(2,1)S(1)}, u32[]{:S(2)}, u32[]{:S(2)}) collective-permute-start(bf16[1024,128]{1,0:T(8,128)(2,1)S(1)} %get-tuple-element.26), channel_id=1, source_target_pairs={{0,64},{64,0},{1,65},{65,1},{2,66},{66,2},{3,67},{67,3},{4,68},{68... | collective-permute-start | bytes 786440 | tf_op jit(solution)/shard_map/ppermute | solution.py:66
  6.5 3.4 %collective-permute-done = bf16[1024,128]{1,0:T(8,128)(2,1)S(1)} collective-permute-done((bf16[1024,128]{1,0:T(8,128)(2,1)S(1)}, bf16[1024,128]{1,0:T(8,128)(2,1)S(1)}, u32[]{:S(2)}, u32[]{:S(2)}) %collective-permute-start) | collective-permute-done | bytes 262176 | tf_op jit(solution)/shard_map/ppermute | solution.py:66
  9.9 0.7 broadcast_in_dim.8
  10.6 13.7 %all-to-all-start = ((f32[64,4,128]{2,1,0:T(4,128)}), f32[64,4,128]{2,1,0:T(4,128)S(1)}, u32[]{:S(2)}, u32[]{:S(2)}) async-start(f32[64,4,128]{2,1,0:T(4,128)} %broadcast_in_dim.8), calls=%async_computation | async-start | bytes 262144 | tf_op jit(solution)/shard_map/all_to_all | solution.py:29
  24.6 4.5 %collective-permute-start.1 = (bf16[2,1024,128]{2,1,0:T(8,128)(2,1)S(1)}, bf16[2,1024,128]{2,1,0:T(8,128)(2,1)S(1)}, u32[]{:S(2)}, u32[]{:S(2)}) collective-permute-start(bf16[2,1024,128]{2,1,0:T(8,128)(2,1)S(1)} %pad_maximum_fusion.refs_0_), channel_id=1, source_target_pairs={{2,0},{4,2},{6,4},{0,6},{3,1},{5,3},{7,5},{1,7},{10,8},{12,10},{14... | collective-permute-start | bytes 1572872 | tf_op jit(solution)/shard_map/ppermute | solution.py:76
  29.1 6.4 %all-to-all-done = f32[64,4,128]{2,1,0:T(4,128)S(1)} async-done(((f32[64,4,128]{2,1,0:T(4,128)}), f32[64,4,128]{2,1,0:T(4,128)S(1)}, u32[]{:S(2)}, u32[]{:S(2)}) %all-to-all-start) | async-done | bytes 131104 | tf_op jit(solution)/shard_map/all_to_all | solution.py:29
  36.1 4.7 %collective-permute-done.1.refs_1_ = bf16[2,1024,128]{2,1,0:T(8,128)(2,1)S(1)} collective-permute-done((bf16[2,1024,128]{2,1,0:T(8,128)(2,1)S(1)}, bf16[2,1024,128]{2,1,0:T(8,128)(2,1)S(1)}, u32[]{:S(2)}, u32[]{:S(2)}) %collective-permute-start.1) | collective-permute-done | bytes 524320 | tf_op jit(solution)/shard_map/ppermute | solution.py:76
  40.8 0.9 broadcast_in_dim.10
  41.8 14.1 %all-to-all-start.1 = ((bf16[64,40,128]{2,1,0:T(8,128)(2,1)}), bf16[64,40,128]{2,1,0:T(8,128)(2,1)S(1)}, u32[]{:S(2)}, u32[]{:S(2)}) async-start(bf16[64,40,128]{2,1,0:T(8,128)(2,1)} %bitcast.15), calls=%async_computation.1 | async-start | bytes 1310720 | tf_op jit(solution)/shard_map/all_to_all | solution.py:119
  55.9 3.3 %collective-permute-start.4 = (bf16[2,1024,128]{2,1,0:T(8,128)(2,1)S(1)}, bf16[2,1024,128]{2,1,0:T(8,128)(2,1)S(1)}, u32[]{:S(2)}, u32[]{:S(2)}) collective-permute-start(bf16[2,1024,128]{2,1,0:T(8,128)(2,1)S(1)} %pad_maximum_fusion.refs_0_), channel_id=1, source_target_pairs={{6,0},{0,2},{2,4},{4,6},{7,1},{1,3},{3,5},{5,7},{14,8},{8,10},{10,... | collective-permute-start | bytes 1572872 | tf_op jit(solution)/shard_map/ppermute | solution.py:76
  59.2 4.3 %collective-permute-start.3 = (bf16[2,1024,128]{2,1,0:T(8,128)(2,1)S(1)}, bf16[2,1024,128]{2,1,0:T(8,128)(2,1)S(1)}, u32[]{:S(2)}, u32[]{:S(2)}) collective-permute-start(bf16[2,1024,128]{2,1,0:T(8,128)(2,1)S(1)} %pad_maximum_fusion.refs_0_), channel_id=1, source_target_pairs={{4,0},{6,2},{0,4},{2,6},{5,1},{7,3},{1,5},{3,7},{12,8},{14,10},{8,... | collective-permute-start | bytes 1572872 | tf_op jit(solution)/shard_map/ppermute | solution.py:76
  63.5 12.8 %all-to-all-done.1 = bf16[64,40,128]{2,1,0:T(8,128)(2,1)S(1)} async-done(((bf16[64,40,128]{2,1,0:T(8,128)(2,1)}), bf16[64,40,128]{2,1,0:T(8,128)(2,1)S(1)}, u32[]{:S(2)}, u32[]{:S(2)}) %all-to-all-start.1) | async-done | bytes 655392 | tf_op jit(solution)/shard_map/all_to_all | solution.py:119
  76.3 2.5 %collective-permute-start.2 = (bf16[64,32,128]{2,1,0:T(8,128)(2,1)S(1)}, bf16[64,32,128]{2,1,0:T(8,128)(2,1)S(1)}, u32[]{:S(2)}, u32[]{:S(2)}) collective-permute-start(bf16[64,32,128]{2,1,0:T(8,128)(2,1)S(1)} %slice.36.mine_ref), channel_id=1, source_target_pairs={{0,1},{1,0},{2,3},{3,2},{4,5},{5,4},{6,7},{7,6},{8,9},{9,8},{10,11... | collective-permute-start | bytes 1572872 | tf_op jit(solution)/shard_map/ppermute | solution.py:124
  78.8 11.8 %collective-permute-done.3.refs_2_ = bf16[2,1024,128]{2,1,0:T(8,128)(2,1)S(1)} collective-permute-done((bf16[2,1024,128]{2,1,0:T(8,128)(2,1)S(1)}, bf16[2,1024,128]{2,1,0:T(8,128)(2,1)S(1)}, u32[]{:S(2)}, u32[]{:S(2)}) %collective-permute-start.3) | collective-permute-done | bytes 524320 | tf_op jit(solution)/shard_map/ppermute | solution.py:76
  90.5 2.2 %rotate.1 = bf16[8,256,256]{2,1,0:T(8,128)(2,1)} custom-call(bf16[64,32,128]{2,1,0:T(8,128)(2,1)S(1)} %slice.36.mine_ref, bf16[64,32,128]{2,1,0:T(8,128)(2,1)S(1)} %collective-permute-done.2.other_ref, bf16[2,1024,128]{2,1,0:T(8,128)(2,1)S(1)} %pad_maximum_fusion.refs_0_, bf16[2,1024,128]{2,1,0:T(8,128)(2,1)S(1)} %collective-permute-done.1.refs_1_, ...), custom_call_target="tpu_custom_call" | custom-call | tf_op jit(solution)/shard_map/rotate/pallas_call | solution.py:125
  92.8 6.1 %all-to-all-start.2 = ((bf16[8,256,256]{2,1,0:T(8,128)(2,1)}), bf16[8,256,256]{2,1,0:T(8,128)(2,1)S(1)}, u32[]{:S(2)}, u32[]{:S(2)}) async-start(bf16[8,256,256]{2,1,0:T(8,128)(2,1)} %rotate.1), calls=%async_computation.2 | async-start | bytes 2097152 | tf_op jit(solution)/shard_map/all_to_all | solution.py:134
  98.9 0.7 collective-permute-start.5
  99.7 0.6 dynamic_slice.18
  100.3 0.7 add_divide_fusion
  100.9 27.2 %all-to-all-done.2 = bf16[8,256,256]{2,1,0:T(8,128)(2,1)S(1)} async-done(((bf16[8,256,256]{2,1,0:T(8,128)(2,1)}), bf16[8,256,256]{2,1,0:T(8,128)(2,1)S(1)}, u32[]{:S(2)}, u32[]{:S(2)}) %all-to-all-start.2) | async-done | bytes 1048608 | tf_op jit(solution)/shard_map/all_to_all | solution.py:134
  128.8 2.6 %psum.7 = f32[2,128]{1,0:T(2,128)S(1)} all-reduce(f32[2,128]{1,0:T(2,128)S(1)} %reshape.134), channel_id=1, replica_groups=mesh['zh'=4,'zl'=2,'tensor'=8,'x'=4,'core'=2] {'core'}, use_global_device_ids=true, to_apply=%region_5.6 | all-reduce | flops 256 | bytes 2048 | tf_op jit(solution)/shard_map/psum | solution.py:146
  131.4 23.6 %all_to_all.20 = f32[256,2,128]{2,1,0:T(2,128)S(1)} all-to-all(f32[256,2,128]{2,1,0:T(2,128)S(1)} %broadcast_in_dim.22), channel_id=1, replica_groups=mesh['zh'=4,'zl'=2,'tensor'=8,'x'=4,'core'=2] {'zh','zl','tensor','x'}, dimensions={0} | all-to-all | bytes 524288 | tf_op jit(solution)/shard_map/all_to_all | solution.py:29
  155.3 0.7 reshape.135
  (45 shorter events, 2.2 us)
Async XLA Ops:
  0.0 6.2 %copy-start.1 = (f32[2,64,128]{2,1,0:T(8,128)S(1)}, f32[2,64,128]{2,1,0:T(8,128)}, u32[]{:S(2)}) copy-start(f32[2,64,128]{2,1,0:T(8,128)} %param.17) | copy-start | bytes 196612
  0.0 6.3 %copy-start = (bf16[512,128]{1,0:T(8,128)(2,1)S(1)}, bf16[512,128]{1,0:T(8,128)(2,1)}, u32[]{:S(2)}) copy-start(bf16[512,128]{1,0:T(8,128)(2,1)} %param.10) | copy-start | bytes 393220
  0.0 6.5 %copy-start.3 = (s32[1,512]{1,0:T(1,128)S(1)}, s32[1,512]{1,0:T(1,128)}, u32[]{:S(2)}) copy-start(s32[1,512]{1,0:T(1,128)} %param.13) | copy-start | bytes 6148
  0.0 24.3 %copy-start.6 = (bf16[128]{0:T(256)(128)(2,1)S(1)}, bf16[128]{0:T(256)(128)(2,1)}, u32[]{:S(2)}) copy-start(bf16[128]{0:T(256)(128)(2,1)} %param.11) | copy-start | bytes 772
  0.0 24.3 %copy-start.2 = (bf16[2,64,64]{2,1,0:T(8,128)(2,1)S(1)}, bf16[2,64,64]{2,1,0:T(8,128)(2,1)}, u32[]{:S(2)}) copy-start(bf16[2,64,64]{2,1,0:T(8,128)(2,1)} %param.16) | copy-start | bytes 49156
  1.2 34.3 %copy-start.4 = (bf16[512,2,64]{0,2,1:T(8,128)(2,1)S(1)}, bf16[512,2,64]{0,2,1:T(8,128)(2,1)}, u32[]{:S(2)}) copy-start(bf16[512,2,64]{0,2,1:T(8,128)(2,1)} %param.12) | copy-start | bytes 393220
  1.2 8.7 %collective-permute-start = (bf16[1024,128]{1,0:T(8,128)(2,1)S(1)}, bf16[1024,128]{1,0:T(8,128)(2,1)S(1)}, u32[]{:S(2)}, u32[]{:S(2)}) collective-permute-start(bf16[1024,128]{1,0:T(8,128)(2,1)S(1)} %get-tuple-element.26), channel_id=1, source_target_pairs={{0,64},{64,0},{1,65},{65,1},{2,66},{66,2},{3,67},{67,3},{4,68},{68... | collective-permute-start | bytes 786440 | tf_op jit(solution)/shard_map/ppermute | solution.py:66
  10.6 25.3 %copy-start.5 = (bf16[2,2,64,128]{3,2,1,0:T(8,128)(2,1)S(1)}, bf16[2,2,64,128]{3,2,1,0:T(8,128)(2,1)}, u32[]{:S(2)}) copy-start(bf16[2,2,64,128]{3,2,1,0:T(8,128)(2,1)} %param.14) | copy-start | bytes 196612
  10.6 24.9 %all-to-all-start = ((f32[64,4,128]{2,1,0:T(4,128)}), f32[64,4,128]{2,1,0:T(4,128)S(1)}, u32[]{:S(2)}, u32[]{:S(2)}) async-start(f32[64,4,128]{2,1,0:T(4,128)} %broadcast_in_dim.8), calls=%async_computation | async-start | bytes 262144 | tf_op jit(solution)/shard_map/all_to_all | solution.py:29
  24.6 16.3 %collective-permute-start.1 = (bf16[2,1024,128]{2,1,0:T(8,128)(2,1)S(1)}, bf16[2,1024,128]{2,1,0:T(8,128)(2,1)S(1)}, u32[]{:S(2)}, u32[]{:S(2)}) collective-permute-start(bf16[2,1024,128]{2,1,0:T(8,128)(2,1)S(1)} %pad_maximum_fusion.refs_0_), channel_id=1, source_target_pairs={{2,0},{4,2},{6,4},{0,6},{3,1},{5,3},{7,5},{1,7},{10,8},{12,10},{14... | collective-permute-start | bytes 1572872 | tf_op jit(solution)/shard_map/ppermute | solution.py:76
  41.8 34.5 %all-to-all-start.1 = ((bf16[64,40,128]{2,1,0:T(8,128)(2,1)}), bf16[64,40,128]{2,1,0:T(8,128)(2,1)S(1)}, u32[]{:S(2)}, u32[]{:S(2)}) async-start(bf16[64,40,128]{2,1,0:T(8,128)(2,1)} %bitcast.15), calls=%async_computation.1 | async-start | bytes 1310720 | tf_op jit(solution)/shard_map/all_to_all | solution.py:119
  55.9 22.9 %collective-permute-start.4 = (bf16[2,1024,128]{2,1,0:T(8,128)(2,1)S(1)}, bf16[2,1024,128]{2,1,0:T(8,128)(2,1)S(1)}, u32[]{:S(2)}, u32[]{:S(2)}) collective-permute-start(bf16[2,1024,128]{2,1,0:T(8,128)(2,1)S(1)} %pad_maximum_fusion.refs_0_), channel_id=1, source_target_pairs={{6,0},{0,2},{2,4},{4,6},{7,1},{1,3},{3,5},{5,7},{14,8},{8,10},{10,... | collective-permute-start | bytes 1572872 | tf_op jit(solution)/shard_map/ppermute | solution.py:76
  59.2 31.4 %collective-permute-start.3 = (bf16[2,1024,128]{2,1,0:T(8,128)(2,1)S(1)}, bf16[2,1024,128]{2,1,0:T(8,128)(2,1)S(1)}, u32[]{:S(2)}, u32[]{:S(2)}) collective-permute-start(bf16[2,1024,128]{2,1,0:T(8,128)(2,1)S(1)} %pad_maximum_fusion.refs_0_), channel_id=1, source_target_pairs={{4,0},{6,2},{0,4},{2,6},{5,1},{7,3},{1,5},{3,7},{12,8},{14,10},{8,... | collective-permute-start | bytes 1572872 | tf_op jit(solution)/shard_map/ppermute | solution.py:76
  76.3 14.3 %collective-permute-start.2 = (bf16[64,32,128]{2,1,0:T(8,128)(2,1)S(1)}, bf16[64,32,128]{2,1,0:T(8,128)(2,1)S(1)}, u32[]{:S(2)}, u32[]{:S(2)}) collective-permute-start(bf16[64,32,128]{2,1,0:T(8,128)(2,1)S(1)} %slice.36.mine_ref), channel_id=1, source_target_pairs={{0,1},{1,0},{2,3},{3,2},{4,5},{5,4},{6,7},{7,6},{8,9},{9,8},{10,11... | collective-permute-start | bytes 1572872 | tf_op jit(solution)/shard_map/ppermute | solution.py:124
  92.8 35.3 %all-to-all-start.2 = ((bf16[8,256,256]{2,1,0:T(8,128)(2,1)}), bf16[8,256,256]{2,1,0:T(8,128)(2,1)S(1)}, u32[]{:S(2)}, u32[]{:S(2)}) async-start(bf16[8,256,256]{2,1,0:T(8,128)(2,1)} %rotate.1), calls=%async_computation.2 | async-start | bytes 2097152 | tf_op jit(solution)/shard_map/all_to_all | solution.py:134
  98.9 1.4 collective-permute-start.5

commit v5 on v3

--- a/solution.py
+++ b/solution.py
@@ -29,8 +29,7 @@
     return jnp.sum(lax.all_to_all(terms, axes, 0, 0, tiled=True), axis=0)
 
 
-def rotate_kernel(mine_ref, other_ref, *refs):
-    *block_refs, out_ref, rows_ref = refs
+def rotate_kernel(mine_ref, other_ref, blocks_ref, out_ref, rows_ref):
     sources, height, width = mine_ref.shape
     across = rows_ref.shape[1] // width
     for half, ref in enumerate((mine_ref, other_ref)):
@@ -38,9 +37,9 @@
             top = (half * (sources // across) + source // across) * height
             left = (source % across) * width
             rows_ref[top : top + height, left : left + width] = ref[source]
-    shifts = len(block_refs)
-    for shift, ref in enumerate(block_refs):
-        columns = jnp.concatenate([ref[0], ref[1]], axis=1)
+    shifts = blocks_ref.shape[0]
+    for shift in range(shifts):
+        columns = jnp.concatenate([blocks_ref[shift, 0], blocks_ref[shift, 1]], axis=1)
         product = jnp.dot(rows_ref[...], columns, preferred_element_type=jnp.float32)
         out_ref[shift] = product[:, :width].astype(jnp.bfloat16)
         out_ref[shifts + shift] = product[:, width:].astype(jnp.bfloat16)
@@ -70,9 +69,9 @@
     for zl in range(n_zl):
         for h in range(n_t):
             for x in range(n_x):
-                source = ((zl ^ (h // n_x)) * n_t + h) * n_x + (x + h % n_x) % n_x
+                source = ((zl ^ (h // n_x)) * n_t + h // n_x * n_x + x) * n_x + h % n_x
                 moves.append((source, (zl * n_t + h) * n_x + x))
-    wanted = jnp.bitwise_xor(module, t // n_x) * n_x + (lax.axis_index("x") - t % n_x) % n_x
+    wanted = jnp.bitwise_xor(module, t // n_x) * n_x + t % n_x
     eigen_part = lax.dynamic_index_in_dim(
         eigenvalues.reshape(MODULES * n_x, a_rows, width), wanted, axis=0, keepdims=False
     )
@@ -82,11 +81,10 @@
     squares = jnp.sum(values * values, axis=1)
     totals = everywhere(squares.reshape(-1, 128), ("tensor",) + FACTOR).reshape(-1)
 
-    totals, pair = lax.optimization_barrier((totals, pair))
-    blocks = [pair] + [
-        lax.ppermute(pair, "x", [((x + step) % n_x, x) for x in range(n_x)])
-        for step in range(1, n_x)
-    ]
+    eigen_sums = split_three(jnp.sum(eigenvalues, axis=(1, 2)))
+    extra = jnp.zeros((8, width), jnp.bfloat16).at[:3, :MODULES].set(eigen_sums)
+    totals, pair, extra = lax.optimization_barrier((totals, pair, extra))
+    blocks = lax.all_gather(pair, "x", axis=0)
 
     normed = (
         values * lax.rsqrt(totals / D + 1e-05)[:, None] * norm_gain.astype(jnp.float32)
@@ -106,8 +104,6 @@
         preferred_element_type=jnp.float32,
     ).astype(jnp.bfloat16)
     turned = turned.reshape(MODULES, n_x, n_c, rows_dev, width)
-    eigen_sums = split_three(jnp.sum(eigenvalues, axis=(1, 2)))
-    extra = jnp.zeros((8, width), jnp.bfloat16).at[:3, :MODULES].set(eigen_sums)
     parcel = jnp.concatenate(
         [turned, jnp.broadcast_to(extra, (MODULES, n_x, n_c) + extra.shape)], axis=3
     )
@@ -122,12 +118,12 @@
     partial = pl.pallas_call(
         rotate_kernel,
         out_shape=jax.ShapeDtypeStruct((n_t, 2 * n_dp * rows_dev, 128), jnp.bfloat16),
-        in_specs=[pl.BlockSpec(memory_space=pltpu.VMEM)] * (2 + n_x),
+        in_specs=[pl.BlockSpec(memory_space=pltpu.VMEM)] * 3,
         out_specs=pl.BlockSpec(memory_space=pltpu.VMEM),
         scratch_shapes=[pltpu.VMEM((2 * n_dp * rows_dev, n_f * width), jnp.bfloat16)],
         compiler_params=pltpu.CompilerParams(vmem_limit_bytes=32 << 20),
         name="rotate",
-    )(mine, other, *blocks)
+    )(mine, other, blocks)
     partial = lax.all_to_all(partial, "tensor", 0, 0, tiled=True)
     rotated = jnp.sum(partial.astype(jnp.float32), axis=0)
     rotated = rotated.reshape(2, n_dp * CAND_DEV, a_rows, -1)

time: 144 us -> 156 us (1.083)
  blocking collectives: 28.6 us -> 63.5 us
  starting transfers between devices: 49.9 us -> 25.3 us
  waiting for transfers between devices: 54.5 us -> 39.5 us
  between operations: 0.3 us -> 13.6 us
  other arithmetic: 2.59 us -> 4.24 us
    all_to_all x0 -> x1, blocking collectives: none -> 34 us  [body(): parcel = lax.all_to_all(parcel, DP + FACTOR, 0, 0, tiled=True)]
    all_to_all x1 -> x0, starting transfers between devices: 13.8 us -> none  [body(): parcel = lax.all_to_all(parcel, DP + FACTOR, 0, 0, tiled=True)]
    ppermute x3 -> x0, waiting for transfers between devices: 11.8 us -> none  [body(): lax.ppermute(pair, 'x', [((x + step) % n_x, x) for x in range(n_x)])]
    ppermute x3 -> x0, starting transfers between devices: 10.7 us -> none  [body(): lax.ppermute(pair, 'x', [((x + step) % n_x, x) for x in range(n_x)])]
    all_to_all x1 -> x0, waiting for transfers between devices: 9.66 us -> none  [body(): parcel = lax.all_to_all(parcel, DP + FACTOR, 0, 0, tiled=True)]
    all_gather x0 -> x1, waiting for transfers between devices: none -> 6.31 us  [body(): blocks = lax.all_gather(pair, 'x', axis=0)]
    unnamed x15, local copies, waits for them, and re-layouts: 0.13 us -> 1.71 us
  transfers between devices with their start and end apart: 9 -> 6, of which waited for: 5 -> 5; matrix products, arithmetic and copies ran while one was open for 2% -> 3% of each run, Pallas kernels for 0% -> 0%
where the time goes in v5:
time: 156 us; the launch traced here: 155 us
  blocking collectives  63.5 us (41%)
  waiting for transfers between devices  39.5 us (25%)
  starting transfers between devices  25.3 us (16%)
  between operations  13.6 us (9%)
  local copies, waits for them, and re-layouts  5.82 us (4%)
  other arithmetic  4.24 us (3%)
  Pallas kernels  2.26 us (1%)
    all_to_all x1, blocking collectives, body(): parcel = lax.all_to_all(parcel, DP + FACTOR, 0, 0, tiled=True)  34 us
    all_to_all x1, blocking collectives, everywhere(): return jnp.sum(lax.all_to_all(terms, axes, 0, 0, tiled=True), axis=0)  26.9 us
    all_to_all x1, waiting for transfers between devices, body(): partial = lax.all_to_all(partial, 'tensor', 0, 0, tiled=True)  26.5 us
    all_to_all x1, starting transfers between devices, everywhere(): return jnp.sum(lax.all_to_all(terms, axes, 0, 0, tiled=True), axis=0)  11.6 us
    all_to_all x1, starting transfers between devices, body(): partial = lax.all_to_all(partial, 'tensor', 0, 0, tiled=True)  6.5 us
    all_gather x1, waiting for transfers between devices, body(): blocks = lax.all_gather(pair, 'x', axis=0)  6.31 us
    all_to_all x1, waiting for transfers between devices, everywhere(): return jnp.sum(lax.all_to_all(terms, axes, 0, 0, tiled=True), axis=0)  5 us
    ppermute x1, starting transfers between devices, body(): lax.ppermute(lax.dynamic_index_in_dim(input_basis, 1 - module, axis=0, ke...  4 us
  transfers between devices with their start and end apart: 6, of which 5 were waited for; matrix products, arithmetic and copies ran while one was open for 3% of the time, Pallas kernels for 0%

profile of v5, /device:TPU:1, one launch (start us, length us, event | category | flops | bytes accessed | tf_op | source)
XLA Modules:
  0.0 155.0 jit_solution(15007799663226712782)
XLA Ops:
  6.6 1.1 fusion.2
  7.7 0.7 broadcast_in_dim.8
  8.3 11.6 %all-to-all-start = ((f32[64,4,128]{2,1,0:T(4,128)}), f32[64,4,128]{2,1,0:T(4,128)S(1)}, u32[]{:S(2)}, u32[]{:S(2)}) async-start(f32[64,4,128]{2,1,0:T(4,128)} %broadcast_in_dim.8), calls=%async_computation | async-start | bytes 262144 | tf_op jit(solution)/shard_map/all_to_all | solution.py:29
  20.0 1.1 constant_dynamic-slice_fusion
  21.1 4.0 %collective-permute-start = (bf16[1024,128]{1,0:T(8,128)(2,1)S(1)}, bf16[1024,128]{1,0:T(8,128)(2,1)S(1)}, u32[]{:S(2)}, u32[]{:S(2)}) collective-permute-start(bf16[1024,128]{1,0:T(8,128)(2,1)S(1)} %get-tuple-element.24), channel_id=1, source_target_pairs={{0,64},{64,0},{1,65},{65,1},{2,66},{66,2},{3,67},{67,3},{4,68},{68... | collective-permute-start | bytes 786440 | tf_op jit(solution)/shard_map/ppermute | solution.py:62
  25.1 0.9 reduce_sum.58
  26.1 5.0 %all-to-all-done = f32[64,4,128]{2,1,0:T(4,128)S(1)} async-done(((f32[64,4,128]{2,1,0:T(4,128)}), f32[64,4,128]{2,1,0:T(4,128)S(1)}, u32[]{:S(2)}, u32[]{:S(2)}) %all-to-all-start) | async-done | bytes 131104 | tf_op jit(solution)/shard_map/all_to_all | solution.py:29
  31.4 0.8 pad_maximum_fusion
  32.4 0.3 fusion.1
  33.1 34.0 %all_to_all.20 = bf16[64,40,128]{2,1,0:T(8,128)(2,1)S(1)} all-to-all(bf16[64,40,128]{2,1,0:T(8,128)(2,1)S(1)} %bitcast.55), channel_id=1, replica_groups=mesh['zh'=4,'zl'=2,'tensor'=8,'x'=4,'core'=2] {'zh','zl','x','core'}, dimensions={0} | all-to-all | bytes 1310720 | tf_op jit(solution)/shard_map/all_to_all | solution.py:112
  67.1 2.5 %collective-permute-start.1 = (bf16[64,32,128]{2,1,0:T(8,128)(2,1)S(1)}, bf16[64,32,128]{2,1,0:T(8,128)(2,1)S(1)}, u32[]{:S(2)}, u32[]{:S(2)}) collective-permute-start(bf16[64,32,128]{2,1,0:T(8,128)(2,1)S(1)} %slice.38.mine_ref), channel_id=1, source_target_pairs={{0,1},{1,0},{2,3},{3,2},{4,5},{5,4},{6,7},{7,6},{8,9},{9,8},{10,11... | collective-permute-start | bytes 1572872 | tf_op jit(solution)/shard_map/ppermute | solution.py:117
  69.6 1.5 collective-permute-done.1.other_ref
  71.1 6.3 %all-gather.3.cloned.1.call-done = bf16[8,1024,128]{2,1,0:T(8,128)(2,1)} async-done(((bf16[2,1024,128]{2,1,0:T(8,128)(2,1)}), bf16[8,1024,128]{2,1,0:T(8,128)(2,1)}) %all-gather.3.cloned.1.call-update) | async-done | bytes 2097168 | tf_op jit(solution)/shard_map/all_gather | solution.py:87
  77.4 1.6 %copy-done = bf16[8,1024,128]{2,1,0:T(8,128)(2,1)S(1)} copy-done((bf16[8,1024,128]{2,1,0:T(8,128)(2,1)S(1)}, bf16[8,1024,128]{2,1,0:T(8,128)(2,1)}, u32[]{:S(2)}) %copy-start) | copy-done | bytes 2097176
  79.0 2.3 %rotate.1 = bf16[8,512,128]{2,1,0:T(8,128)(2,1)} custom-call(bf16[64,32,128]{2,1,0:T(8,128)(2,1)S(1)} %slice.38.mine_ref, bf16[64,32,128]{2,1,0:T(8,128)(2,1)S(1)} %collective-permute-done.1.other_ref, bf16[4,2,1024,128]{3,2,1,0:T(8,128)(2,1)S(1)} %bitcast.54), custom_call_target="tpu_custom_call" | custom-call | tf_op jit(solution)/shard_map/rotate/pallas_call | solution.py:118
  81.3 6.5 %all-to-all-start.2 = ((bf16[8,512,128]{2,1,0:T(8,128)(2,1)}), bf16[8,512,128]{2,1,0:T(8,128)(2,1)S(1)}, u32[]{:S(2)}, u32[]{:S(2)}) async-start(bf16[8,512,128]{2,1,0:T(8,128)(2,1)} %rotate.1), calls=%async_computation.2 | async-start | bytes 2097152 | tf_op jit(solution)/shard_map/all_to_all | solution.py:127
  87.8 0.7 dynamic-slice_bitcast_fusion.1
  88.5 0.6 collective-permute-start.2
  89.2 0.6 dynamic_slice.18
  89.8 0.7 add_divide_fusion
  90.5 26.5 %all-to-all-done.2 = bf16[8,512,128]{2,1,0:T(8,128)(2,1)S(1)} async-done(((bf16[8,512,128]{2,1,0:T(8,128)(2,1)}), bf16[8,512,128]{2,1,0:T(8,128)(2,1)S(1)}, u32[]{:S(2)}, u32[]{:S(2)}) %all-to-all-start.2) | async-done | bytes 1048608 | tf_op jit(solution)/shard_map/all_to_all | solution.py:127
  117.6 2.6 %psum.7 = f32[2,128]{1,0:T(2,128)S(1)} all-reduce(f32[2,128]{1,0:T(2,128)S(1)} %reshape.126), channel_id=1, replica_groups=mesh['zh'=4,'zl'=2,'tensor'=8,'x'=4,'core'=2] {'core'}, use_global_device_ids=true, to_apply=%region_5.6 | all-reduce | flops 256 | bytes 2048 | tf_op jit(solution)/shard_map/psum | solution.py:137
  120.3 26.9 %all_to_all.21 = f32[256,2,128]{2,1,0:T(2,128)S(1)} all-to-all(f32[256,2,128]{2,1,0:T(2,128)S(1)} %broadcast_in_dim.22), channel_id=1, replica_groups=mesh['zh'=4,'zl'=2,'tensor'=8,'x'=4,'core'=2] {'zh','zl','tensor','x'}, dimensions={0} | all-to-all | bytes 524288 | tf_op jit(solution)/shard_map/all_to_all | solution.py:29
  147.5 0.7 reshape.127
  (41 shorter events, 1.9 us)
Async XLA Ops:
  6.5 25.9 %copy-start.1 = (bf16[512,128]{1,0:T(8,128)(2,1)S(1)}, bf16[512,128]{1,0:T(8,128)(2,1)}, u32[]{:S(2)}) copy-start(bf16[512,128]{1,0:T(8,128)(2,1)} %param.10) | copy-start | bytes 393220
  6.5 25.7 %copy-start.6 = (bf16[128]{0:T(256)(128)(2,1)S(1)}, bf16[128]{0:T(256)(128)(2,1)}, u32[]{:S(2)}) copy-start(bf16[128]{0:T(256)(128)(2,1)} %param.11) | copy-start | bytes 772
  6.5 25.7 %copy-start.2 = (bf16[2,64,64]{2,1,0:T(8,128)(2,1)S(1)}, bf16[2,64,64]{2,1,0:T(8,128)(2,1)}, u32[]{:S(2)}) copy-start(bf16[2,64,64]{2,1,0:T(8,128)(2,1)} %param.16) | copy-start | bytes 49156
  6.5 25.8 %copy-start.3 = (s32[1,512]{1,0:T(1,128)S(1)}, s32[1,512]{1,0:T(1,128)}, u32[]{:S(2)}) copy-start(s32[1,512]{1,0:T(1,128)} %param.13) | copy-start | bytes 6148
  6.5 25.9 %copy-start.4 = (bf16[512,2,64]{0,2,1:T(8,128)(2,1)S(1)}, bf16[512,2,64]{0,2,1:T(8,128)(2,1)}, u32[]{:S(2)}) copy-start(bf16[512,2,64]{0,2,1:T(8,128)(2,1)} %param.12) | copy-start | bytes 393220
  6.5 26.2 %copy-start.5 = (bf16[2,2,64,128]{3,2,1,0:T(8,128)(2,1)S(1)}, bf16[2,2,64,128]{3,2,1,0:T(8,128)(2,1)}, u32[]{:S(2)}) copy-start(bf16[2,2,64,128]{3,2,1,0:T(8,128)(2,1)} %param.14) | copy-start | bytes 196612
  8.3 22.7 %all-to-all-start = ((f32[64,4,128]{2,1,0:T(4,128)}), f32[64,4,128]{2,1,0:T(4,128)S(1)}, u32[]{:S(2)}, u32[]{:S(2)}) async-start(f32[64,4,128]{2,1,0:T(4,128)} %broadcast_in_dim.8), calls=%async_computation | async-start | bytes 262144 | tf_op jit(solution)/shard_map/all_to_all | solution.py:29
  20.0 57.5 %all-gather.3.cloned.1.call-start = ((), (), s32[]{:S(2)}) async-start(), calls=%async_computation.4 | async-start | bytes 2621440 | tf_op jit(solution)/shard_map/all_gather | solution.py:87
  21.1 10.3 %collective-permute-start = (bf16[1024,128]{1,0:T(8,128)(2,1)S(1)}, bf16[1024,128]{1,0:T(8,128)(2,1)S(1)}, u32[]{:S(2)}, u32[]{:S(2)}) collective-permute-start(bf16[1024,128]{1,0:T(8,128)(2,1)S(1)} %get-tuple-element.24), channel_id=1, source_target_pairs={{0,64},{64,0},{1,65},{65,1},{2,66},{66,2},{3,67},{67,3},{4,68},{68... | collective-permute-start | bytes 786440 | tf_op jit(solution)/shard_map/ppermute | solution.py:62
  67.1 4.0 %collective-permute-start.1 = (bf16[64,32,128]{2,1,0:T(8,128)(2,1)S(1)}, bf16[64,32,128]{2,1,0:T(8,128)(2,1)S(1)}, u32[]{:S(2)}, u32[]{:S(2)}) collective-permute-start(bf16[64,32,128]{2,1,0:T(8,128)(2,1)S(1)} %slice.38.mine_ref), channel_id=1, source_target_pairs={{0,1},{1,0},{2,3},{3,2},{4,5},{5,4},{6,7},{7,6},{8,9},{9,8},{10,11... | collective-permute-start | bytes 1572872 | tf_op jit(solution)/shard_map/ppermute | solution.py:117
  77.4 1.6 %copy-start = (bf16[8,1024,128]{2,1,0:T(8,128)(2,1)S(1)}, bf16[8,1024,128]{2,1,0:T(8,128)(2,1)}, u32[]{:S(2)}) copy-start(bf16[8,1024,128]{2,1,0:T(8,128)(2,1)} %all-gather.3.cloned.1.call-done) | copy-start | bytes 6291460
  81.3 35.7 %all-to-all-start.2 = ((bf16[8,512,128]{2,1,0:T(8,128)(2,1)}), bf16[8,512,128]{2,1,0:T(8,128)(2,1)S(1)}, u32[]{:S(2)}, u32[]{:S(2)}) async-start(bf16[8,512,128]{2,1,0:T(8,128)(2,1)} %rotate.1), calls=%async_computation.2 | async-start | bytes 2097152 | tf_op jit(solution)/shard_map/all_to_all | solution.py:127
  88.5 1.3 collective-permute-start.2
Sparse Core Ops, SparseCore 0:
  32.4 45.0 all-gather.2

commit v6 on v5

v6 whole, which is shorter than its diff:
```python
import math

import jax
import jax.numpy as jnp
from jax import lax
from jax.experimental import pallas as pl
from jax.experimental.pallas import tpu as pltpu
from jax.sharding import Mesh, PartitionSpec as P

D = 8192
R = 64
MODULES = 2
CAND_DEV = 2
FACTOR = ("x", "core")


def everywhere(value, axes):
    peers = math.prod(lax.axis_size(axis) for axis in axes)
    terms = jnp.broadcast_to(value, (peers,) + value.shape)
    return jnp.sum(lax.all_to_all(terms, axes, 0, 0, tiled=True), axis=0)


def prologue_kernel(resid_ref, eigen_ref, squares_ref, sums_ref):
    tokens, width = resid_ref.shape
    rows = []
    for top in range(0, tokens, width):
        values = resid_ref[top : top + width].astype(jnp.float32)
        rows.append(jnp.sum((values * values).T, axis=0, keepdims=True))
    squares_ref[...] = jnp.broadcast_to(jnp.concatenate(rows, axis=0), squares_ref.shape)
    terms = []
    for module in range(MODULES):
        rest = jnp.sum(eigen_ref[module], axis=0, keepdims=True)
        for _ in range(3):
            term = rest.astype(jnp.bfloat16).astype(jnp.float32)
            terms.append(term)
            rest = rest - term
    terms.append(jnp.zeros((sums_ref.shape[0] - 3 * MODULES, width), jnp.float32))
    sums_ref[...] = jnp.concatenate(terms, axis=0).astype(jnp.bfloat16)


def rotate_kernel(parcel_ref, near_ref, far_ref, out_ref, rows_ref):
    sources, _, width = parcel_ref.shape
    rows, depth = rows_ref.shape
    across = depth // width
    height = rows // 2 // (sources // across)
    for source in range(sources):
        for half in range(2):
            top = half * (rows // 2) + source // across * height
            left = (source % across) * width
            rows_ref[top : top + height, left : left + width] = parcel_ref[
                source, half * height : (half + 1) * height
            ]
    for shift in range(near_ref.shape[0]):
        columns = jnp.concatenate([near_ref[shift], far_ref[shift]], axis=1)
        product = jnp.dot(rows_ref[...], columns, preferred_element_type=jnp.float32)
        out_ref[2 * shift] = product[:, :width].astype(jnp.bfloat16)
        out_ref[2 * shift + 1] = product[:, width:].astype(jnp.bfloat16)


def body(
    resid, norm_gain, cotangent, segment_ids, query_grads, input_basis, output_basis, eigenvalues
):
    n_dp, n_t = lax.axis_size("dp"), lax.axis_size("tensor")
    n_x, n_c = lax.axis_size("x"), lax.axis_size("core")
    n_f = n_x * n_c
    t, x, core = lax.axis_index("tensor"), lax.axis_index("x"), lax.axis_index("core")
    tokens, width = resid.shape
    a_rows = MODULES * R // n_f
    rows_dev = 2 * CAND_DEV * a_rows

    module = x % MODULES

    own = lax.dynamic_index_in_dim(input_basis, module, axis=0, keepdims=False)
    rest = lax.dynamic_index_in_dim(input_basis, 1 - module, axis=0, keepdims=False)
    near = jnp.stack(
        [own]
        + [
            lax.ppermute(
                rest if step % MODULES else own, "x", [((k + step) % n_x, k) for k in range(n_x)]
            )
            for step in range(1, n_x)
        ]
    )
    far = lax.ppermute(near, "core", [(0, 1), (1, 0)])

    moves = []
    for h in range(n_t):
        for k in range(n_x):
            for c in range(n_c):
                source = (h * n_x + (k + h // n_c) % n_x) * n_c + (c ^ (h % n_c))
                moves.append((source, (h * n_x + k) * n_c + c))
    to_x = (x - t // n_c) % n_x
    wanted = (to_x % MODULES * (n_x // MODULES) + to_x // MODULES) * n_c + (core ^ (t % n_c))
    eigen_part = lax.dynamic_index_in_dim(
        eigenvalues.reshape(n_f, a_rows, width), wanted, axis=0, keepdims=False
    )
    eigen = lax.ppermute(eigen_part, ("tensor", "x", "core"), moves)

    squares, eigen_sums = pl.pallas_call(
        prologue_kernel,
        out_shape=(
            jax.ShapeDtypeStruct((n_t * n_f, tokens // width, width), jnp.float32),
            jax.ShapeDtypeStruct((8, width), jnp.bfloat16),
        ),
        in_specs=[pl.BlockSpec(memory_space=pltpu.VMEM)] * 2,
        out_specs=[pl.BlockSpec(memory_space=pltpu.VMEM)] * 2,
        name="prologue",
    )(resid, eigenvalues)
    squares = lax.all_to_all(squares, ("tensor",) + FACTOR, 0, 0, tiled=True)
    totals = jnp.sum(squares, axis=0).reshape(-1)

    values = resid.astype(jnp.float32)
    normed = (
        values * lax.rsqrt(totals / D + 1e-05)[:, None] * norm_gain.astype(jnp.float32)
    ).astype(jnp.bfloat16)
    onehot = (
        segment_ids[0][None, :] == jnp.arange(CAND_DEV, dtype=jnp.int32)[:, None]
    ).astype(jnp.bfloat16)
    weighted = onehot[:, :, None, None] * cotangent[None]
    grads = jnp.einsum(
        "stmb,ti->smbi", weighted, normed, preferred_element_type=jnp.float32
    ).astype(jnp.bfloat16)
    stack = jnp.concatenate([grads, query_grads], axis=0)
    turned = jnp.einsum(
        "mbxca,nmbi->xmcnai",
        output_basis.reshape(MODULES, R, n_x // MODULES, n_c, a_rows),
        stack,
        preferred_element_type=jnp.float32,
    ).astype(jnp.bfloat16)
    turned = turned.reshape(n_f, rows_dev, width)
    parcel = jnp.concatenate(
        [turned, jnp.broadcast_to(eigen_sums, (n_f,) + eigen_sums.shape)], axis=1
    )
    parcel = jnp.broadcast_to(parcel, (n_dp,) + parcel.shape)
    parcel = parcel.reshape((n_dp * n_f,) + parcel.shape[-2:])
    parcel = lax.all_to_all(parcel, ("dp",) + FACTOR, 0, 0, tiled=True)
    sums = parcel[:, rows_dev : rows_dev + 3 * MODULES].astype(jnp.float32)
    sums = jnp.sum(sums.reshape(-1, MODULES, 3 * width), axis=(0, 2))
    damping = 0.1 * sums / (R * D)

    partial = pl.pallas_call(
        rotate_kernel,
        out_shape=jax.ShapeDtypeStruct((n_t, n_dp * rows_dev, width), jnp.bfloat16),
        in_specs=[pl.BlockSpec(memory_space=pltpu.VMEM)] * 3,
        out_specs=pl.BlockSpec(memory_space=pltpu.VMEM),
        scratch_shapes=[pltpu.VMEM((n_dp * rows_dev, n_f * width), jnp.bfloat16)],
        compiler_params=pltpu.CompilerParams(vmem_limit_bytes=32 << 20),
        name="rotate",
    )(parcel, near, far)
    partial = lax.all_to_all(partial, "tensor", 0, 0, tiled=True)
    rotated = jnp.sum(partial.astype(jnp.float32), axis=0)
    rotated = rotated.reshape(2, n_dp * CAND_DEV, a_rows, width)

    weight = 1.0 / (eigen + lax.dynamic_index_in_dim(damping, module, keepdims=False))
    scores = jnp.einsum(
        "naj,kaj->nk", rotated[0] * weight, rotated[1], precision=lax.Precision.HIGHEST
    )
    shape = scores.shape
    scores = lax.psum(scores.reshape(2, -1), "core")
    return everywhere(scores, ("dp", "tensor", "x")).reshape(shape)


def solution(mesh):
    n_dp, n_t, n_f = (mesh.shape[name] for name in ("dp", "tensor", "factor"))
    fine = Mesh(mesh.devices.reshape(n_dp, n_t, n_f // 2, 2), ("dp", "tensor") + FACTOR)
    features = ("tensor",) + FACTOR
    columns = ("dp",) + FACTOR
    placed = (
        P("dp", features),
        P(features),
        P("dp", None, None),
        P("dp", None),
        P("dp", None, None, features),
        P(None, "tensor", columns),
        P(),
        P(None, None, columns),
    )
    return jax.shard_map(body, mesh=fine, in_specs=placed, out_specs=P(), check_vma=False)
```

time: 156 us -> 140 us (0.90)
  blocking collectives: 63.5 us -> 29.8 us
  starting transfers between devices: 25.3 us -> 42.2 us
  waiting for transfers between devices: 39.5 us -> 53.9 us
  between operations: 13.6 us -> 0.27 us
  Pallas kernels: 2.26 us -> 4 us
    all_to_all x1 -> x0, blocking collectives: 34 us -> none  [body(): parcel = lax.all_to_all(parcel, DP + FACTOR, 0, 0, tiled=True)]
    ppermute x3 -> x5, waiting for transfers between devices: 1.73 us -> 18.9 us  [the longest x3 16.6 us: body(): lax.ppermute(rest if step % MODULES else own, 'x', [((k + step) % n_x, k)...]
    all_to_all x1 -> x2, starting transfers between devices: 11.6 us -> 24.1 us  [the longest x1 12.3 us: body(): parcel = lax.all_to_all(parcel, ('dp',) + FACTOR, 0, 0, tiled=True)]
    ppermute x3 -> x5, starting transfers between devices: 7.11 us -> 14.6 us  [the longest x3 10.7 us: body(): lax.ppermute(rest if step % MODULES else own, 'x', [((k + step) % n_x, k)...]
    all_gather x1 -> x0, waiting for transfers between devices: 6.31 us -> none  [body(): blocks = lax.all_gather(pair, 'x', axis=0)]
    all_to_all x1 -> x2, waiting for transfers between devices: 5 us -> 8.91 us  [the longest x1 8.91 us: body(): squares = lax.all_to_all(squares, ('tensor',) + FACTOR, 0, 0, tiled=True)]
    all_to_all x1, starting transfers between devices: 6.5 us -> 3.56 us  [body(): partial = lax.all_to_all(partial, 'tensor', 0, 0, tiled=True)]
    reduce_sum x3, other arithmetic: 2.15 us -> 0.38 us  [the longest x2 0.3 us: body(): sums = jnp.sum(sums.reshape(-1, MODULES, 3 * width), axis=(0, 2))]
  transfers between devices with their start and end apart: 6 -> 8, of which waited for: 5 -> 6; matrix products, arithmetic and copies ran while one was open for 3% -> 3% of each run, Pallas kernels for 0% -> 0%
where the time goes in v6:
time: 140 us; the launch traced here: 139 us
  waiting for transfers between devices  53.9 us (38%)
  starting transfers between devices  42.2 us (30%)
  blocking collectives  29.8 us (21%)
  local copies, waits for them, and re-layouts  4.34 us (3%)
  Pallas kernels  4 us (3%)
  other arithmetic  2.99 us (2%)
  matrix products  1.75 us (1%)
    all_to_all x1, blocking collectives, everywhere(): return jnp.sum(lax.all_to_all(terms, axes, 0, 0, tiled=True), axis=0)  27.2 us
    all_to_all x1, waiting for transfers between devices, body(): partial = lax.all_to_all(partial, 'tensor', 0, 0, tiled=True)  26.1 us
    ppermute x3, waiting for transfers between devices, body(): lax.ppermute(rest if step % MODULES else own, 'x', [((k + step) % n_x, k)...  16.6 us
    all_to_all x1, starting transfers between devices, body(): parcel = lax.all_to_all(parcel, ('dp',) + FACTOR, 0, 0, tiled=True)  12.3 us
    all_to_all x1, starting transfers between devices, body(): squares = lax.all_to_all(squares, ('tensor',) + FACTOR, 0, 0, tiled=True)  11.8 us
    ppermute x3, starting transfers between devices, body(): lax.ppermute(rest if step % MODULES else own, 'x', [((k + step) % n_x, k)...  10.7 us
    all_to_all x1, waiting for transfers between devices, body(): squares = lax.all_to_all(squares, ('tensor',) + FACTOR, 0, 0, tiled=True)  8.91 us
    all_to_all x1, starting transfers between devices, body(): partial = lax.all_to_all(partial, 'tensor', 0, 0, tiled=True)  3.56 us
  transfers between devices with their start and end apart: 8, of which 6 were waited for; matrix products, arithmetic and copies ran while one was open for 3% of the time, Pallas kernels for 0%

profile of v6, /device:TPU:1, one launch (start us, length us, event | category | flops | bytes accessed | tf_op | source)
XLA Modules:
  0.0 139.3 jit_solution(6890607671615115986)
XLA Ops:
  0.0 1.7 %prologue.1 = (f32[64,4,128]{2,1,0:T(4,128)}, bf16[8,128]{1,0:T(8,128)(2,1)}) custom-call(bf16[512,128]{1,0:T(8,128)(2,1)} %resid_ref.1, f32[2,64,128]{2,1,0:T(8,128)} %eigen_ref.1), custom_call_target="tpu_custom_call" | custom-call | tf_op jit(solution)/shard_map/prologue/pallas_call | solution.py:99
  1.7 11.8 %all-to-all-start = ((f32[64,4,128]{2,1,0:T(4,128)}), f32[64,4,128]{2,1,0:T(4,128)S(1)}, u32[]{:S(2)}, u32[]{:S(2)}) async-start(f32[64,4,128]{2,1,0:T(4,128)} %get-tuple-element.7), calls=%async_computation | async-start | bytes 262144 | tf_op jit(solution)/shard_map/all_to_all | solution.py:109
  13.5 0.8 copy.24
  14.4 0.7 convert_element_type.33
  15.0 0.7 compare_convert_fusion
  15.7 8.9 %all-to-all-done = f32[64,4,128]{2,1,0:T(4,128)S(1)} async-done(((f32[64,4,128]{2,1,0:T(4,128)}), f32[64,4,128]{2,1,0:T(4,128)S(1)}, u32[]{:S(2)}, u32[]{:S(2)}) %all-to-all-start) | async-done | bytes 131104 | tf_op jit(solution)/shard_map/all_to_all | solution.py:109
  24.7 1.3 convolution_convert_fusion.1
  26.3 1.2 broadcast_in_dim.7
  27.4 12.3 %all-to-all-start.1 = ((bf16[64,72,128]{2,1,0:T(8,128)(2,1)}), bf16[64,72,128]{2,1,0:T(8,128)(2,1)S(1)}, u32[]{:S(2)}, u32[]{:S(2)}) async-start(bf16[64,72,128]{2,1,0:T(8,128)(2,1)} %bitcast.10), calls=%async_computation.1 | async-start | bytes 2359296 | tf_op jit(solution)/shard_map/all_to_all | solution.py:136
  39.8 3.3 %collective-permute-start.2 = (bf16[1024,128]{1,0:T(8,128)(2,1)S(1)}, bf16[1024,128]{1,0:T(8,128)(2,1)S(1)}, u32[]{:S(2)}, u32[]{:S(2)}) collective-permute-start(bf16[1024,128]{1,0:T(8,128)(2,1)S(1)} %get-tuple-element.10), channel_id=1, source_target_pairs={{6,0},{0,2},{2,4},{4,6},{7,1},{1,3},{3,5},{5,7},{14,8},{8,10},{10,... | collective-permute-start | bytes 786440 | tf_op jit(solution)/shard_map/ppermute | solution.py:78
  43.1 4.3 %collective-permute-start.1 = (bf16[1024,128]{1,0:T(8,128)(2,1)S(1)}, bf16[1024,128]{1,0:T(8,128)(2,1)S(1)}, u32[]{:S(2)}, u32[]{:S(2)}) collective-permute-start(bf16[1024,128]{1,0:T(8,128)(2,1)S(1)} %bitcast.37), channel_id=1, source_target_pairs={{4,0},{6,2},{0,4},{2,6},{5,1},{7,3},{1,5},{3,7},{12,8},{14,10},{8,... | collective-permute-start | bytes 786440 | tf_op jit(solution)/shard_map/ppermute | solution.py:78
  47.5 3.1 %collective-permute-start = (bf16[1024,128]{1,0:T(8,128)(2,1)S(1)}, bf16[1024,128]{1,0:T(8,128)(2,1)S(1)}, u32[]{:S(2)}, u32[]{:S(2)}) collective-permute-start(bf16[1024,128]{1,0:T(8,128)(2,1)S(1)} %get-tuple-element.10), channel_id=1, source_target_pairs={{2,0},{4,2},{6,4},{0,6},{3,1},{5,3},{7,5},{1,7},{10,8},{12,10},{14... | collective-permute-start | bytes 786440 | tf_op jit(solution)/shard_map/ppermute | solution.py:78
  50.6 3.6 %collective-permute-done.2 = bf16[1024,128]{1,0:T(8,128)(2,1)S(1)} collective-permute-done((bf16[1024,128]{1,0:T(8,128)(2,1)S(1)}, bf16[1024,128]{1,0:T(8,128)(2,1)S(1)}, u32[]{:S(2)}, u32[]{:S(2)}) %collective-permute-start.2) | collective-permute-done | bytes 262176 | tf_op jit(solution)/shard_map/ppermute | solution.py:78
  54.2 12.0 %collective-permute-done.1 = bf16[1024,128]{1,0:T(8,128)(2,1)S(1)} collective-permute-done((bf16[1024,128]{1,0:T(8,128)(2,1)S(1)}, bf16[1024,128]{1,0:T(8,128)(2,1)S(1)}, u32[]{:S(2)}, u32[]{:S(2)}) %collective-permute-start.1) | collective-permute-done | bytes 262176 | tf_op jit(solution)/shard_map/ppermute | solution.py:78
  66.1 1.0 collective-permute-done
  67.3 3.2 %collective-permute-start.3 = (bf16[4,1024,128]{2,1,0:T(8,128)(2,1)S(1)}, bf16[4,1024,128]{2,1,0:T(8,128)(2,1)S(1)}, u32[]{:S(2)}, u32[]{:S(2)}) collective-permute-start(bf16[4,1024,128]{2,1,0:T(8,128)(2,1)S(1)} %pad_maximum_fusion.near_ref), channel_id=1, source_target_pairs={{0,1},{1,0},{2,3},{3,2},{4,5},{5,4},{6,7},{7,6},{8,9},{9,8},{10,11... | collective-permute-start | bytes 3145736 | tf_op jit(solution)/shard_map/ppermute | solution.py:84
  70.5 2.3 %collective-permute-done.3.far_ref = bf16[4,1024,128]{2,1,0:T(8,128)(2,1)S(1)} collective-permute-done((bf16[4,1024,128]{2,1,0:T(8,128)(2,1)S(1)}, bf16[4,1024,128]{2,1,0:T(8,128)(2,1)S(1)}, u32[]{:S(2)}, u32[]{:S(2)}) %collective-permute-start.3) | collective-permute-done | bytes 1048608 | tf_op jit(solution)/shard_map/ppermute | solution.py:84
  72.8 2.3 %rotate.1 = bf16[8,512,128]{2,1,0:T(8,128)(2,1)} custom-call(bf16[64,72,128]{2,1,0:T(8,128)(2,1)S(1)} %all-to-all-done.1.parcel_ref, bf16[4,1024,128]{2,1,0:T(8,128)(2,1)S(1)} %pad_maximum_fusion.near_ref, bf16[4,1024,128]{2,1,0:T(8,128)(2,1)S(1)} %collective-permute-done.3.far_ref), custom_call_target="tpu_custom_call" | custom-call | tf_op jit(solution)/shard_map/rotate/pallas_call | solution.py:141
  75.1 3.6 %all-to-all-start.2 = ((bf16[8,512,128]{2,1,0:T(8,128)(2,1)}), bf16[8,512,128]{2,1,0:T(8,128)(2,1)S(1)}, u32[]{:S(2)}, u32[]{:S(2)}) async-start(bf16[8,512,128]{2,1,0:T(8,128)(2,1)} %rotate.1), calls=%async_computation.2 | async-start | bytes 2097152 | tf_op jit(solution)/shard_map/all_to_all | solution.py:150
  78.7 0.7 dynamic-slice_bitcast_fusion.1
  81.7 26.1 %all-to-all-done.2 = bf16[8,512,128]{2,1,0:T(8,128)(2,1)S(1)} async-done(((bf16[8,512,128]{2,1,0:T(8,128)(2,1)}), bf16[8,512,128]{2,1,0:T(8,128)(2,1)S(1)}, u32[]{:S(2)}, u32[]{:S(2)}) %all-to-all-start.2) | async-done | bytes 1048608 | tf_op jit(solution)/shard_map/all_to_all | solution.py:150
  108.4 2.6 %psum.7 = f32[2,128]{1,0:T(2,128)S(1)} all-reduce(f32[2,128]{1,0:T(2,128)S(1)} %reshape.68), channel_id=1, replica_groups=mesh['dp'=8,'tensor'=8,'x'=4,'core'=2] {'core'}, use_global_device_ids=true, to_apply=%region_4.5 | all-reduce | flops 256 | bytes 2048 | tf_op jit(solution)/shard_map/psum | solution.py:159
  111.1 27.2 %all_to_all.20 = f32[256,2,128]{2,1,0:T(2,128)S(1)} all-to-all(f32[256,2,128]{2,1,0:T(2,128)S(1)} %broadcast_in_dim.8), channel_id=1, replica_groups=mesh['dp'=8,'tensor'=8,'x'=4,'core'=2] {'dp','tensor','x'}, dimensions={0} | all-to-all | bytes 524288 | tf_op jit(solution)/shard_map/all_to_all | solution.py:20
  138.6 0.7 reshape.69
  (29 shorter events, 3.7 us)
Async XLA Ops:
  0.0 26.0 %copy-start.2 = (bf16[2,2,64,128]{3,2,1,0:T(8,128)(2,1)S(1)}, bf16[2,2,64,128]{3,2,1,0:T(8,128)(2,1)}, u32[]{:S(2)}) copy-start(bf16[2,2,64,128]{3,2,1,0:T(8,128)(2,1)} %param.12) | copy-start | bytes 196612
  1.7 24.5 %copy-start.1 = (bf16[8,128]{1,0:T(8,128)(2,1)S(1)}, bf16[8,128]{1,0:T(8,128)(2,1)}, u32[]{:S(2)}) copy-start(bf16[8,128]{1,0:T(8,128)(2,1)} %get-tuple-element.8) | copy-start | bytes 6148
  1.7 22.9 %all-to-all-start = ((f32[64,4,128]{2,1,0:T(4,128)}), f32[64,4,128]{2,1,0:T(4,128)S(1)}, u32[]{:S(2)}, u32[]{:S(2)}) async-start(f32[64,4,128]{2,1,0:T(4,128)} %get-tuple-element.7), calls=%async_computation | async-start | bytes 262144 | tf_op jit(solution)/shard_map/all_to_all | solution.py:109
  27.4 12.4 %copy-start = (bf16[2,1024,128]{2,1,0:T(8,128)(2,1)S(1)}, bf16[2,1024,128]{2,1,0:T(8,128)(2,1)}, u32[]{:S(2)}) copy-start(bf16[2,1024,128]{2,1,0:T(8,128)(2,1)} %param.13) | copy-start | bytes 1572868
  27.4 45.4 %all-to-all-start.1 = ((bf16[64,72,128]{2,1,0:T(8,128)(2,1)}), bf16[64,72,128]{2,1,0:T(8,128)(2,1)S(1)}, u32[]{:S(2)}, u32[]{:S(2)}) async-start(bf16[64,72,128]{2,1,0:T(8,128)(2,1)} %bitcast.10), calls=%async_computation.1 | async-start | bytes 2359296 | tf_op jit(solution)/shard_map/all_to_all | solution.py:136
  39.8 14.3 %collective-permute-start.2 = (bf16[1024,128]{1,0:T(8,128)(2,1)S(1)}, bf16[1024,128]{1,0:T(8,128)(2,1)S(1)}, u32[]{:S(2)}, u32[]{:S(2)}) collective-permute-start(bf16[1024,128]{1,0:T(8,128)(2,1)S(1)} %get-tuple-element.10), channel_id=1, source_target_pairs={{6,0},{0,2},{2,4},{4,6},{7,1},{1,3},{3,5},{5,7},{14,8},{8,10},{10,... | collective-permute-start | bytes 786440 | tf_op jit(solution)/shard_map/ppermute | solution.py:78
  43.1 23.0 %collective-permute-start.1 = (bf16[1024,128]{1,0:T(8,128)(2,1)S(1)}, bf16[1024,128]{1,0:T(8,128)(2,1)S(1)}, u32[]{:S(2)}, u32[]{:S(2)}) collective-permute-start(bf16[1024,128]{1,0:T(8,128)(2,1)S(1)} %bitcast.37), channel_id=1, source_target_pairs={{4,0},{6,2},{0,4},{2,6},{5,1},{7,3},{1,5},{3,7},{12,8},{14,10},{8,... | collective-permute-start | bytes 786440 | tf_op jit(solution)/shard_map/ppermute | solution.py:78
  47.5 19.7 %collective-permute-start = (bf16[1024,128]{1,0:T(8,128)(2,1)S(1)}, bf16[1024,128]{1,0:T(8,128)(2,1)S(1)}, u32[]{:S(2)}, u32[]{:S(2)}) collective-permute-start(bf16[1024,128]{1,0:T(8,128)(2,1)S(1)} %get-tuple-element.10), channel_id=1, source_target_pairs={{2,0},{4,2},{6,4},{0,6},{3,1},{5,3},{7,5},{1,7},{10,8},{12,10},{14... | collective-permute-start | bytes 786440 | tf_op jit(solution)/shard_map/ppermute | solution.py:78
  67.3 5.5 %collective-permute-start.3 = (bf16[4,1024,128]{2,1,0:T(8,128)(2,1)S(1)}, bf16[4,1024,128]{2,1,0:T(8,128)(2,1)S(1)}, u32[]{:S(2)}, u32[]{:S(2)}) collective-permute-start(bf16[4,1024,128]{2,1,0:T(8,128)(2,1)S(1)} %pad_maximum_fusion.near_ref), channel_id=1, source_target_pairs={{0,1},{1,0},{2,3},{3,2},{4,5},{5,4},{6,7},{7,6},{8,9},{9,8},{10,11... | collective-permute-start | bytes 3145736 | tf_op jit(solution)/shard_map/ppermute | solution.py:84
  75.1 32.8 %all-to-all-start.2 = ((bf16[8,512,128]{2,1,0:T(8,128)(2,1)}), bf16[8,512,128]{2,1,0:T(8,128)(2,1)S(1)}, u32[]{:S(2)}, u32[]{:S(2)}) async-start(bf16[8,512,128]{2,1,0:T(8,128)(2,1)} %rotate.1), calls=%async_computation.2 | async-start | bytes 2097152 | tf_op jit(solution)/shard_map/all_to_all | solution.py:150
  79.4 1.6 %collective-permute-start.4 = (f32[16,128]{1,0:T(8,128)S(1)}, f32[16,128]{1,0:T(8,128)S(1)}, u32[]{:S(2)}, u32[]{:S(2)}) collective-permute-start(f32[16,128]{1,0:T(8,128)S(1)} %dynamic-slice_bitcast_fusion.1), channel_id=1, source_target_pairs={{0,0},{1,1},{2,2},{3,3},{4,4},{5,5},{6,6},{7,7},{9,8},{8,9},{11,10... | collective-permute-start | bytes 24584 | tf_op jit(solution)/shard_map/ppermute | solution.py:97

commit v7 on v6

--- a/solution.py
+++ b/solution.py
@@ -1,3 +1,4 @@
+import functools
 import math
 
 import jax
@@ -70,19 +71,6 @@
 
     module = x % MODULES
 
-    own = lax.dynamic_index_in_dim(input_basis, module, axis=0, keepdims=False)
-    rest = lax.dynamic_index_in_dim(input_basis, 1 - module, axis=0, keepdims=False)
-    near = jnp.stack(
-        [own]
-        + [
-            lax.ppermute(
-                rest if step % MODULES else own, "x", [((k + step) % n_x, k) for k in range(n_x)]
-            )
-            for step in range(1, n_x)
-        ]
-    )
-    far = lax.ppermute(near, "core", [(0, 1), (1, 0)])
-
     moves = []
     for h in range(n_t):
         for k in range(n_x):
@@ -108,6 +96,20 @@
     )(resid, eigenvalues)
     squares = lax.all_to_all(squares, ("tensor",) + FACTOR, 0, 0, tiled=True)
     totals = jnp.sum(squares, axis=0).reshape(-1)
+
+    def shifted(value, step):
+        return lax.ppermute(value, "x", [((k + step) % n_x, k) for k in range(n_x)])
+
+    across = [shifted(input_basis, step) for step in range(2, n_x, 2)]
+    totals, *across = lax.optimization_barrier((totals, *across))
+    pick = functools.partial(lax.dynamic_index_in_dim, axis=0, keepdims=False)
+    own, rest = pick(input_basis, module), pick(input_basis, 1 - module)
+    near = [own] + [
+        shifted(rest, step) if step % 2 else pick(across[step // 2 - 1], module)
+        for step in range(1, n_x)
+    ]
+    near = jnp.stack(near)
+    far = lax.ppermute(near, "core", [(0, 1), (1, 0)])
 
     values = resid.astype(jnp.float32)
     normed = (
@@ -156,8 +158,8 @@
         "naj,kaj->nk", rotated[0] * weight, rotated[1], precision=lax.Precision.HIGHEST
     )
     shape = scores.shape
-    scores = lax.psum(scores.reshape(2, -1), "core")
-    return everywhere(scores, ("dp", "tensor", "x")).reshape(shape)
+    scores = jnp.sum(lax.all_gather(scores.reshape(2, -1), FACTOR, axis=0), axis=0)
+    return everywhere(scores, ("dp", "tensor")).reshape(shape)
 
 
 def solution(mesh):

time: 140 us -> 136 us (0.971)
  blocking collectives: 29.8 us -> 25.4 us
    all_to_all x1, blocking collectives: 27.2 us -> 15.3 us  [everywhere(): return jnp.sum(lax.all_to_all(terms, axes, 0, 0, tiled=True), axis=0)]
    all_gather x0 -> x1, blocking collectives: none -> 10.2 us  [body(): lax.all_gather(scores.reshape(2, -1), FACTOR, axis=0)]
    all_to_all x1, waiting for transfers between devices: 0.01 us -> 7.85 us  [body(): parcel = lax.all_to_all(parcel, ('dp',) + FACTOR, 0, 0, tiled=True)]
    ppermute x3, waiting for transfers between devices: 16.6 us -> 9.82 us  [shifted(): return lax.ppermute(value, 'x', [((k + step) % n_x, k) for k in range(n_x)])]
    psum x1 -> x0, blocking collectives: 2.59 us -> none  [body(): scores = lax.psum(scores.reshape(2, -1), 'core')]
    all_to_all x1, starting transfers between devices: 11.8 us -> 9.32 us  [body(): squares = lax.all_to_all(squares, ('tensor',) + FACTOR, 0, 0, tiled=True)]
    ppermute x3, starting transfers between devices: 10.7 us -> 12.1 us  [shifted(): return lax.ppermute(value, 'x', [((k + step) % n_x, k) for k in range(n_x)])]
  transfers between devices with their start and end apart: 8 -> 8, of which waited for: 6 -> 6; matrix products, arithmetic and copies ran while one was open for 3% -> 4% of each run, Pallas kernels for 0% -> 1%
where the time goes in v7:
time: 136 us; the launch traced here: 135 us
  waiting for transfers between devices  54.9 us (40%)
  starting transfers between devices  41.8 us (31%)
  blocking collectives  25.4 us (19%)
  local copies, waits for them, and re-layouts  4.32 us (3%)
  Pallas kernels  3.97 us (3%)
  other arithmetic  2.8 us (2%)
  matrix products  1.75 us (1%)
    all_to_all x1, waiting for transfers between devices, body(): partial = lax.all_to_all(partial, 'tensor', 0, 0, tiled=True)  26 us
    all_to_all x1, blocking collectives, everywhere(): return jnp.sum(lax.all_to_all(terms, axes, 0, 0, tiled=True), axis=0)  15.3 us
    all_to_all x1, starting transfers between devices, body(): parcel = lax.all_to_all(parcel, ('dp',) + FACTOR, 0, 0, tiled=True)  12.3 us
    ppermute x3, starting transfers between devices, shifted(): return lax.ppermute(value, 'x', [((k + step) % n_x, k) for k in range(n_x)])  12.1 us
    all_gather x1, blocking collectives, body(): lax.all_gather(scores.reshape(2, -1), FACTOR, axis=0)  10.2 us
    ppermute x3, waiting for transfers between devices, shifted(): return lax.ppermute(value, 'x', [((k + step) % n_x, k) for k in range(n_x)])  9.82 us
    all_to_all x1, starting transfers between devices, body(): squares = lax.all_to_all(squares, ('tensor',) + FACTOR, 0, 0, tiled=True)  9.32 us
    all_to_all x1, waiting for transfers between devices, body(): squares = lax.all_to_all(squares, ('tensor',) + FACTOR, 0, 0, tiled=True)  8.91 us
  transfers between devices with their start and end apart: 8, of which 6 were waited for; matrix products, arithmetic and copies ran while one was open for 4% of the time, Pallas kernels for 1%

profile of v7, /device:TPU:1, one launch (start us, length us, event | category | flops | bytes accessed | tf_op | source)
XLA Modules:
  0.0 135.3 jit_solution(13993432731280637768)
XLA Ops:
  0.0 5.6 %collective-permute-start = (bf16[2,1024,128]{2,1,0:T(8,128)(2,1)}, bf16[2,1024,128]{2,1,0:T(8,128)(2,1)S(1)}, u32[]{:S(2)}, u32[]{:S(2)}) collective-permute-start(bf16[2,1024,128]{2,1,0:T(8,128)(2,1)} %param.13), channel_id=1, source_target_pairs={{4,0},{6,2},{0,4},{2,6},{5,1},{7,3},{1,5},{3,7},{12,8},{14,10},{8,... | collective-permute-start | bytes 1572872 | tf_op jit(solution)/shard_map/ppermute | solution.py:101
  5.6 1.7 %prologue.1 = (f32[64,4,128]{2,1,0:T(4,128)}, bf16[8,128]{1,0:T(8,128)(2,1)}) custom-call(bf16[512,128]{1,0:T(8,128)(2,1)} %resid_ref.1, f32[2,64,128]{2,1,0:T(8,128)} %eigen_ref.1), custom_call_target="tpu_custom_call" | custom-call | tf_op jit(solution)/shard_map/prologue/pallas_call | solution.py:87
  7.3 9.3 %all-to-all-start = ((f32[64,4,128]{2,1,0:T(4,128)}), f32[64,4,128]{2,1,0:T(4,128)S(1)}, u32[]{:S(2)}, u32[]{:S(2)}) async-start(f32[64,4,128]{2,1,0:T(4,128)} %get-tuple-element.9), calls=%async_computation | async-start | bytes 262144 | tf_op jit(solution)/shard_map/all_to_all | solution.py:97
  16.7 0.8 copy.29
  17.5 0.7 convert_element_type.33
  18.2 0.7 compare_convert_fusion
  18.9 8.9 %all-to-all-done = f32[64,4,128]{2,1,0:T(4,128)S(1)} async-done(((f32[64,4,128]{2,1,0:T(4,128)}), f32[64,4,128]{2,1,0:T(4,128)S(1)}, u32[]{:S(2)}, u32[]{:S(2)}) %all-to-all-start) | async-done | bytes 131104 | tf_op jit(solution)/shard_map/all_to_all | solution.py:97
  27.9 1.3 convolution_convert_fusion.1
  29.4 1.2 broadcast_in_dim.7
  30.6 12.3 %all-to-all-start.1 = ((bf16[64,72,128]{2,1,0:T(8,128)(2,1)}), bf16[64,72,128]{2,1,0:T(8,128)(2,1)S(1)}, u32[]{:S(2)}, u32[]{:S(2)}) async-start(bf16[64,72,128]{2,1,0:T(8,128)(2,1)} %bitcast.10), calls=%async_computation.1 | async-start | bytes 2359296 | tf_op jit(solution)/shard_map/all_to_all | solution.py:138
  43.0 3.3 %collective-permute-start.2 = (bf16[1024,128]{1,0:T(8,128)(2,1)S(1)}, bf16[1024,128]{1,0:T(8,128)(2,1)S(1)}, u32[]{:S(2)}, u32[]{:S(2)}) collective-permute-start(bf16[1024,128]{1,0:T(8,128)(2,1)S(1)} %get-tuple-element.14), channel_id=1, source_target_pairs={{6,0},{0,2},{2,4},{4,6},{7,1},{1,3},{3,5},{5,7},{14,8},{8,10},{10,... | collective-permute-start | bytes 786440 | tf_op jit(solution)/shard_map/ppermute | solution.py:101
  46.3 3.2 %collective-permute-start.1 = (bf16[1024,128]{1,0:T(8,128)(2,1)S(1)}, bf16[1024,128]{1,0:T(8,128)(2,1)S(1)}, u32[]{:S(2)}, u32[]{:S(2)}) collective-permute-start(bf16[1024,128]{1,0:T(8,128)(2,1)S(1)} %get-tuple-element.14), channel_id=1, source_target_pairs={{2,0},{4,2},{6,4},{0,6},{3,1},{5,3},{7,5},{1,7},{10,8},{12,10},{14... | collective-permute-start | bytes 786440 | tf_op jit(solution)/shard_map/ppermute | solution.py:101
  49.5 7.8 %collective-permute-done.2 = bf16[1024,128]{1,0:T(8,128)(2,1)S(1)} collective-permute-done((bf16[1024,128]{1,0:T(8,128)(2,1)S(1)}, bf16[1024,128]{1,0:T(8,128)(2,1)S(1)}, u32[]{:S(2)}, u32[]{:S(2)}) %collective-permute-start.2) | collective-permute-done | bytes 262176 | tf_op jit(solution)/shard_map/ppermute | solution.py:101
  57.3 2.0 %collective-permute-done.1 = bf16[1024,128]{1,0:T(8,128)(2,1)S(1)} collective-permute-done((bf16[1024,128]{1,0:T(8,128)(2,1)S(1)}, bf16[1024,128]{1,0:T(8,128)(2,1)S(1)}, u32[]{:S(2)}, u32[]{:S(2)}) %collective-permute-start.1) | collective-permute-done | bytes 262176 | tf_op jit(solution)/shard_map/ppermute | solution.py:101
  59.5 3.9 %collective-permute-start.3 = (bf16[4,1024,128]{2,1,0:T(8,128)(2,1)S(1)}, bf16[4,1024,128]{2,1,0:T(8,128)(2,1)S(1)}, u32[]{:S(2)}, u32[]{:S(2)}) collective-permute-start(bf16[4,1024,128]{2,1,0:T(8,128)(2,1)S(1)} %pad_maximum_fusion.near_ref), channel_id=1, source_target_pairs={{0,1},{1,0},{2,3},{3,2},{4,5},{5,4},{6,7},{7,6},{8,9},{9,8},{10,11... | collective-permute-start | bytes 3145736 | tf_op jit(solution)/shard_map/ppermute | solution.py:112
  63.4 2.3 %collective-permute-done.3.far_ref = bf16[4,1024,128]{2,1,0:T(8,128)(2,1)S(1)} collective-permute-done((bf16[4,1024,128]{2,1,0:T(8,128)(2,1)S(1)}, bf16[4,1024,128]{2,1,0:T(8,128)(2,1)S(1)}, u32[]{:S(2)}, u32[]{:S(2)}) %collective-permute-start.3) | collective-permute-done | bytes 1048608 | tf_op jit(solution)/shard_map/ppermute | solution.py:112
  65.7 7.8 %all-to-all-done.1.parcel_ref = bf16[64,72,128]{2,1,0:T(8,128)(2,1)S(1)} async-done(((bf16[64,72,128]{2,1,0:T(8,128)(2,1)}), bf16[64,72,128]{2,1,0:T(8,128)(2,1)S(1)}, u32[]{:S(2)}, u32[]{:S(2)}) %all-to-all-start.1) | async-done | bytes 1179680 | tf_op jit(solution)/shard_map/all_to_all | solution.py:138
  73.5 2.3 %rotate.1 = bf16[8,512,128]{2,1,0:T(8,128)(2,1)} custom-call(bf16[64,72,128]{2,1,0:T(8,128)(2,1)S(1)} %all-to-all-done.1.parcel_ref, bf16[4,1024,128]{2,1,0:T(8,128)(2,1)S(1)} %pad_maximum_fusion.near_ref, bf16[4,1024,128]{2,1,0:T(8,128)(2,1)S(1)} %collective-permute-done.3.far_ref), custom_call_target="tpu_custom_call" | custom-call | tf_op jit(solution)/shard_map/rotate/pallas_call | solution.py:143
  75.8 3.6 %all-to-all-start.2 = ((bf16[8,512,128]{2,1,0:T(8,128)(2,1)}), bf16[8,512,128]{2,1,0:T(8,128)(2,1)S(1)}, u32[]{:S(2)}, u32[]{:S(2)}) async-start(bf16[8,512,128]{2,1,0:T(8,128)(2,1)} %rotate.1), calls=%async_computation.2 | async-start | bytes 2097152 | tf_op jit(solution)/shard_map/all_to_all | solution.py:152
  79.4 0.7 dynamic-slice_bitcast_fusion.1
  82.4 26.0 %all-to-all-done.2 = bf16[8,512,128]{2,1,0:T(8,128)(2,1)S(1)} async-done(((bf16[8,512,128]{2,1,0:T(8,128)(2,1)}), bf16[8,512,128]{2,1,0:T(8,128)(2,1)S(1)}, u32[]{:S(2)}, u32[]{:S(2)}) %all-to-all-start.2) | async-done | bytes 1048608 | tf_op jit(solution)/shard_map/all_to_all | solution.py:152
  109.0 10.2 %all_gather.3 = f32[8,2,128]{2,1,0:T(2,128)S(1)} all-gather(f32[1,2,128]{2,1,0:T(2,128)S(1)} %all_gather_reshape.3), channel_id=1, replica_groups=mesh['dp'=8,'tensor'=8,'x'=4,'core'=2] {'x','core'}, dimensions={0}, use_global_device_ids=true | all-gather | bytes 9216 | tf_op jit(solution)/shard_map/all_gather | solution.py:161
  119.2 15.3 %all_to_all.20 = f32[64,2,128]{2,1,0:T(2,128)S(1)} all-to-all(f32[64,2,128]{2,1,0:T(2,128)S(1)} %broadcast_in_dim.8), channel_id=1, replica_groups=mesh['dp'=8,'tensor'=8,'x'=4,'core'=2] {'dp','tensor'}, dimensions={0} | all-to-all | bytes 131072 | tf_op jit(solution)/shard_map/all_to_all | solution.py:21
  134.6 0.7 reshape.57
  (31 shorter events, 3.5 us)
Async XLA Ops:
  0.0 29.2 %copy-start.2 = (bf16[2,2,64,128]{3,2,1,0:T(8,128)(2,1)S(1)}, bf16[2,2,64,128]{3,2,1,0:T(8,128)(2,1)}, u32[]{:S(2)}) copy-start(bf16[2,2,64,128]{3,2,1,0:T(8,128)(2,1)} %param.12) | copy-start | bytes 196612
  0.0 27.8 %collective-permute-start = (bf16[2,1024,128]{2,1,0:T(8,128)(2,1)}, bf16[2,1024,128]{2,1,0:T(8,128)(2,1)S(1)}, u32[]{:S(2)}, u32[]{:S(2)}) collective-permute-start(bf16[2,1024,128]{2,1,0:T(8,128)(2,1)} %param.13), channel_id=1, source_target_pairs={{4,0},{6,2},{0,4},{2,6},{5,1},{7,3},{1,5},{3,7},{12,8},{14,10},{8,... | collective-permute-start | bytes 1572872 | tf_op jit(solution)/shard_map/ppermute | solution.py:101
  7.3 22.1 %copy-start.1 = (bf16[8,128]{1,0:T(8,128)(2,1)S(1)}, bf16[8,128]{1,0:T(8,128)(2,1)}, u32[]{:S(2)}) copy-start(bf16[8,128]{1,0:T(8,128)(2,1)} %get-tuple-element.11) | copy-start | bytes 6148
  7.3 20.4 %all-to-all-start = ((f32[64,4,128]{2,1,0:T(4,128)}), f32[64,4,128]{2,1,0:T(4,128)S(1)}, u32[]{:S(2)}, u32[]{:S(2)}) async-start(f32[64,4,128]{2,1,0:T(4,128)} %get-tuple-element.9), calls=%async_computation | async-start | bytes 262144 | tf_op jit(solution)/shard_map/all_to_all | solution.py:97
  30.6 12.4 %copy-start = (bf16[2,1024,128]{2,1,0:T(8,128)(2,1)S(1)}, bf16[2,1024,128]{2,1,0:T(8,128)(2,1)}, u32[]{:S(2)}) copy-start(bf16[2,1024,128]{2,1,0:T(8,128)(2,1)} %param.13) | copy-start | bytes 1572868
  30.6 42.9 %all-to-all-start.1 = ((bf16[64,72,128]{2,1,0:T(8,128)(2,1)}), bf16[64,72,128]{2,1,0:T(8,128)(2,1)S(1)}, u32[]{:S(2)}, u32[]{:S(2)}) async-start(bf16[64,72,128]{2,1,0:T(8,128)(2,1)} %bitcast.10), calls=%async_computation.1 | async-start | bytes 2359296 | tf_op jit(solution)/shard_map/all_to_all | solution.py:138
  43.0 14.3 %collective-permute-start.2 = (bf16[1024,128]{1,0:T(8,128)(2,1)S(1)}, bf16[1024,128]{1,0:T(8,128)(2,1)S(1)}, u32[]{:S(2)}, u32[]{:S(2)}) collective-permute-start(bf16[1024,128]{1,0:T(8,128)(2,1)S(1)} %get-tuple-element.14), channel_id=1, source_target_pairs={{6,0},{0,2},{2,4},{4,6},{7,1},{1,3},{3,5},{5,7},{14,8},{8,10},{10,... | collective-permute-start | bytes 786440 | tf_op jit(solution)/shard_map/ppermute | solution.py:101
  46.3 13.1 %collective-permute-start.1 = (bf16[1024,128]{1,0:T(8,128)(2,1)S(1)}, bf16[1024,128]{1,0:T(8,128)(2,1)S(1)}, u32[]{:S(2)}, u32[]{:S(2)}) collective-permute-start(bf16[1024,128]{1,0:T(8,128)(2,1)S(1)} %get-tuple-element.14), channel_id=1, source_target_pairs={{2,0},{4,2},{6,4},{0,6},{3,1},{5,3},{7,5},{1,7},{10,8},{12,10},{14... | collective-permute-start | bytes 786440 | tf_op jit(solution)/shard_map/ppermute | solution.py:101
  59.5 6.2 %collective-permute-start.3 = (bf16[4,1024,128]{2,1,0:T(8,128)(2,1)S(1)}, bf16[4,1024,128]{2,1,0:T(8,128)(2,1)S(1)}, u32[]{:S(2)}, u32[]{:S(2)}) collective-permute-start(bf16[4,1024,128]{2,1,0:T(8,128)(2,1)S(1)} %pad_maximum_fusion.near_ref), channel_id=1, source_target_pairs={{0,1},{1,0},{2,3},{3,2},{4,5},{5,4},{6,7},{7,6},{8,9},{9,8},{10,11... | collective-permute-start | bytes 3145736 | tf_op jit(solution)/shard_map/ppermute | solution.py:112
  75.8 32.7 %all-to-all-start.2 = ((bf16[8,512,128]{2,1,0:T(8,128)(2,1)}), bf16[8,512,128]{2,1,0:T(8,128)(2,1)S(1)}, u32[]{:S(2)}, u32[]{:S(2)}) async-start(bf16[8,512,128]{2,1,0:T(8,128)(2,1)} %rotate.1), calls=%async_computation.2 | async-start | bytes 2097152 | tf_op jit(solution)/shard_map/all_to_all | solution.py:152
  80.1 1.6 %collective-permute-start.4 = (f32[16,128]{1,0:T(8,128)S(1)}, f32[16,128]{1,0:T(8,128)S(1)}, u32[]{:S(2)}, u32[]{:S(2)}) collective-permute-start(f32[16,128]{1,0:T(8,128)S(1)} %dynamic-slice_bitcast_fusion.1), channel_id=1, source_target_pairs={{0,0},{1,1},{2,2},{3,3},{4,4},{5,5},{6,6},{7,7},{9,8},{8,9},{11,10... | collective-permute-start | bytes 24584 | tf_op jit(solution)/shard_map/ppermute | solution.py:85

commit v8 on v7

--- a/solution.py
+++ b/solution.py
@@ -18,7 +18,7 @@
 def everywhere(value, axes):
     peers = math.prod(lax.axis_size(axis) for axis in axes)
     terms = jnp.broadcast_to(value, (peers,) + value.shape)
-    return jnp.sum(lax.all_to_all(terms, axes, 0, 0, tiled=True), axis=0)
+    return lax.all_to_all(terms, axes, 0, 0, tiled=True)
 
 
 def prologue_kernel(resid_ref, eigen_ref, squares_ref, sums_ref):
@@ -37,6 +37,15 @@
             rest = rest - term
     terms.append(jnp.zeros((sums_ref.shape[0] - 3 * MODULES, width), jnp.float32))
     sums_ref[...] = jnp.concatenate(terms, axis=0).astype(jnp.bfloat16)
+
+
+def finish_kernel(terms_ref, out_ref):
+    total = jnp.sum(terms_ref[...], axis=0)
+    size = out_ref.shape[1]
+    per_row = total.shape[1] // size
+    for row in range(out_ref.shape[0]):
+        left = row % per_row * size
+        out_ref[row : row + 1, :] = total[row // per_row : row // per_row + 1, left : left + size]
 
 
 def rotate_kernel(parcel_ref, near_ref, far_ref, out_ref, rows_ref):
@@ -101,7 +110,15 @@
         return lax.ppermute(value, "x", [((k + step) % n_x, k) for k in range(n_x)])
 
     across = [shifted(input_basis, step) for step in range(2, n_x, 2)]
-    totals, *across = lax.optimization_barrier((totals, *across))
+    masked = [
+        jnp.where(segment_ids[0] == candidate, cotangent.transpose(1, 2, 0), 0)
+        for candidate in range(CAND_DEV)
+    ]
+    weighted = jnp.stack(masked).reshape(-1, tokens)
+    values = resid.astype(jnp.float32)
+    totals, weighted, values, *across = lax.optimization_barrier(
+        (totals, weighted, values, *across)
+    )
     pick = functools.partial(lax.dynamic_index_in_dim, axis=0, keepdims=False)
     own, rest = pick(input_basis, module), pick(input_basis, 1 - module)
     near = [own] + [
@@ -111,17 +128,11 @@
     near = jnp.stack(near)
     far = lax.ppermute(near, "core", [(0, 1), (1, 0)])
 
-    values = resid.astype(jnp.float32)
     normed = (
         values * lax.rsqrt(totals / D + 1e-05)[:, None] * norm_gain.astype(jnp.float32)
     ).astype(jnp.bfloat16)
-    onehot = (
-        segment_ids[0][None, :] == jnp.arange(CAND_DEV, dtype=jnp.int32)[:, None]
-    ).astype(jnp.bfloat16)
-    weighted = onehot[:, :, None, None] * cotangent[None]
-    grads = jnp.einsum(
-        "stmb,ti->smbi", weighted, normed, preferred_element_type=jnp.float32
-    ).astype(jnp.bfloat16)
+    grads = jnp.dot(weighted, normed, preferred_element_type=jnp.float32).astype(jnp.bfloat16)
+    grads = grads.reshape(CAND_DEV, MODULES, R, width)
     stack = jnp.concatenate([grads, query_grads], axis=0)
     turned = jnp.einsum(
         "mbxca,nmbi->xmcnai",
@@ -159,7 +170,13 @@
     )
     shape = scores.shape
     scores = jnp.sum(lax.all_gather(scores.reshape(2, -1), FACTOR, axis=0), axis=0)
-    return everywhere(scores, ("dp", "tensor")).reshape(shape)
+    return pl.pallas_call(
+        finish_kernel,
+        out_shape=jax.ShapeDtypeStruct(shape, jnp.float32),
+        in_specs=[pl.BlockSpec(memory_space=pltpu.VMEM)],
+        out_specs=pl.BlockSpec(memory_space=pltpu.VMEM),
+        name="finish",
+    )(everywhere(scores, ("dp", "tensor")))
 
 
 def solution(mesh):

time: 136 us -> 136 us (level)
  waiting for transfers between devices: 54.9 us -> 52.9 us
  other arithmetic: 2.8 us -> 4.62 us
  Pallas kernels: 3.97 us -> 5.55 us
    all_to_all x1, waiting for transfers between devices: 8.91 us -> 6.98 us  [body(): squares = lax.all_to_all(squares, ('tensor',) + FACTOR, 0, 0, tiled=True)]
    pallas_call x0 -> x1, Pallas kernels: none -> 1.58 us  [body(): pl.pallas_call(finish_kernel, out_shape=jax.ShapeDtypeStruct(shape, jnp.f...]
  transfers between devices with their start and end apart: 8 -> 8, of which waited for: 6 -> 6; matrix products, arithmetic and copies ran while one was open for 4% -> 5% of each run, Pallas kernels for 1% -> 1%
where the time goes in v8:
time: 136 us; the launch traced here: 135 us
  waiting for transfers between devices  52.9 us (39%)
  starting transfers between devices  41.7 us (31%)
  blocking collectives  25.7 us (19%)
  Pallas kernels  5.55 us (4%)
  other arithmetic  4.62 us (3%)
  local copies, waits for them, and re-layouts  3.64 us (3%)
    all_to_all x1, waiting for transfers between devices, body(): partial = lax.all_to_all(partial, 'tensor', 0, 0, tiled=True)  26 us
    all_to_all x1, blocking collectives, everywhere(): return lax.all_to_all(terms, axes, 0, 0, tiled=True)  15.6 us
    all_to_all x1, starting transfers between devices, body(): parcel = lax.all_to_all(parcel, ('dp',) + FACTOR, 0, 0, tiled=True)  12.3 us
    ppermute x3, starting transfers between devices, shifted(): return lax.ppermute(value, 'x', [((k + step) % n_x, k) for k in range(n_x)])  12 us
    all_gather x1, blocking collectives, body(): lax.all_gather(scores.reshape(2, -1), FACTOR, axis=0)  10.2 us
    ppermute x3, waiting for transfers between devices, shifted(): return lax.ppermute(value, 'x', [((k + step) % n_x, k) for k in range(n_x)])  9.82 us
    all_to_all x1, starting transfers between devices, body(): squares = lax.all_to_all(squares, ('tensor',) + FACTOR, 0, 0, tiled=True)  9.32 us
    all_to_all x1, waiting for transfers between devices, body(): parcel = lax.all_to_all(parcel, ('dp',) + FACTOR, 0, 0, tiled=True)  7.85 us
  transfers between devices with their start and end apart: 8, of which 6 were waited for; matrix products, arithmetic and copies ran while one was open for 5% of the time, Pallas kernels for 1%

profile of v8, /device:TPU:1, one launch (start us, length us, event | category | flops | bytes accessed | tf_op | source)
XLA Modules:
  0.0 135.3 jit_solution(6546311516078971299)
XLA Ops:
  0.0 5.5 %collective-permute-start = (bf16[2,1024,128]{2,1,0:T(8,128)(2,1)}, bf16[2,1024,128]{2,1,0:T(8,128)(2,1)S(1)}, u32[]{:S(2)}, u32[]{:S(2)}) collective-permute-start(bf16[2,1024,128]{2,1,0:T(8,128)(2,1)} %param.13), channel_id=1, source_target_pairs={{4,0},{6,2},{0,4},{2,6},{5,1},{7,3},{1,5},{3,7},{12,8},{14,10},{8,... | collective-permute-start | bytes 1572872 | tf_op jit(solution)/shard_map/ppermute | solution.py:110
  5.5 1.7 %prologue.1 = (f32[64,4,128]{2,1,0:T(4,128)}, bf16[8,128]{1,0:T(8,128)(2,1)}) custom-call(bf16[512,128]{1,0:T(8,128)(2,1)} %resid_ref.1, f32[2,64,128]{2,1,0:T(8,128)} %eigen_ref.1), custom_call_target="tpu_custom_call" | custom-call | tf_op jit(solution)/shard_map/prologue/pallas_call | solution.py:96
  7.2 9.3 %all-to-all-start = ((f32[64,4,128]{2,1,0:T(4,128)}), f32[64,4,128]{2,1,0:T(4,128)S(1)}, u32[]{:S(2)}, u32[]{:S(2)}) async-start(f32[64,4,128]{2,1,0:T(4,128)} %get-tuple-element.11), calls=%async_computation | async-start | bytes 262144 | tf_op jit(solution)/shard_map/all_to_all | solution.py:106
  16.5 0.9 convert_element_type.27
  17.5 0.9 copy.20
  19.0 0.7 compare_reduce_fusion.1
  19.7 0.9 select_bitcast_fusion.1
  20.6 7.0 %all-to-all-done = f32[64,4,128]{2,1,0:T(4,128)S(1)} async-done(((f32[64,4,128]{2,1,0:T(4,128)}), f32[64,4,128]{2,1,0:T(4,128)S(1)}, u32[]{:S(2)}, u32[]{:S(2)}) %all-to-all-start) | async-done | bytes 131104 | tf_op jit(solution)/shard_map/all_to_all | solution.py:106
  28.3 1.2 broadcast_in_dim.28
  29.5 12.3 %all-to-all-start.1 = ((bf16[64,72,128]{2,1,0:T(8,128)(2,1)}), bf16[64,72,128]{2,1,0:T(8,128)(2,1)S(1)}, u32[]{:S(2)}, u32[]{:S(2)}) async-start(bf16[64,72,128]{2,1,0:T(8,128)(2,1)} %bitcast.13), calls=%async_computation.1 | async-start | bytes 2359296 | tf_op jit(solution)/shard_map/all_to_all | solution.py:149
  41.9 3.3 %collective-permute-start.2 = (bf16[1024,128]{1,0:T(8,128)(2,1)S(1)}, bf16[1024,128]{1,0:T(8,128)(2,1)S(1)}, u32[]{:S(2)}, u32[]{:S(2)}) collective-permute-start(bf16[1024,128]{1,0:T(8,128)(2,1)S(1)} %get-tuple-element.20), channel_id=1, source_target_pairs={{6,0},{0,2},{2,4},{4,6},{7,1},{1,3},{3,5},{5,7},{14,8},{8,10},{10,... | collective-permute-start | bytes 786440 | tf_op jit(solution)/shard_map/ppermute | solution.py:110
  45.2 3.2 %collective-permute-start.1 = (bf16[1024,128]{1,0:T(8,128)(2,1)S(1)}, bf16[1024,128]{1,0:T(8,128)(2,1)S(1)}, u32[]{:S(2)}, u32[]{:S(2)}) collective-permute-start(bf16[1024,128]{1,0:T(8,128)(2,1)S(1)} %get-tuple-element.20), channel_id=1, source_target_pairs={{2,0},{4,2},{6,4},{0,6},{3,1},{5,3},{7,5},{1,7},{10,8},{12,10},{14... | collective-permute-start | bytes 786440 | tf_op jit(solution)/shard_map/ppermute | solution.py:110
  48.4 7.8 %collective-permute-done.2 = bf16[1024,128]{1,0:T(8,128)(2,1)S(1)} collective-permute-done((bf16[1024,128]{1,0:T(8,128)(2,1)S(1)}, bf16[1024,128]{1,0:T(8,128)(2,1)S(1)}, u32[]{:S(2)}, u32[]{:S(2)}) %collective-permute-start.2) | collective-permute-done | bytes 262176 | tf_op jit(solution)/shard_map/ppermute | solution.py:110
  56.2 2.0 %collective-permute-done.1 = bf16[1024,128]{1,0:T(8,128)(2,1)S(1)} collective-permute-done((bf16[1024,128]{1,0:T(8,128)(2,1)S(1)}, bf16[1024,128]{1,0:T(8,128)(2,1)S(1)}, u32[]{:S(2)}, u32[]{:S(2)}) %collective-permute-start.1) | collective-permute-done | bytes 262176 | tf_op jit(solution)/shard_map/ppermute | solution.py:110
  58.4 3.9 %collective-permute-start.3 = (bf16[4,1024,128]{2,1,0:T(8,128)(2,1)S(1)}, bf16[4,1024,128]{2,1,0:T(8,128)(2,1)S(1)}, u32[]{:S(2)}, u32[]{:S(2)}) collective-permute-start(bf16[4,1024,128]{2,1,0:T(8,128)(2,1)S(1)} %pad_maximum_fusion.near_ref), channel_id=1, source_target_pairs={{0,1},{1,0},{2,3},{3,2},{4,5},{5,4},{6,7},{7,6},{8,9},{9,8},{10,11... | collective-permute-start | bytes 3145736 | tf_op jit(solution)/shard_map/ppermute | solution.py:129
  62.3 2.3 %collective-permute-done.3.far_ref = bf16[4,1024,128]{2,1,0:T(8,128)(2,1)S(1)} collective-permute-done((bf16[4,1024,128]{2,1,0:T(8,128)(2,1)S(1)}, bf16[4,1024,128]{2,1,0:T(8,128)(2,1)S(1)}, u32[]{:S(2)}, u32[]{:S(2)}) %collective-permute-start.3) | collective-permute-done | bytes 1048608 | tf_op jit(solution)/shard_map/ppermute | solution.py:129
  64.6 7.8 %all-to-all-done.1.parcel_ref = bf16[64,72,128]{2,1,0:T(8,128)(2,1)S(1)} async-done(((bf16[64,72,128]{2,1,0:T(8,128)(2,1)}), bf16[64,72,128]{2,1,0:T(8,128)(2,1)S(1)}, u32[]{:S(2)}, u32[]{:S(2)}) %all-to-all-start.1) | async-done | bytes 1179680 | tf_op jit(solution)/shard_map/all_to_all | solution.py:149
  72.4 2.3 %rotate.1 = bf16[8,512,128]{2,1,0:T(8,128)(2,1)} custom-call(bf16[64,72,128]{2,1,0:T(8,128)(2,1)S(1)} %all-to-all-done.1.parcel_ref, bf16[4,1024,128]{2,1,0:T(8,128)(2,1)S(1)} %pad_maximum_fusion.near_ref, bf16[4,1024,128]{2,1,0:T(8,128)(2,1)S(1)} %collective-permute-done.3.far_ref), custom_call_target="tpu_custom_call" | custom-call | tf_op jit(solution)/shard_map/rotate/pallas_call | solution.py:154
  74.7 3.6 %all-to-all-start.2 = ((bf16[8,512,128]{2,1,0:T(8,128)(2,1)}), bf16[8,512,128]{2,1,0:T(8,128)(2,1)S(1)}, u32[]{:S(2)}, u32[]{:S(2)}) async-start(bf16[8,512,128]{2,1,0:T(8,128)(2,1)} %rotate.1), calls=%async_computation.2 | async-start | bytes 2097152 | tf_op jit(solution)/shard_map/all_to_all | solution.py:163
  78.3 0.7 dynamic-slice_bitcast_fusion.1
  81.3 26.0 %all-to-all-done.2 = bf16[8,512,128]{2,1,0:T(8,128)(2,1)S(1)} async-done(((bf16[8,512,128]{2,1,0:T(8,128)(2,1)}), bf16[8,512,128]{2,1,0:T(8,128)(2,1)S(1)}, u32[]{:S(2)}, u32[]{:S(2)}) %all-to-all-start.2) | async-done | bytes 1048608 | tf_op jit(solution)/shard_map/all_to_all | solution.py:163
  107.9 10.2 %all_gather.3 = f32[8,2,128]{2,1,0:T(2,128)S(1)} all-gather(f32[1,2,128]{2,1,0:T(2,128)S(1)} %all_gather_reshape.3), channel_id=1, replica_groups=mesh['dp'=8,'tensor'=8,'x'=4,'core'=2] {'x','core'}, dimensions={0}, use_global_device_ids=true | all-gather | bytes 9216 | tf_op jit(solution)/shard_map/all_gather | solution.py:172
  118.1 15.6 %all_to_all.20.terms_ref = f32[64,2,128]{2,1,0:T(2,128)} all-to-all(f32[64,2,128]{2,1,0:T(2,128)S(1)} %broadcast_in_dim.29), channel_id=1, replica_groups=mesh['dp'=8,'tensor'=8,'x'=4,'core'=2] {'dp','tensor'}, dimensions={0} | all-to-all | bytes 131072 | tf_op jit(solution)/shard_map/all_to_all | solution.py:21
  133.7 1.6 %finish.1 = f32[16,16]{1,0:T(8,128)} custom-call(f32[64,2,128]{2,1,0:T(2,128)} %all_to_all.20.terms_ref), custom_call_target="tpu_custom_call" | custom-call | tf_op jit(solution)/shard_map/finish/pallas_call | solution.py:173
  (33 shorter events, 4.4 us)
Async XLA Ops:
  0.0 27.7 %collective-permute-start = (bf16[2,1024,128]{2,1,0:T(8,128)(2,1)}, bf16[2,1024,128]{2,1,0:T(8,128)(2,1)S(1)}, u32[]{:S(2)}, u32[]{:S(2)}) collective-permute-start(bf16[2,1024,128]{2,1,0:T(8,128)(2,1)} %param.13), channel_id=1, source_target_pairs={{4,0},{6,2},{0,4},{2,6},{5,1},{7,3},{1,5},{3,7},{12,8},{14,10},{8,... | collective-permute-start | bytes 1572872 | tf_op jit(solution)/shard_map/ppermute | solution.py:110
  7.2 20.9 %copy-start.2 = (bf16[2,2,64,128]{3,2,1,0:T(8,128)(2,1)S(1)}, bf16[2,2,64,128]{3,2,1,0:T(8,128)(2,1)}, u32[]{:S(2)}) copy-start(bf16[2,2,64,128]{3,2,1,0:T(8,128)(2,1)} %param.12) | copy-start | bytes 196612
  7.2 20.4 %all-to-all-start = ((f32[64,4,128]{2,1,0:T(4,128)}), f32[64,4,128]{2,1,0:T(4,128)S(1)}, u32[]{:S(2)}, u32[]{:S(2)}) async-start(f32[64,4,128]{2,1,0:T(4,128)} %get-tuple-element.11), calls=%async_computation | async-start | bytes 262144 | tf_op jit(solution)/shard_map/all_to_all | solution.py:106
  17.4 10.8 %copy-start.1 = (bf16[8,128]{1,0:T(8,128)(2,1)S(1)}, bf16[8,128]{1,0:T(8,128)(2,1)}, u32[]{:S(2)}) copy-start(bf16[8,128]{1,0:T(8,128)(2,1)} %get-tuple-element.15) | copy-start | bytes 6148
  29.5 12.4 %copy-start = (bf16[2,1024,128]{2,1,0:T(8,128)(2,1)S(1)}, bf16[2,1024,128]{2,1,0:T(8,128)(2,1)}, u32[]{:S(2)}) copy-start(bf16[2,1024,128]{2,1,0:T(8,128)(2,1)} %param.13) | copy-start | bytes 1572868
  29.5 42.9 %all-to-all-start.1 = ((bf16[64,72,128]{2,1,0:T(8,128)(2,1)}), bf16[64,72,128]{2,1,0:T(8,128)(2,1)S(1)}, u32[]{:S(2)}, u32[]{:S(2)}) async-start(bf16[64,72,128]{2,1,0:T(8,128)(2,1)} %bitcast.13), calls=%async_computation.1 | async-start | bytes 2359296 | tf_op jit(solution)/shard_map/all_to_all | solution.py:149
  41.9 14.3 %collective-permute-start.2 = (bf16[1024,128]{1,0:T(8,128)(2,1)S(1)}, bf16[1024,128]{1,0:T(8,128)(2,1)S(1)}, u32[]{:S(2)}, u32[]{:S(2)}) collective-permute-start(bf16[1024,128]{1,0:T(8,128)(2,1)S(1)} %get-tuple-element.20), channel_id=1, source_target_pairs={{6,0},{0,2},{2,4},{4,6},{7,1},{1,3},{3,5},{5,7},{14,8},{8,10},{10,... | collective-permute-start | bytes 786440 | tf_op jit(solution)/shard_map/ppermute | solution.py:110
  45.2 13.1 %collective-permute-start.1 = (bf16[1024,128]{1,0:T(8,128)(2,1)S(1)}, bf16[1024,128]{1,0:T(8,128)(2,1)S(1)}, u32[]{:S(2)}, u32[]{:S(2)}) collective-permute-start(bf16[1024,128]{1,0:T(8,128)(2,1)S(1)} %get-tuple-element.20), channel_id=1, source_target_pairs={{2,0},{4,2},{6,4},{0,6},{3,1},{5,3},{7,5},{1,7},{10,8},{12,10},{14... | collective-permute-start | bytes 786440 | tf_op jit(solution)/shard_map/ppermute | solution.py:110
  58.4 6.2 %collective-permute-start.3 = (bf16[4,1024,128]{2,1,0:T(8,128)(2,1)S(1)}, bf16[4,1024,128]{2,1,0:T(8,128)(2,1)S(1)}, u32[]{:S(2)}, u32[]{:S(2)}) collective-permute-start(bf16[4,1024,128]{2,1,0:T(8,128)(2,1)S(1)} %pad_maximum_fusion.near_ref), channel_id=1, source_target_pairs={{0,1},{1,0},{2,3},{3,2},{4,5},{5,4},{6,7},{7,6},{8,9},{9,8},{10,11... | collective-permute-start | bytes 3145736 | tf_op jit(solution)/shard_map/ppermute | solution.py:129
  74.7 32.7 %all-to-all-start.2 = ((bf16[8,512,128]{2,1,0:T(8,128)(2,1)}), bf16[8,512,128]{2,1,0:T(8,128)(2,1)S(1)}, u32[]{:S(2)}, u32[]{:S(2)}) async-start(bf16[8,512,128]{2,1,0:T(8,128)(2,1)} %rotate.1), calls=%async_computation.2 | async-start | bytes 2097152 | tf_op jit(solution)/shard_map/all_to_all | solution.py:163
  79.0 1.6 %collective-permute-start.4 = (f32[16,128]{1,0:T(8,128)S(1)}, f32[16,128]{1,0:T(8,128)S(1)}, u32[]{:S(2)}, u32[]{:S(2)}) collective-permute-start(f32[16,128]{1,0:T(8,128)S(1)} %dynamic-slice_bitcast_fusion.1), channel_id=1, source_target_pairs={{0,0},{1,1},{2,2},{3,3},{4,4},{5,5},{6,6},{7,7},{9,8},{8,9},{11,10... | collective-permute-start | bytes 24584 | tf_op jit(solution)/shard_map/ppermute | solution.py:94

commit v9 on v8

--- a/solution.py
+++ b/solution.py
@@ -37,15 +37,6 @@
             rest = rest - term
     terms.append(jnp.zeros((sums_ref.shape[0] - 3 * MODULES, width), jnp.float32))
     sums_ref[...] = jnp.concatenate(terms, axis=0).astype(jnp.bfloat16)
-
-
-def finish_kernel(terms_ref, out_ref):
-    total = jnp.sum(terms_ref[...], axis=0)
-    size = out_ref.shape[1]
-    per_row = total.shape[1] // size
-    for row in range(out_ref.shape[0]):
-        left = row % per_row * size
-        out_ref[row : row + 1, :] = total[row // per_row : row // per_row + 1, left : left + size]
 
 
 def rotate_kernel(parcel_ref, near_ref, far_ref, out_ref, rows_ref):
@@ -170,13 +161,7 @@
     )
     shape = scores.shape
     scores = jnp.sum(lax.all_gather(scores.reshape(2, -1), FACTOR, axis=0), axis=0)
-    return pl.pallas_call(
-        finish_kernel,
-        out_shape=jax.ShapeDtypeStruct(shape, jnp.float32),
-        in_specs=[pl.BlockSpec(memory_space=pltpu.VMEM)],
-        out_specs=pl.BlockSpec(memory_space=pltpu.VMEM),
-        name="finish",
-    )(everywhere(scores, ("dp", "tensor")))
+    return jnp.sum(everywhere(scores, ("dp", "tensor")), axis=0).reshape(shape)
 
 
 def solution(mesh):

time: 136 us -> 135 us (level)
  Pallas kernels: 5.55 us -> 3.97 us
    pallas_call x1 -> x0, Pallas kernels: 1.58 us -> none  [body(): pl.pallas_call(finish_kernel, out_shape=jax.ShapeDtypeStruct(shape, jnp.f...]
where the time goes in v9:
time: 135 us; the launch traced here: 134 us
  waiting for transfers between devices  52.9 us (39%)
  starting transfers between devices  41.7 us (31%)
  blocking collectives  25.4 us (19%)
  other arithmetic  4.7 us (3%)
  local copies, waits for them, and re-layouts  4.33 us (3%)
  Pallas kernels  3.97 us (3%)
    all_to_all x1, waiting for transfers between devices, body(): partial = lax.all_to_all(partial, 'tensor', 0, 0, tiled=True)  26 us
    all_to_all x1, blocking collectives, everywhere(): return lax.all_to_all(terms, axes, 0, 0, tiled=True)  15.3 us
    all_to_all x1, starting transfers between devices, body(): parcel = lax.all_to_all(parcel, ('dp',) + FACTOR, 0, 0, tiled=True)  12.3 us
    ppermute x3, starting transfers between devices, shifted(): return lax.ppermute(value, 'x', [((k + step) % n_x, k) for k in range(n_x)])  12 us
    all_gather x1, blocking collectives, body(): lax.all_gather(scores.reshape(2, -1), FACTOR, axis=0)  10.2 us
    ppermute x3, waiting for transfers between devices, shifted(): return lax.ppermute(value, 'x', [((k + step) % n_x, k) for k in range(n_x)])  9.82 us
    all_to_all x1, starting transfers between devices, body(): squares = lax.all_to_all(squares, ('tensor',) + FACTOR, 0, 0, tiled=True)  9.32 us
    all_to_all x1, waiting for transfers between devices, body(): parcel = lax.all_to_all(parcel, ('dp',) + FACTOR, 0, 0, tiled=True)  7.85 us
  transfers between devices with their start and end apart: 8, of which 6 were waited for; matrix products, arithmetic and copies ran while one was open for 5% of the time, Pallas kernels for 1%

profile of v9, /device:TPU:1, one launch (start us, length us, event | category | flops | bytes accessed | tf_op | source)
XLA Modules:
  0.0 134.2 jit_solution(17117745300403180407)
XLA Ops:
  0.0 5.5 %collective-permute-start = (bf16[2,1024,128]{2,1,0:T(8,128)(2,1)}, bf16[2,1024,128]{2,1,0:T(8,128)(2,1)S(1)}, u32[]{:S(2)}, u32[]{:S(2)}) collective-permute-start(bf16[2,1024,128]{2,1,0:T(8,128)(2,1)} %param.13), channel_id=1, source_target_pairs={{4,0},{6,2},{0,4},{2,6},{5,1},{7,3},{1,5},{3,7},{12,8},{14,10},{8,... | collective-permute-start | bytes 1572872 | tf_op jit(solution)/shard_map/ppermute | solution.py:101
  5.5 1.7 %prologue.1 = (f32[64,4,128]{2,1,0:T(4,128)}, bf16[8,128]{1,0:T(8,128)(2,1)}) custom-call(bf16[512,128]{1,0:T(8,128)(2,1)} %resid_ref.1, f32[2,64,128]{2,1,0:T(8,128)} %eigen_ref.1), custom_call_target="tpu_custom_call" | custom-call | tf_op jit(solution)/shard_map/prologue/pallas_call | solution.py:87
  7.2 9.3 %all-to-all-start = ((f32[64,4,128]{2,1,0:T(4,128)}), f32[64,4,128]{2,1,0:T(4,128)S(1)}, u32[]{:S(2)}, u32[]{:S(2)}) async-start(f32[64,4,128]{2,1,0:T(4,128)} %get-tuple-element.11), calls=%async_computation | async-start | bytes 262144 | tf_op jit(solution)/shard_map/all_to_all | solution.py:97
  16.5 0.9 convert_element_type.27
  17.5 0.9 copy.32
  19.0 0.7 compare_reduce_fusion.1
  19.7 0.9 select_bitcast_fusion.1
  20.6 7.0 %all-to-all-done = f32[64,4,128]{2,1,0:T(4,128)S(1)} async-done(((f32[64,4,128]{2,1,0:T(4,128)}), f32[64,4,128]{2,1,0:T(4,128)S(1)}, u32[]{:S(2)}, u32[]{:S(2)}) %all-to-all-start) | async-done | bytes 131104 | tf_op jit(solution)/shard_map/all_to_all | solution.py:97
  28.3 1.2 broadcast_in_dim.28
  29.5 12.3 %all-to-all-start.1 = ((bf16[64,72,128]{2,1,0:T(8,128)(2,1)}), bf16[64,72,128]{2,1,0:T(8,128)(2,1)S(1)}, u32[]{:S(2)}, u32[]{:S(2)}) async-start(bf16[64,72,128]{2,1,0:T(8,128)(2,1)} %bitcast.13), calls=%async_computation.1 | async-start | bytes 2359296 | tf_op jit(solution)/shard_map/all_to_all | solution.py:140
  41.9 3.3 %collective-permute-start.2 = (bf16[1024,128]{1,0:T(8,128)(2,1)S(1)}, bf16[1024,128]{1,0:T(8,128)(2,1)S(1)}, u32[]{:S(2)}, u32[]{:S(2)}) collective-permute-start(bf16[1024,128]{1,0:T(8,128)(2,1)S(1)} %get-tuple-element.20), channel_id=1, source_target_pairs={{6,0},{0,2},{2,4},{4,6},{7,1},{1,3},{3,5},{5,7},{14,8},{8,10},{10,... | collective-permute-start | bytes 786440 | tf_op jit(solution)/shard_map/ppermute | solution.py:101
  45.2 3.2 %collective-permute-start.1 = (bf16[1024,128]{1,0:T(8,128)(2,1)S(1)}, bf16[1024,128]{1,0:T(8,128)(2,1)S(1)}, u32[]{:S(2)}, u32[]{:S(2)}) collective-permute-start(bf16[1024,128]{1,0:T(8,128)(2,1)S(1)} %get-tuple-element.20), channel_id=1, source_target_pairs={{2,0},{4,2},{6,4},{0,6},{3,1},{5,3},{7,5},{1,7},{10,8},{12,10},{14... | collective-permute-start | bytes 786440 | tf_op jit(solution)/shard_map/ppermute | solution.py:101
  48.4 7.8 %collective-permute-done.2 = bf16[1024,128]{1,0:T(8,128)(2,1)S(1)} collective-permute-done((bf16[1024,128]{1,0:T(8,128)(2,1)S(1)}, bf16[1024,128]{1,0:T(8,128)(2,1)S(1)}, u32[]{:S(2)}, u32[]{:S(2)}) %collective-permute-start.2) | collective-permute-done | bytes 262176 | tf_op jit(solution)/shard_map/ppermute | solution.py:101
  56.2 2.0 %collective-permute-done.1 = bf16[1024,128]{1,0:T(8,128)(2,1)S(1)} collective-permute-done((bf16[1024,128]{1,0:T(8,128)(2,1)S(1)}, bf16[1024,128]{1,0:T(8,128)(2,1)S(1)}, u32[]{:S(2)}, u32[]{:S(2)}) %collective-permute-start.1) | collective-permute-done | bytes 262176 | tf_op jit(solution)/shard_map/ppermute | solution.py:101
  58.4 3.9 %collective-permute-start.3 = (bf16[4,1024,128]{2,1,0:T(8,128)(2,1)S(1)}, bf16[4,1024,128]{2,1,0:T(8,128)(2,1)S(1)}, u32[]{:S(2)}, u32[]{:S(2)}) collective-permute-start(bf16[4,1024,128]{2,1,0:T(8,128)(2,1)S(1)} %pad_maximum_fusion.near_ref), channel_id=1, source_target_pairs={{0,1},{1,0},{2,3},{3,2},{4,5},{5,4},{6,7},{7,6},{8,9},{9,8},{10,11... | collective-permute-start | bytes 3145736 | tf_op jit(solution)/shard_map/ppermute | solution.py:120
  62.3 2.3 %collective-permute-done.3.far_ref = bf16[4,1024,128]{2,1,0:T(8,128)(2,1)S(1)} collective-permute-done((bf16[4,1024,128]{2,1,0:T(8,128)(2,1)S(1)}, bf16[4,1024,128]{2,1,0:T(8,128)(2,1)S(1)}, u32[]{:S(2)}, u32[]{:S(2)}) %collective-permute-start.3) | collective-permute-done | bytes 1048608 | tf_op jit(solution)/shard_map/ppermute | solution.py:120
  64.6 7.8 %all-to-all-done.1.parcel_ref = bf16[64,72,128]{2,1,0:T(8,128)(2,1)S(1)} async-done(((bf16[64,72,128]{2,1,0:T(8,128)(2,1)}), bf16[64,72,128]{2,1,0:T(8,128)(2,1)S(1)}, u32[]{:S(2)}, u32[]{:S(2)}) %all-to-all-start.1) | async-done | bytes 1179680 | tf_op jit(solution)/shard_map/all_to_all | solution.py:140
  72.4 2.3 %rotate.1 = bf16[8,512,128]{2,1,0:T(8,128)(2,1)} custom-call(bf16[64,72,128]{2,1,0:T(8,128)(2,1)S(1)} %all-to-all-done.1.parcel_ref, bf16[4,1024,128]{2,1,0:T(8,128)(2,1)S(1)} %pad_maximum_fusion.near_ref, bf16[4,1024,128]{2,1,0:T(8,128)(2,1)S(1)} %collective-permute-done.3.far_ref), custom_call_target="tpu_custom_call" | custom-call | tf_op jit(solution)/shard_map/rotate/pallas_call | solution.py:145
  74.7 3.6 %all-to-all-start.2 = ((bf16[8,512,128]{2,1,0:T(8,128)(2,1)}), bf16[8,512,128]{2,1,0:T(8,128)(2,1)S(1)}, u32[]{:S(2)}, u32[]{:S(2)}) async-start(bf16[8,512,128]{2,1,0:T(8,128)(2,1)} %rotate.1), calls=%async_computation.2 | async-start | bytes 2097152 | tf_op jit(solution)/shard_map/all_to_all | solution.py:154
  78.3 0.7 dynamic-slice_bitcast_fusion.1
  81.3 26.0 %all-to-all-done.2 = bf16[8,512,128]{2,1,0:T(8,128)(2,1)S(1)} async-done(((bf16[8,512,128]{2,1,0:T(8,128)(2,1)}), bf16[8,512,128]{2,1,0:T(8,128)(2,1)S(1)}, u32[]{:S(2)}, u32[]{:S(2)}) %all-to-all-start.2) | async-done | bytes 1048608 | tf_op jit(solution)/shard_map/all_to_all | solution.py:154
  107.9 10.2 %all_gather.3 = f32[8,2,128]{2,1,0:T(2,128)S(1)} all-gather(f32[1,2,128]{2,1,0:T(2,128)S(1)} %all_gather_reshape.3), channel_id=1, replica_groups=mesh['dp'=8,'tensor'=8,'x'=4,'core'=2] {'x','core'}, dimensions={0}, use_global_device_ids=true | all-gather | bytes 9216 | tf_op jit(solution)/shard_map/all_gather | solution.py:163
  118.1 15.3 %all_to_all.20 = f32[64,2,128]{2,1,0:T(2,128)S(1)} all-to-all(f32[64,2,128]{2,1,0:T(2,128)S(1)} %broadcast_in_dim.29), channel_id=1, replica_groups=mesh['dp'=8,'tensor'=8,'x'=4,'core'=2] {'dp','tensor'}, dimensions={0} | all-to-all | bytes 131072 | tf_op jit(solution)/shard_map/all_to_all | solution.py:21
  133.5 0.7 reshape.47
  (34 shorter events, 4.5 us)
Async XLA Ops:
  0.0 27.7 %collective-permute-start = (bf16[2,1024,128]{2,1,0:T(8,128)(2,1)}, bf16[2,1024,128]{2,1,0:T(8,128)(2,1)S(1)}, u32[]{:S(2)}, u32[]{:S(2)}) collective-permute-start(bf16[2,1024,128]{2,1,0:T(8,128)(2,1)} %param.13), channel_id=1, source_target_pairs={{4,0},{6,2},{0,4},{2,6},{5,1},{7,3},{1,5},{3,7},{12,8},{14,10},{8,... | collective-permute-start | bytes 1572872 | tf_op jit(solution)/shard_map/ppermute | solution.py:101
  7.2 20.9 %copy-start.2 = (bf16[2,2,64,128]{3,2,1,0:T(8,128)(2,1)S(1)}, bf16[2,2,64,128]{3,2,1,0:T(8,128)(2,1)}, u32[]{:S(2)}) copy-start(bf16[2,2,64,128]{3,2,1,0:T(8,128)(2,1)} %param.12) | copy-start | bytes 196612
  7.2 20.4 %all-to-all-start = ((f32[64,4,128]{2,1,0:T(4,128)}), f32[64,4,128]{2,1,0:T(4,128)S(1)}, u32[]{:S(2)}, u32[]{:S(2)}) async-start(f32[64,4,128]{2,1,0:T(4,128)} %get-tuple-element.11), calls=%async_computation | async-start | bytes 262144 | tf_op jit(solution)/shard_map/all_to_all | solution.py:97
  17.4 10.8 %copy-start.1 = (bf16[8,128]{1,0:T(8,128)(2,1)S(1)}, bf16[8,128]{1,0:T(8,128)(2,1)}, u32[]{:S(2)}) copy-start(bf16[8,128]{1,0:T(8,128)(2,1)} %get-tuple-element.15) | copy-start | bytes 6148
  29.5 12.4 %copy-start = (bf16[2,1024,128]{2,1,0:T(8,128)(2,1)S(1)}, bf16[2,1024,128]{2,1,0:T(8,128)(2,1)}, u32[]{:S(2)}) copy-start(bf16[2,1024,128]{2,1,0:T(8,128)(2,1)} %param.13) | copy-start | bytes 1572868
  29.5 42.9 %all-to-all-start.1 = ((bf16[64,72,128]{2,1,0:T(8,128)(2,1)}), bf16[64,72,128]{2,1,0:T(8,128)(2,1)S(1)}, u32[]{:S(2)}, u32[]{:S(2)}) async-start(bf16[64,72,128]{2,1,0:T(8,128)(2,1)} %bitcast.13), calls=%async_computation.1 | async-start | bytes 2359296 | tf_op jit(solution)/shard_map/all_to_all | solution.py:140
  41.9 14.3 %collective-permute-start.2 = (bf16[1024,128]{1,0:T(8,128)(2,1)S(1)}, bf16[1024,128]{1,0:T(8,128)(2,1)S(1)}, u32[]{:S(2)}, u32[]{:S(2)}) collective-permute-start(bf16[1024,128]{1,0:T(8,128)(2,1)S(1)} %get-tuple-element.20), channel_id=1, source_target_pairs={{6,0},{0,2},{2,4},{4,6},{7,1},{1,3},{3,5},{5,7},{14,8},{8,10},{10,... | collective-permute-start | bytes 786440 | tf_op jit(solution)/shard_map/ppermute | solution.py:101
  45.2 13.1 %collective-permute-start.1 = (bf16[1024,128]{1,0:T(8,128)(2,1)S(1)}, bf16[1024,128]{1,0:T(8,128)(2,1)S(1)}, u32[]{:S(2)}, u32[]{:S(2)}) collective-permute-start(bf16[1024,128]{1,0:T(8,128)(2,1)S(1)} %get-tuple-element.20), channel_id=1, source_target_pairs={{2,0},{4,2},{6,4},{0,6},{3,1},{5,3},{7,5},{1,7},{10,8},{12,10},{14... | collective-permute-start | bytes 786440 | tf_op jit(solution)/shard_map/ppermute | solution.py:101
  58.4 6.2 %collective-permute-start.3 = (bf16[4,1024,128]{2,1,0:T(8,128)(2,1)S(1)}, bf16[4,1024,128]{2,1,0:T(8,128)(2,1)S(1)}, u32[]{:S(2)}, u32[]{:S(2)}) collective-permute-start(bf16[4,1024,128]{2,1,0:T(8,128)(2,1)S(1)} %pad_maximum_fusion.near_ref), channel_id=1, source_target_pairs={{0,1},{1,0},{2,3},{3,2},{4,5},{5,4},{6,7},{7,6},{8,9},{9,8},{10,11... | collective-permute-start | bytes 3145736 | tf_op jit(solution)/shard_map/ppermute | solution.py:120
  74.7 32.7 %all-to-all-start.2 = ((bf16[8,512,128]{2,1,0:T(8,128)(2,1)}), bf16[8,512,128]{2,1,0:T(8,128)(2,1)S(1)}, u32[]{:S(2)}, u32[]{:S(2)}) async-start(bf16[8,512,128]{2,1,0:T(8,128)(2,1)} %rotate.1), calls=%async_computation.2 | async-start | bytes 2097152 | tf_op jit(solution)/shard_map/all_to_all | solution.py:154
  79.0 1.6 %collective-permute-start.4 = (f32[16,128]{1,0:T(8,128)S(1)}, f32[16,128]{1,0:T(8,128)S(1)}, u32[]{:S(2)}, u32[]{:S(2)}) collective-permute-start(f32[16,128]{1,0:T(8,128)S(1)} %dynamic-slice_bitcast_fusion.1), channel_id=1, source_target_pairs={{0,0},{1,1},{2,2},{3,3},{4,4},{5,5},{6,6},{7,7},{9,8},{8,9},{11,10... | collective-permute-start | bytes 24584 | tf_op jit(solution)/shard_map/ppermute | solution.py:85

commit v10 on v9

--- a/solution.py
+++ b/solution.py
@@ -107,9 +107,7 @@
     ]
     weighted = jnp.stack(masked).reshape(-1, tokens)
     values = resid.astype(jnp.float32)
-    totals, weighted, values, *across = lax.optimization_barrier(
-        (totals, weighted, values, *across)
-    )
+    totals, weighted, values = lax.optimization_barrier((totals, weighted, values))
     pick = functools.partial(lax.dynamic_index_in_dim, axis=0, keepdims=False)
     own, rest = pick(input_basis, module), pick(input_basis, 1 - module)
     near = [own] + [
@@ -137,6 +135,7 @@
     )
     parcel = jnp.broadcast_to(parcel, (n_dp,) + parcel.shape)
     parcel = parcel.reshape((n_dp * n_f,) + parcel.shape[-2:])
+    parcel, *across = lax.optimization_barrier((parcel, *across))
     parcel = lax.all_to_all(parcel, ("dp",) + FACTOR, 0, 0, tiled=True)
     sums = parcel[:, rows_dev : rows_dev + 3 * MODULES].astype(jnp.float32)
     sums = jnp.sum(sums.reshape(-1, MODULES, 3 * width), axis=(0, 2))

time: 135 us -> 142 us (1.052)
  starting transfers between devices: 41.7 us -> 47.7 us
  waiting for transfers between devices: 52.9 us -> 54.5 us
    ppermute x3, waiting for transfers between devices: 9.82 us -> 16 us  [shifted(): return lax.ppermute(value, 'x', [((k + step) % n_x, k) for k in range(n_x)])]
    all_to_all x1, waiting for transfers between devices: 6.98 us -> 2.17 us  [body(): squares = lax.all_to_all(squares, ('tensor',) + FACTOR, 0, 0, tiled=True)]
    all_to_all x1, starting transfers between devices: 3.56 us -> 6.21 us  [body(): partial = lax.all_to_all(partial, 'tensor', 0, 0, tiled=True)]
    all_to_all x1, starting transfers between devices: 9.32 us -> 11.8 us  [body(): squares = lax.all_to_all(squares, ('tensor',) + FACTOR, 0, 0, tiled=True)]
    all_to_all x1, starting transfers between devices: 12.3 us -> 13.9 us  [body(): parcel = lax.all_to_all(parcel, ('dp',) + FACTOR, 0, 0, tiled=True)]
  transfers between devices with their start and end apart: 8 -> 8, of which waited for: 6 -> 7; matrix products, arithmetic and copies ran while one was open for 5% -> 5% of each run, Pallas kernels for 1% -> 0%
where the time goes in v10:
time: 142 us
  waiting for transfers between devices  54.5 us (38%)
  starting transfers between devices  47.7 us (34%)
  blocking collectives  25.4 us (18%)
  other arithmetic  4.7 us (3%)
  local copies, waits for them, and re-layouts  4.32 us (3%)
  Pallas kernels  3.96 us (3%)
    all_to_all x1, waiting for transfers between devices, body(): partial = lax.all_to_all(partial, 'tensor', 0, 0, tiled=True)  26.2 us
    ppermute x3, waiting for transfers between devices, shifted(): return lax.ppermute(value, 'x', [((k + step) % n_x, k) for k in range(n_x)])  16 us
    all_to_all x1, blocking collectives, everywhere(): return lax.all_to_all(terms, axes, 0, 0, tiled=True)  15.3 us
    all_to_all x1, starting transfers between devices, body(): parcel = lax.all_to_all(parcel, ('dp',) + FACTOR, 0, 0, tiled=True)  13.9 us
    all_to_all x1, starting transfers between devices, body(): squares = lax.all_to_all(squares, ('tensor',) + FACTOR, 0, 0, tiled=True)  11.8 us
    ppermute x3, starting transfers between devices, shifted(): return lax.ppermute(value, 'x', [((k + step) % n_x, k) for k in range(n_x)])  11.3 us
    all_gather x1, blocking collectives, body(): lax.all_gather(scores.reshape(2, -1), FACTOR, axis=0)  10.2 us
    all_to_all x1, waiting for transfers between devices, body(): parcel = lax.all_to_all(parcel, ('dp',) + FACTOR, 0, 0, tiled=True)  7.85 us
  transfers between devices with their start and end apart: 8, of which 7 were waited for; matrix products, arithmetic and copies ran while one was open for 5% of the time, Pallas kernels for 0%

profile of v10, /device:TPU:1, one launch (start us, length us, event | category | flops | bytes accessed | tf_op | source)
XLA Modules:
  0.0 141.6 jit_solution(9868086425941112904)
XLA Ops:
  0.0 1.7 %prologue.1 = (f32[64,4,128]{2,1,0:T(4,128)}, bf16[8,128]{1,0:T(8,128)(2,1)}) custom-call(bf16[512,128]{1,0:T(8,128)(2,1)} %resid_ref.1, f32[2,64,128]{2,1,0:T(8,128)} %eigen_ref.1), custom_call_target="tpu_custom_call" | custom-call | tf_op jit(solution)/shard_map/prologue/pallas_call | solution.py:87
  1.7 11.8 %all-to-all-start = ((f32[64,4,128]{2,1,0:T(4,128)}), f32[64,4,128]{2,1,0:T(4,128)S(1)}, u32[]{:S(2)}, u32[]{:S(2)}) async-start(f32[64,4,128]{2,1,0:T(4,128)} %get-tuple-element.11), calls=%async_computation | async-start | bytes 262144 | tf_op jit(solution)/shard_map/all_to_all | solution.py:97
  13.5 4.8 %collective-permute-start = (bf16[2,1024,128]{2,1,0:T(8,128)(2,1)}, bf16[2,1024,128]{2,1,0:T(8,128)(2,1)S(1)}, u32[]{:S(2)}, u32[]{:S(2)}) collective-permute-start(bf16[2,1024,128]{2,1,0:T(8,128)(2,1)} %param.13), channel_id=1, source_target_pairs={{4,0},{6,2},{0,4},{2,6},{5,1},{7,3},{1,5},{3,7},{12,8},{14,10},{8,... | collective-permute-start | bytes 1572872 | tf_op jit(solution)/shard_map/ppermute | solution.py:101
  18.3 0.9 convert_element_type.27
  19.2 0.9 copy.32
  20.1 0.7 compare_reduce_fusion.1
  21.4 0.9 select_bitcast_fusion.1
  22.4 2.2 %all-to-all-done = f32[64,4,128]{2,1,0:T(4,128)S(1)} async-done(((f32[64,4,128]{2,1,0:T(4,128)}), f32[64,4,128]{2,1,0:T(4,128)S(1)}, u32[]{:S(2)}, u32[]{:S(2)}) %all-to-all-start) | async-done | bytes 131104 | tf_op jit(solution)/shard_map/all_to_all | solution.py:97
  25.3 6.2 %collective-permute-done = bf16[2,1024,128]{2,1,0:T(8,128)(2,1)S(1)} collective-permute-done((bf16[2,1024,128]{2,1,0:T(8,128)(2,1)}, bf16[2,1024,128]{2,1,0:T(8,128)(2,1)S(1)}, u32[]{:S(2)}, u32[]{:S(2)}) %collective-permute-start) | collective-permute-done | bytes 524320 | tf_op jit(solution)/shard_map/ppermute | solution.py:101
  31.4 1.2 broadcast_in_dim.28
  32.6 13.9 %all-to-all-start.1 = ((bf16[64,72,128]{2,1,0:T(8,128)(2,1)}), bf16[64,72,128]{2,1,0:T(8,128)(2,1)S(1)}, u32[]{:S(2)}, u32[]{:S(2)}) async-start(bf16[64,72,128]{2,1,0:T(8,128)(2,1)} %bitcast.13), calls=%async_computation.1 | async-start | bytes 2359296 | tf_op jit(solution)/shard_map/all_to_all | solution.py:139
  46.6 3.3 %collective-permute-start.2 = (bf16[1024,128]{1,0:T(8,128)(2,1)S(1)}, bf16[1024,128]{1,0:T(8,128)(2,1)S(1)}, u32[]{:S(2)}, u32[]{:S(2)}) collective-permute-start(bf16[1024,128]{1,0:T(8,128)(2,1)S(1)} %get-tuple-element.20), channel_id=1, source_target_pairs={{6,0},{0,2},{2,4},{4,6},{7,1},{1,3},{3,5},{5,7},{14,8},{8,10},{10,... | collective-permute-start | bytes 786440 | tf_op jit(solution)/shard_map/ppermute | solution.py:101
  49.9 3.2 %collective-permute-start.1 = (bf16[1024,128]{1,0:T(8,128)(2,1)S(1)}, bf16[1024,128]{1,0:T(8,128)(2,1)S(1)}, u32[]{:S(2)}, u32[]{:S(2)}) collective-permute-start(bf16[1024,128]{1,0:T(8,128)(2,1)S(1)} %get-tuple-element.20), channel_id=1, source_target_pairs={{2,0},{4,2},{6,4},{0,6},{3,1},{5,3},{7,5},{1,7},{10,8},{12,10},{14... | collective-permute-start | bytes 786440 | tf_op jit(solution)/shard_map/ppermute | solution.py:101
  53.1 7.8 %collective-permute-done.2 = bf16[1024,128]{1,0:T(8,128)(2,1)S(1)} collective-permute-done((bf16[1024,128]{1,0:T(8,128)(2,1)S(1)}, bf16[1024,128]{1,0:T(8,128)(2,1)S(1)}, u32[]{:S(2)}, u32[]{:S(2)}) %collective-permute-start.2) | collective-permute-done | bytes 262176 | tf_op jit(solution)/shard_map/ppermute | solution.py:101
  60.9 2.0 %collective-permute-done.1 = bf16[1024,128]{1,0:T(8,128)(2,1)S(1)} collective-permute-done((bf16[1024,128]{1,0:T(8,128)(2,1)S(1)}, bf16[1024,128]{1,0:T(8,128)(2,1)S(1)}, u32[]{:S(2)}, u32[]{:S(2)}) %collective-permute-start.1) | collective-permute-done | bytes 262176 | tf_op jit(solution)/shard_map/ppermute | solution.py:101
  63.1 3.9 %collective-permute-start.3 = (bf16[4,1024,128]{2,1,0:T(8,128)(2,1)S(1)}, bf16[4,1024,128]{2,1,0:T(8,128)(2,1)S(1)}, u32[]{:S(2)}, u32[]{:S(2)}) collective-permute-start(bf16[4,1024,128]{2,1,0:T(8,128)(2,1)S(1)} %pad_maximum_fusion.near_ref), channel_id=1, source_target_pairs={{0,1},{1,0},{2,3},{3,2},{4,5},{5,4},{6,7},{7,6},{8,9},{9,8},{10,11... | collective-permute-start | bytes 3145736 | tf_op jit(solution)/shard_map/ppermute | solution.py:118
  67.0 2.3 %collective-permute-done.3.far_ref = bf16[4,1024,128]{2,1,0:T(8,128)(2,1)S(1)} collective-permute-done((bf16[4,1024,128]{2,1,0:T(8,128)(2,1)S(1)}, bf16[4,1024,128]{2,1,0:T(8,128)(2,1)S(1)}, u32[]{:S(2)}, u32[]{:S(2)}) %collective-permute-start.3) | collective-permute-done | bytes 1048608 | tf_op jit(solution)/shard_map/ppermute | solution.py:118
  69.2 7.8 %all-to-all-done.1.parcel_ref = bf16[64,72,128]{2,1,0:T(8,128)(2,1)S(1)} async-done(((bf16[64,72,128]{2,1,0:T(8,128)(2,1)}), bf16[64,72,128]{2,1,0:T(8,128)(2,1)S(1)}, u32[]{:S(2)}, u32[]{:S(2)}) %all-to-all-start.1) | async-done | bytes 1179680 | tf_op jit(solution)/shard_map/all_to_all | solution.py:139
  77.1 2.3 %rotate.1 = bf16[8,512,128]{2,1,0:T(8,128)(2,1)} custom-call(bf16[64,72,128]{2,1,0:T(8,128)(2,1)S(1)} %all-to-all-done.1.parcel_ref, bf16[4,1024,128]{2,1,0:T(8,128)(2,1)S(1)} %pad_maximum_fusion.near_ref, bf16[4,1024,128]{2,1,0:T(8,128)(2,1)S(1)} %collective-permute-done.3.far_ref), custom_call_target="tpu_custom_call" | custom-call | tf_op jit(solution)/shard_map/rotate/pallas_call | solution.py:144
  79.3 6.2 %all-to-all-start.2 = ((bf16[8,512,128]{2,1,0:T(8,128)(2,1)}), bf16[8,512,128]{2,1,0:T(8,128)(2,1)S(1)}, u32[]{:S(2)}, u32[]{:S(2)}) async-start(bf16[8,512,128]{2,1,0:T(8,128)(2,1)} %rotate.1), calls=%async_computation.2 | async-start | bytes 2097152 | tf_op jit(solution)/shard_map/all_to_all | solution.py:153
  85.5 0.7 dynamic-slice_bitcast_fusion.1
  88.5 26.2 %all-to-all-done.2 = bf16[8,512,128]{2,1,0:T(8,128)(2,1)S(1)} async-done(((bf16[8,512,128]{2,1,0:T(8,128)(2,1)}), bf16[8,512,128]{2,1,0:T(8,128)(2,1)S(1)}, u32[]{:S(2)}, u32[]{:S(2)}) %all-to-all-start.2) | async-done | bytes 1048608 | tf_op jit(solution)/shard_map/all_to_all | solution.py:153
  115.3 10.2 %all_gather.3 = f32[8,2,128]{2,1,0:T(2,128)S(1)} all-gather(f32[1,2,128]{2,1,0:T(2,128)S(1)} %all_gather_reshape.3), channel_id=1, replica_groups=mesh['dp'=8,'tensor'=8,'x'=4,'core'=2] {'x','core'}, dimensions={0}, use_global_device_ids=true | all-gather | bytes 9216 | tf_op jit(solution)/shard_map/all_gather | solution.py:162
  125.5 15.3 %all_to_all.20 = f32[64,2,128]{2,1,0:T(2,128)S(1)} all-to-all(f32[64,2,128]{2,1,0:T(2,128)S(1)} %broadcast_in_dim.29), channel_id=1, replica_groups=mesh['dp'=8,'tensor'=8,'x'=4,'core'=2] {'dp','tensor'}, dimensions={0} | all-to-all | bytes 131072 | tf_op jit(solution)/shard_map/all_to_all | solution.py:21
  (34 shorter events, 5.2 us)
Async XLA Ops:
  1.7 23.3 %copy-start.2 = (bf16[2,2,64,128]{3,2,1,0:T(8,128)(2,1)S(1)}, bf16[2,2,64,128]{3,2,1,0:T(8,128)(2,1)}, u32[]{:S(2)}) copy-start(bf16[2,2,64,128]{3,2,1,0:T(8,128)(2,1)} %param.12) | copy-start | bytes 196612
  1.7 22.9 %all-to-all-start = ((f32[64,4,128]{2,1,0:T(4,128)}), f32[64,4,128]{2,1,0:T(4,128)S(1)}, u32[]{:S(2)}, u32[]{:S(2)}) async-start(f32[64,4,128]{2,1,0:T(4,128)} %get-tuple-element.11), calls=%async_computation | async-start | bytes 262144 | tf_op jit(solution)/shard_map/all_to_all | solution.py:97
  13.5 17.9 %collective-permute-start = (bf16[2,1024,128]{2,1,0:T(8,128)(2,1)}, bf16[2,1024,128]{2,1,0:T(8,128)(2,1)S(1)}, u32[]{:S(2)}, u32[]{:S(2)}) collective-permute-start(bf16[2,1024,128]{2,1,0:T(8,128)(2,1)} %param.13), channel_id=1, source_target_pairs={{4,0},{6,2},{0,4},{2,6},{5,1},{7,3},{1,5},{3,7},{12,8},{14,10},{8,... | collective-permute-start | bytes 1572872 | tf_op jit(solution)/shard_map/ppermute | solution.py:101
  19.2 6.0 %copy-start.1 = (bf16[8,128]{1,0:T(8,128)(2,1)S(1)}, bf16[8,128]{1,0:T(8,128)(2,1)}, u32[]{:S(2)}) copy-start(bf16[8,128]{1,0:T(8,128)(2,1)} %get-tuple-element.15) | copy-start | bytes 6148
  32.6 13.9 %copy-start = (bf16[2,1024,128]{2,1,0:T(8,128)(2,1)S(1)}, bf16[2,1024,128]{2,1,0:T(8,128)(2,1)}, u32[]{:S(2)}) copy-start(bf16[2,1024,128]{2,1,0:T(8,128)(2,1)} %param.13) | copy-start | bytes 1572868
  32.6 44.5 %all-to-all-start.1 = ((bf16[64,72,128]{2,1,0:T(8,128)(2,1)}), bf16[64,72,128]{2,1,0:T(8,128)(2,1)S(1)}, u32[]{:S(2)}, u32[]{:S(2)}) async-start(bf16[64,72,128]{2,1,0:T(8,128)(2,1)} %bitcast.13), calls=%async_computation.1 | async-start | bytes 2359296 | tf_op jit(solution)/shard_map/all_to_all | solution.py:139
  46.6 14.3 %collective-permute-start.2 = (bf16[1024,128]{1,0:T(8,128)(2,1)S(1)}, bf16[1024,128]{1,0:T(8,128)(2,1)S(1)}, u32[]{:S(2)}, u32[]{:S(2)}) collective-permute-start(bf16[1024,128]{1,0:T(8,128)(2,1)S(1)} %get-tuple-element.20), channel_id=1, source_target_pairs={{6,0},{0,2},{2,4},{4,6},{7,1},{1,3},{3,5},{5,7},{14,8},{8,10},{10,... | collective-permute-start | bytes 786440 | tf_op jit(solution)/shard_map/ppermute | solution.py:101
  49.9 13.1 %collective-permute-start.1 = (bf16[1024,128]{1,0:T(8,128)(2,1)S(1)}, bf16[1024,128]{1,0:T(8,128)(2,1)S(1)}, u32[]{:S(2)}, u32[]{:S(2)}) collective-permute-start(bf16[1024,128]{1,0:T(8,128)(2,1)S(1)} %get-tuple-element.20), channel_id=1, source_target_pairs={{2,0},{4,2},{6,4},{0,6},{3,1},{5,3},{7,5},{1,7},{10,8},{12,10},{14... | collective-permute-start | bytes 786440 | tf_op jit(solution)/shard_map/ppermute | solution.py:101
  63.1 6.2 %collective-permute-start.3 = (bf16[4,1024,128]{2,1,0:T(8,128)(2,1)S(1)}, bf16[4,1024,128]{2,1,0:T(8,128)(2,1)S(1)}, u32[]{:S(2)}, u32[]{:S(2)}) collective-permute-start(bf16[4,1024,128]{2,1,0:T(8,128)(2,1)S(1)} %pad_maximum_fusion.near_ref), channel_id=1, source_target_pairs={{0,1},{1,0},{2,3},{3,2},{4,5},{5,4},{6,7},{7,6},{8,9},{9,8},{10,11... | collective-permute-start | bytes 3145736 | tf_op jit(solution)/shard_map/ppermute | solution.py:118
  79.3 35.4 %all-to-all-start.2 = ((bf16[8,512,128]{2,1,0:T(8,128)(2,1)}), bf16[8,512,128]{2,1,0:T(8,128)(2,1)S(1)}, u32[]{:S(2)}, u32[]{:S(2)}) async-start(bf16[8,512,128]{2,1,0:T(8,128)(2,1)} %rotate.1), calls=%async_computation.2 | async-start | bytes 2097152 | tf_op jit(solution)/shard_map/all_to_all | solution.py:153
  86.2 1.6 %collective-permute-start.4 = (f32[16,128]{1,0:T(8,128)S(1)}, f32[16,128]{1,0:T(8,128)S(1)}, u32[]{:S(2)}, u32[]{:S(2)}) collective-permute-start(f32[16,128]{1,0:T(8,128)S(1)} %dynamic-slice_bitcast_fusion.1), channel_id=1, source_target_pairs={{0,0},{1,1},{2,2},{3,3},{4,4},{5,5},{6,6},{7,7},{9,8},{8,9},{11,10... | collective-permute-start | bytes 24584 | tf_op jit(solution)/shard_map/ppermute | solution.py:85

commit v11 on v9

--- a/solution.py
+++ b/solution.py
@@ -39,7 +39,7 @@
     sums_ref[...] = jnp.concatenate(terms, axis=0).astype(jnp.bfloat16)
 
 
-def rotate_kernel(parcel_ref, near_ref, far_ref, out_ref, rows_ref):
+def rotate_kernel(parcel_ref, near_ref, far_ref, out_ref, rows_ref, part_ref, sems):
     sources, _, width = parcel_ref.shape
     rows, depth = rows_ref.shape
     across = depth // width
@@ -51,11 +51,17 @@
             rows_ref[top : top + height, left : left + width] = parcel_ref[
                 source, half * height : (half + 1) * height
             ]
+    copies = []
     for shift in range(near_ref.shape[0]):
         columns = jnp.concatenate([near_ref[shift], far_ref[shift]], axis=1)
         product = jnp.dot(rows_ref[...], columns, preferred_element_type=jnp.float32)
-        out_ref[2 * shift] = product[:, :width].astype(jnp.bfloat16)
-        out_ref[2 * shift + 1] = product[:, width:].astype(jnp.bfloat16)
+        part_ref[shift, 0] = product[:, :width].astype(jnp.bfloat16)
+        part_ref[shift, 1] = product[:, width:].astype(jnp.bfloat16)
+        copy = pltpu.make_async_copy(part_ref.at[shift], out_ref.at[shift], sems.at[shift])
+        copy.start()
+        copies.append(copy)
+    for copy in copies:
+        copy.wait()
 
 
 def body(
@@ -142,15 +148,21 @@
     sums = jnp.sum(sums.reshape(-1, MODULES, 3 * width), axis=(0, 2))
     damping = 0.1 * sums / (R * D)
 
+    shape = (n_x, n_c, n_dp * rows_dev, width)
     partial = pl.pallas_call(
         rotate_kernel,
-        out_shape=jax.ShapeDtypeStruct((n_t, n_dp * rows_dev, width), jnp.bfloat16),
+        out_shape=jax.ShapeDtypeStruct(shape, jnp.bfloat16),
         in_specs=[pl.BlockSpec(memory_space=pltpu.VMEM)] * 3,
-        out_specs=pl.BlockSpec(memory_space=pltpu.VMEM),
-        scratch_shapes=[pltpu.VMEM((n_dp * rows_dev, n_f * width), jnp.bfloat16)],
+        out_specs=pl.BlockSpec(memory_space=pl.ANY),
+        scratch_shapes=[
+            pltpu.VMEM((n_dp * rows_dev, n_f * width), jnp.bfloat16),
+            pltpu.VMEM(shape, jnp.bfloat16),
+            pltpu.SemaphoreType.DMA((n_x,)),
+        ],
         compiler_params=pltpu.CompilerParams(vmem_limit_bytes=32 << 20),
         name="rotate",
     )(parcel, near, far)
+    partial = partial.reshape((n_t,) + shape[2:])
     partial = lax.all_to_all(partial, "tensor", 0, 0, tiled=True)
     rotated = jnp.sum(partial.astype(jnp.float32), axis=0)
     rotated = rotated.reshape(2, n_dp * CAND_DEV, a_rows, width)

time: 135 us -> 135 us (level)
  no operation moved by 1% of the time
where the time goes in v11:
time: 135 us; the launch traced here: 134 us
  waiting for transfers between devices  52.9 us (39%)
  starting transfers between devices  41.7 us (31%)
  blocking collectives  25.4 us (19%)
  other arithmetic  4.7 us (3%)
  local copies, waits for them, and re-layouts  4.33 us (3%)
  Pallas kernels  3.85 us (3%)
    all_to_all x1, waiting for transfers between devices, body(): partial = lax.all_to_all(partial, 'tensor', 0, 0, tiled=True)  26 us
    all_to_all x1, blocking collectives, everywhere(): return lax.all_to_all(terms, axes, 0, 0, tiled=True)  15.3 us
    all_to_all x1, starting transfers between devices, body(): parcel = lax.all_to_all(parcel, ('dp',) + FACTOR, 0, 0, tiled=True)  12.3 us
    ppermute x3, starting transfers between devices, shifted(): return lax.ppermute(value, 'x', [((k + step) % n_x, k) for k in range(n_x)])  12 us
    all_gather x1, blocking collectives, body(): lax.all_gather(scores.reshape(2, -1), FACTOR, axis=0)  10.2 us
    ppermute x3, waiting for transfers between devices, shifted(): return lax.ppermute(value, 'x', [((k + step) % n_x, k) for k in range(n_x)])  9.82 us
    all_to_all x1, starting transfers between devices, body(): squares = lax.all_to_all(squares, ('tensor',) + FACTOR, 0, 0, tiled=True)  9.32 us
    all_to_all x1, waiting for transfers between devices, body(): parcel = lax.all_to_all(parcel, ('dp',) + FACTOR, 0, 0, tiled=True)  7.85 us
  transfers between devices with their start and end apart: 8, of which 6 were waited for; matrix products, arithmetic and copies ran while one was open for 5% of the time, Pallas kernels for 1%

profile of v11, /device:TPU:1, one launch (start us, length us, event | category | flops | bytes accessed | tf_op | source)
XLA Modules:
  0.0 134.1 jit_solution(8281736951644177967)
XLA Ops:
  0.0 5.5 %collective-permute-start = (bf16[2,1024,128]{2,1,0:T(8,128)(2,1)}, bf16[2,1024,128]{2,1,0:T(8,128)(2,1)S(1)}, u32[]{:S(2)}, u32[]{:S(2)}) collective-permute-start(bf16[2,1024,128]{2,1,0:T(8,128)(2,1)} %param.13), channel_id=1, source_target_pairs={{4,0},{6,2},{0,4},{2,6},{5,1},{7,3},{1,5},{3,7},{12,8},{14,10},{8,... | collective-permute-start | bytes 1572872 | tf_op jit(solution)/shard_map/ppermute | solution.py:107
  5.5 1.7 %prologue.1 = (f32[64,4,128]{2,1,0:T(4,128)}, bf16[8,128]{1,0:T(8,128)(2,1)}) custom-call(bf16[512,128]{1,0:T(8,128)(2,1)} %resid_ref.1, f32[2,64,128]{2,1,0:T(8,128)} %eigen_ref.1), custom_call_target="tpu_custom_call" | custom-call | tf_op jit(solution)/shard_map/prologue/pallas_call | solution.py:93
  7.2 9.3 %all-to-all-start = ((f32[64,4,128]{2,1,0:T(4,128)}), f32[64,4,128]{2,1,0:T(4,128)S(1)}, u32[]{:S(2)}, u32[]{:S(2)}) async-start(f32[64,4,128]{2,1,0:T(4,128)} %get-tuple-element.11), calls=%async_computation | async-start | bytes 262144 | tf_op jit(solution)/shard_map/all_to_all | solution.py:103
  16.5 0.9 convert_element_type.27
  17.5 0.9 copy.32
  19.0 0.7 compare_reduce_fusion.1
  19.7 0.9 select_bitcast_fusion.1
  20.6 7.0 %all-to-all-done = f32[64,4,128]{2,1,0:T(4,128)S(1)} async-done(((f32[64,4,128]{2,1,0:T(4,128)}), f32[64,4,128]{2,1,0:T(4,128)S(1)}, u32[]{:S(2)}, u32[]{:S(2)}) %all-to-all-start) | async-done | bytes 131104 | tf_op jit(solution)/shard_map/all_to_all | solution.py:103
  28.3 1.2 broadcast_in_dim.28
  29.5 12.3 %all-to-all-start.1 = ((bf16[64,72,128]{2,1,0:T(8,128)(2,1)}), bf16[64,72,128]{2,1,0:T(8,128)(2,1)S(1)}, u32[]{:S(2)}, u32[]{:S(2)}) async-start(bf16[64,72,128]{2,1,0:T(8,128)(2,1)} %bitcast.13), calls=%async_computation.1 | async-start | bytes 2359296 | tf_op jit(solution)/shard_map/all_to_all | solution.py:146
  41.9 3.3 %collective-permute-start.2 = (bf16[1024,128]{1,0:T(8,128)(2,1)S(1)}, bf16[1024,128]{1,0:T(8,128)(2,1)S(1)}, u32[]{:S(2)}, u32[]{:S(2)}) collective-permute-start(bf16[1024,128]{1,0:T(8,128)(2,1)S(1)} %get-tuple-element.20), channel_id=1, source_target_pairs={{6,0},{0,2},{2,4},{4,6},{7,1},{1,3},{3,5},{5,7},{14,8},{8,10},{10,... | collective-permute-start | bytes 786440 | tf_op jit(solution)/shard_map/ppermute | solution.py:107
  45.2 3.2 %collective-permute-start.1 = (bf16[1024,128]{1,0:T(8,128)(2,1)S(1)}, bf16[1024,128]{1,0:T(8,128)(2,1)S(1)}, u32[]{:S(2)}, u32[]{:S(2)}) collective-permute-start(bf16[1024,128]{1,0:T(8,128)(2,1)S(1)} %get-tuple-element.20), channel_id=1, source_target_pairs={{2,0},{4,2},{6,4},{0,6},{3,1},{5,3},{7,5},{1,7},{10,8},{12,10},{14... | collective-permute-start | bytes 786440 | tf_op jit(solution)/shard_map/ppermute | solution.py:107
  48.4 7.8 %collective-permute-done.2 = bf16[1024,128]{1,0:T(8,128)(2,1)S(1)} collective-permute-done((bf16[1024,128]{1,0:T(8,128)(2,1)S(1)}, bf16[1024,128]{1,0:T(8,128)(2,1)S(1)}, u32[]{:S(2)}, u32[]{:S(2)}) %collective-permute-start.2) | collective-permute-done | bytes 262176 | tf_op jit(solution)/shard_map/ppermute | solution.py:107
  56.2 2.0 %collective-permute-done.1 = bf16[1024,128]{1,0:T(8,128)(2,1)S(1)} collective-permute-done((bf16[1024,128]{1,0:T(8,128)(2,1)S(1)}, bf16[1024,128]{1,0:T(8,128)(2,1)S(1)}, u32[]{:S(2)}, u32[]{:S(2)}) %collective-permute-start.1) | collective-permute-done | bytes 262176 | tf_op jit(solution)/shard_map/ppermute | solution.py:107
  58.4 3.9 %collective-permute-start.3 = (bf16[4,1024,128]{2,1,0:T(8,128)(2,1)S(1)}, bf16[4,1024,128]{2,1,0:T(8,128)(2,1)S(1)}, u32[]{:S(2)}, u32[]{:S(2)}) collective-permute-start(bf16[4,1024,128]{2,1,0:T(8,128)(2,1)S(1)} %pad_maximum_fusion.near_ref), channel_id=1, source_target_pairs={{0,1},{1,0},{2,3},{3,2},{4,5},{5,4},{6,7},{7,6},{8,9},{9,8},{10,11... | collective-permute-start | bytes 3145736 | tf_op jit(solution)/shard_map/ppermute | solution.py:126
  62.3 2.3 %collective-permute-done.3.far_ref = bf16[4,1024,128]{2,1,0:T(8,128)(2,1)S(1)} collective-permute-done((bf16[4,1024,128]{2,1,0:T(8,128)(2,1)S(1)}, bf16[4,1024,128]{2,1,0:T(8,128)(2,1)S(1)}, u32[]{:S(2)}, u32[]{:S(2)}) %collective-permute-start.3) | collective-permute-done | bytes 1048608 | tf_op jit(solution)/shard_map/ppermute | solution.py:126
  64.6 7.8 %all-to-all-done.1.parcel_ref = bf16[64,72,128]{2,1,0:T(8,128)(2,1)S(1)} async-done(((bf16[64,72,128]{2,1,0:T(8,128)(2,1)}), bf16[64,72,128]{2,1,0:T(8,128)(2,1)S(1)}, u32[]{:S(2)}, u32[]{:S(2)}) %all-to-all-start.1) | async-done | bytes 1179680 | tf_op jit(solution)/shard_map/all_to_all | solution.py:146
  72.4 2.1 %rotate.1 = bf16[4,2,512,128]{3,2,1,0:T(8,128)(2,1)} custom-call(bf16[64,72,128]{2,1,0:T(8,128)(2,1)S(1)} %all-to-all-done.1.parcel_ref, bf16[4,1024,128]{2,1,0:T(8,128)(2,1)S(1)} %pad_maximum_fusion.near_ref, bf16[4,1024,128]{2,1,0:T(8,128)(2,1)S(1)} %collective-permute-done.3.far_ref), custom_call_target="tpu_custom_call" | custom-call | tf_op jit(solution)/shard_map/rotate/pallas_call | solution.py:152
  74.6 3.6 %all-to-all-start.2 = ((bf16[8,512,128]{2,1,0:T(8,128)(2,1)}), bf16[8,512,128]{2,1,0:T(8,128)(2,1)S(1)}, u32[]{:S(2)}, u32[]{:S(2)}) async-start(bf16[8,512,128]{2,1,0:T(8,128)(2,1)} %bitcast.17), calls=%async_computation.2 | async-start | bytes 2097152 | tf_op jit(solution)/shard_map/all_to_all | solution.py:166
  78.2 0.7 dynamic-slice_bitcast_fusion.1
  81.2 26.0 %all-to-all-done.2 = bf16[8,512,128]{2,1,0:T(8,128)(2,1)S(1)} async-done(((bf16[8,512,128]{2,1,0:T(8,128)(2,1)}), bf16[8,512,128]{2,1,0:T(8,128)(2,1)S(1)}, u32[]{:S(2)}, u32[]{:S(2)}) %all-to-all-start.2) | async-done | bytes 1048608 | tf_op jit(solution)/shard_map/all_to_all | solution.py:166
  107.8 10.2 %all_gather.3 = f32[8,2,128]{2,1,0:T(2,128)S(1)} all-gather(f32[1,2,128]{2,1,0:T(2,128)S(1)} %all_gather_reshape.3), channel_id=1, replica_groups=mesh['dp'=8,'tensor'=8,'x'=4,'core'=2] {'x','core'}, dimensions={0}, use_global_device_ids=true | all-gather | bytes 9216 | tf_op jit(solution)/shard_map/all_gather | solution.py:175
  118.0 15.3 %all_to_all.20 = f32[64,2,128]{2,1,0:T(2,128)S(1)} all-to-all(f32[64,2,128]{2,1,0:T(2,128)S(1)} %broadcast_in_dim.29), channel_id=1, replica_groups=mesh['dp'=8,'tensor'=8,'x'=4,'core'=2] {'dp','tensor'}, dimensions={0} | all-to-all | bytes 131072 | tf_op jit(solution)/shard_map/all_to_all | solution.py:21
  133.4 0.7 reshape.51
  (34 shorter events, 4.5 us)
Async XLA Ops:
  0.0 27.7 %collective-permute-start = (bf16[2,1024,128]{2,1,0:T(8,128)(2,1)}, bf16[2,1024,128]{2,1,0:T(8,128)(2,1)S(1)}, u32[]{:S(2)}, u32[]{:S(2)}) collective-permute-start(bf16[2,1024,128]{2,1,0:T(8,128)(2,1)} %param.13), channel_id=1, source_target_pairs={{4,0},{6,2},{0,4},{2,6},{5,1},{7,3},{1,5},{3,7},{12,8},{14,10},{8,... | collective-permute-start | bytes 1572872 | tf_op jit(solution)/shard_map/ppermute | solution.py:107
  7.2 20.9 %copy-start.2 = (bf16[2,2,64,128]{3,2,1,0:T(8,128)(2,1)S(1)}, bf16[2,2,64,128]{3,2,1,0:T(8,128)(2,1)}, u32[]{:S(2)}) copy-start(bf16[2,2,64,128]{3,2,1,0:T(8,128)(2,1)} %param.12) | copy-start | bytes 196612
  7.2 20.4 %all-to-all-start = ((f32[64,4,128]{2,1,0:T(4,128)}), f32[64,4,128]{2,1,0:T(4,128)S(1)}, u32[]{:S(2)}, u32[]{:S(2)}) async-start(f32[64,4,128]{2,1,0:T(4,128)} %get-tuple-element.11), calls=%async_computation | async-start | bytes 262144 | tf_op jit(solution)/shard_map/all_to_all | solution.py:103
  17.4 10.8 %copy-start.1 = (bf16[8,128]{1,0:T(8,128)(2,1)S(1)}, bf16[8,128]{1,0:T(8,128)(2,1)}, u32[]{:S(2)}) copy-start(bf16[8,128]{1,0:T(8,128)(2,1)} %get-tuple-element.15) | copy-start | bytes 6148
  29.5 12.4 %copy-start = (bf16[2,1024,128]{2,1,0:T(8,128)(2,1)S(1)}, bf16[2,1024,128]{2,1,0:T(8,128)(2,1)}, u32[]{:S(2)}) copy-start(bf16[2,1024,128]{2,1,0:T(8,128)(2,1)} %param.13) | copy-start | bytes 1572868
  29.5 42.9 %all-to-all-start.1 = ((bf16[64,72,128]{2,1,0:T(8,128)(2,1)}), bf16[64,72,128]{2,1,0:T(8,128)(2,1)S(1)}, u32[]{:S(2)}, u32[]{:S(2)}) async-start(bf16[64,72,128]{2,1,0:T(8,128)(2,1)} %bitcast.13), calls=%async_computation.1 | async-start | bytes 2359296 | tf_op jit(solution)/shard_map/all_to_all | solution.py:146
  41.9 14.3 %collective-permute-start.2 = (bf16[1024,128]{1,0:T(8,128)(2,1)S(1)}, bf16[1024,128]{1,0:T(8,128)(2,1)S(1)}, u32[]{:S(2)}, u32[]{:S(2)}) collective-permute-start(bf16[1024,128]{1,0:T(8,128)(2,1)S(1)} %get-tuple-element.20), channel_id=1, source_target_pairs={{6,0},{0,2},{2,4},{4,6},{7,1},{1,3},{3,5},{5,7},{14,8},{8,10},{10,... | collective-permute-start | bytes 786440 | tf_op jit(solution)/shard_map/ppermute | solution.py:107
  45.2 13.1 %collective-permute-start.1 = (bf16[1024,128]{1,0:T(8,128)(2,1)S(1)}, bf16[1024,128]{1,0:T(8,128)(2,1)S(1)}, u32[]{:S(2)}, u32[]{:S(2)}) collective-permute-start(bf16[1024,128]{1,0:T(8,128)(2,1)S(1)} %get-tuple-element.20), channel_id=1, source_target_pairs={{2,0},{4,2},{6,4},{0,6},{3,1},{5,3},{7,5},{1,7},{10,8},{12,10},{14... | collective-permute-start | bytes 786440 | tf_op jit(solution)/shard_map/ppermute | solution.py:107
  58.4 6.2 %collective-permute-start.3 = (bf16[4,1024,128]{2,1,0:T(8,128)(2,1)S(1)}, bf16[4,1024,128]{2,1,0:T(8,128)(2,1)S(1)}, u32[]{:S(2)}, u32[]{:S(2)}) collective-permute-start(bf16[4,1024,128]{2,1,0:T(8,128)(2,1)S(1)} %pad_maximum_fusion.near_ref), channel_id=1, source_target_pairs={{0,1},{1,0},{2,3},{3,2},{4,5},{5,4},{6,7},{7,6},{8,9},{9,8},{10,11... | collective-permute-start | bytes 3145736 | tf_op jit(solution)/shard_map/ppermute | solution.py:126
  74.6 32.7 %all-to-all-start.2 = ((bf16[8,512,128]{2,1,0:T(8,128)(2,1)}), bf16[8,512,128]{2,1,0:T(8,128)(2,1)S(1)}, u32[]{:S(2)}, u32[]{:S(2)}) async-start(bf16[8,512,128]{2,1,0:T(8,128)(2,1)} %bitcast.17), calls=%async_computation.2 | async-start | bytes 2097152 | tf_op jit(solution)/shard_map/all_to_all | solution.py:166
  78.9 1.6 %collective-permute-start.4 = (f32[16,128]{1,0:T(8,128)S(1)}, f32[16,128]{1,0:T(8,128)S(1)}, u32[]{:S(2)}, u32[]{:S(2)}) collective-permute-start(f32[16,128]{1,0:T(8,128)S(1)} %dynamic-slice_bitcast_fusion.1), channel_id=1, source_target_pairs={{0,0},{1,1},{2,2},{3,3},{4,4},{5,5},{6,6},{7,7},{9,8},{8,9},{11,10... | collective-permute-start | bytes 24584 | tf_op jit(solution)/shard_map/ppermute | solution.py:91

commit v12 on v11

--- a/solution.py
+++ b/solution.py
@@ -100,7 +100,7 @@
         out_specs=[pl.BlockSpec(memory_space=pltpu.VMEM)] * 2,
         name="prologue",
     )(resid, eigenvalues)
-    squares = lax.all_to_all(squares, ("tensor",) + FACTOR, 0, 0, tiled=True)
+    squares = lax.all_to_all(squares, FACTOR + ("tensor",), 0, 0, tiled=True)
     totals = jnp.sum(squares, axis=0).reshape(-1)
 
     def shifted(value, step):
@@ -173,7 +173,7 @@
     )
     shape = scores.shape
     scores = jnp.sum(lax.all_gather(scores.reshape(2, -1), FACTOR, axis=0), axis=0)
-    return jnp.sum(everywhere(scores, ("dp", "tensor")), axis=0).reshape(shape)
+    return jnp.sum(everywhere(scores, ("tensor", "dp")), axis=0).reshape(shape)
 
 
 def solution(mesh):

time: 135 us -> 135 us (level)
  starting transfers between devices: 41.7 us -> 43.2 us
    all_to_all x1, starting transfers between devices: 12.3 us -> 13.8 us  [body(): parcel = lax.all_to_all(parcel, ('dp',) + FACTOR, 0, 0, tiled=True)]
where the time goes in v12:
time: 135 us; the launch traced here: 134 us
  waiting for transfers between devices  51.8 us (38%)
  starting transfers between devices  43.2 us (32%)
  blocking collectives  25.5 us (19%)
  other arithmetic  4.7 us (3%)
  local copies, waits for them, and re-layouts  4.33 us (3%)
  Pallas kernels  3.84 us (3%)
    all_to_all x1, waiting for transfers between devices, body(): partial = lax.all_to_all(partial, 'tensor', 0, 0, tiled=True)  26 us
    all_to_all x1, blocking collectives, everywhere(): return lax.all_to_all(terms, axes, 0, 0, tiled=True)  15.3 us
    all_to_all x1, starting transfers between devices, body(): parcel = lax.all_to_all(parcel, ('dp',) + FACTOR, 0, 0, tiled=True)  13.8 us
    ppermute x3, starting transfers between devices, shifted(): return lax.ppermute(value, 'x', [((k + step) % n_x, k) for k in range(n_x)])  12 us
    all_gather x1, blocking collectives, body(): lax.all_gather(scores.reshape(2, -1), FACTOR, axis=0)  10.2 us
    ppermute x3, waiting for transfers between devices, shifted(): return lax.ppermute(value, 'x', [((k + step) % n_x, k) for k in range(n_x)])  9.82 us
    all_to_all x1, starting transfers between devices, body(): squares = lax.all_to_all(squares, FACTOR + ('tensor',), 0, 0, tiled=True)  9.32 us
    all_to_all x1, waiting for transfers between devices, body(): parcel = lax.all_to_all(parcel, ('dp',) + FACTOR, 0, 0, tiled=True)  7.85 us
  transfers between devices with their start and end apart: 8, of which 6 were waited for; matrix products, arithmetic and copies ran while one was open for 5% of the time, Pallas kernels for 1%

profile of v12, /device:TPU:1, one launch (start us, length us, event | category | flops | bytes accessed | tf_op | source)
XLA Modules:
  0.0 134.4 jit_solution(13960745508326217135)
XLA Ops:
  0.0 5.5 %collective-permute-start = (bf16[2,1024,128]{2,1,0:T(8,128)(2,1)}, bf16[2,1024,128]{2,1,0:T(8,128)(2,1)S(1)}, u32[]{:S(2)}, u32[]{:S(2)}) collective-permute-start(bf16[2,1024,128]{2,1,0:T(8,128)(2,1)} %param.13), channel_id=1, source_target_pairs={{4,0},{6,2},{0,4},{2,6},{5,1},{7,3},{1,5},{3,7},{12,8},{14,10},{8,... | collective-permute-start | bytes 1572872 | tf_op jit(solution)/shard_map/ppermute | solution.py:107
  5.5 1.7 %prologue.1 = (f32[64,4,128]{2,1,0:T(4,128)}, bf16[8,128]{1,0:T(8,128)(2,1)}) custom-call(bf16[512,128]{1,0:T(8,128)(2,1)} %resid_ref.1, f32[2,64,128]{2,1,0:T(8,128)} %eigen_ref.1), custom_call_target="tpu_custom_call" | custom-call | tf_op jit(solution)/shard_map/prologue/pallas_call | solution.py:93
  7.2 9.3 %all-to-all-start = ((f32[64,4,128]{2,1,0:T(4,128)}), f32[64,4,128]{2,1,0:T(4,128)S(1)}, u32[]{:S(2)}, u32[]{:S(2)}) async-start(f32[64,4,128]{2,1,0:T(4,128)} %get-tuple-element.11), calls=%async_computation | async-start | bytes 262144 | tf_op jit(solution)/shard_map/all_to_all | solution.py:103
  16.5 0.9 convert_element_type.27
  17.5 0.9 copy.32
  19.0 0.7 compare_reduce_fusion.1
  19.7 0.9 select_bitcast_fusion.1
  20.7 5.8 %all-to-all-done = f32[64,4,128]{2,1,0:T(4,128)S(1)} async-done(((f32[64,4,128]{2,1,0:T(4,128)}), f32[64,4,128]{2,1,0:T(4,128)S(1)}, u32[]{:S(2)}, u32[]{:S(2)}) %all-to-all-start) | async-done | bytes 131104 | tf_op jit(solution)/shard_map/all_to_all | solution.py:103
  27.2 1.2 broadcast_in_dim.28
  28.3 13.8 %all-to-all-start.1 = ((bf16[64,72,128]{2,1,0:T(8,128)(2,1)}), bf16[64,72,128]{2,1,0:T(8,128)(2,1)S(1)}, u32[]{:S(2)}, u32[]{:S(2)}) async-start(bf16[64,72,128]{2,1,0:T(8,128)(2,1)} %bitcast.13), calls=%async_computation.1 | async-start | bytes 2359296 | tf_op jit(solution)/shard_map/all_to_all | solution.py:146
  42.2 3.3 %collective-permute-start.2 = (bf16[1024,128]{1,0:T(8,128)(2,1)S(1)}, bf16[1024,128]{1,0:T(8,128)(2,1)S(1)}, u32[]{:S(2)}, u32[]{:S(2)}) collective-permute-start(bf16[1024,128]{1,0:T(8,128)(2,1)S(1)} %get-tuple-element.20), channel_id=1, source_target_pairs={{6,0},{0,2},{2,4},{4,6},{7,1},{1,3},{3,5},{5,7},{14,8},{8,10},{10,... | collective-permute-start | bytes 786440 | tf_op jit(solution)/shard_map/ppermute | solution.py:107
  45.5 3.2 %collective-permute-start.1 = (bf16[1024,128]{1,0:T(8,128)(2,1)S(1)}, bf16[1024,128]{1,0:T(8,128)(2,1)S(1)}, u32[]{:S(2)}, u32[]{:S(2)}) collective-permute-start(bf16[1024,128]{1,0:T(8,128)(2,1)S(1)} %get-tuple-element.20), channel_id=1, source_target_pairs={{2,0},{4,2},{6,4},{0,6},{3,1},{5,3},{7,5},{1,7},{10,8},{12,10},{14... | collective-permute-start | bytes 786440 | tf_op jit(solution)/shard_map/ppermute | solution.py:107
  48.8 7.8 %collective-permute-done.2 = bf16[1024,128]{1,0:T(8,128)(2,1)S(1)} collective-permute-done((bf16[1024,128]{1,0:T(8,128)(2,1)S(1)}, bf16[1024,128]{1,0:T(8,128)(2,1)S(1)}, u32[]{:S(2)}, u32[]{:S(2)}) %collective-permute-start.2) | collective-permute-done | bytes 262176 | tf_op jit(solution)/shard_map/ppermute | solution.py:107
  56.5 2.0 %collective-permute-done.1 = bf16[1024,128]{1,0:T(8,128)(2,1)S(1)} collective-permute-done((bf16[1024,128]{1,0:T(8,128)(2,1)S(1)}, bf16[1024,128]{1,0:T(8,128)(2,1)S(1)}, u32[]{:S(2)}, u32[]{:S(2)}) %collective-permute-start.1) | collective-permute-done | bytes 262176 | tf_op jit(solution)/shard_map/ppermute | solution.py:107
  58.7 3.9 %collective-permute-start.3 = (bf16[4,1024,128]{2,1,0:T(8,128)(2,1)S(1)}, bf16[4,1024,128]{2,1,0:T(8,128)(2,1)S(1)}, u32[]{:S(2)}, u32[]{:S(2)}) collective-permute-start(bf16[4,1024,128]{2,1,0:T(8,128)(2,1)S(1)} %pad_maximum_fusion.near_ref), channel_id=1, source_target_pairs={{0,1},{1,0},{2,3},{3,2},{4,5},{5,4},{6,7},{7,6},{8,9},{9,8},{10,11... | collective-permute-start | bytes 3145736 | tf_op jit(solution)/shard_map/ppermute | solution.py:126
  62.6 2.3 %collective-permute-done.3.far_ref = bf16[4,1024,128]{2,1,0:T(8,128)(2,1)S(1)} collective-permute-done((bf16[4,1024,128]{2,1,0:T(8,128)(2,1)S(1)}, bf16[4,1024,128]{2,1,0:T(8,128)(2,1)S(1)}, u32[]{:S(2)}, u32[]{:S(2)}) %collective-permute-start.3) | collective-permute-done | bytes 1048608 | tf_op jit(solution)/shard_map/ppermute | solution.py:126
  64.9 7.8 %all-to-all-done.1.parcel_ref = bf16[64,72,128]{2,1,0:T(8,128)(2,1)S(1)} async-done(((bf16[64,72,128]{2,1,0:T(8,128)(2,1)}), bf16[64,72,128]{2,1,0:T(8,128)(2,1)S(1)}, u32[]{:S(2)}, u32[]{:S(2)}) %all-to-all-start.1) | async-done | bytes 1179680 | tf_op jit(solution)/shard_map/all_to_all | solution.py:146
  72.7 2.1 %rotate.1 = bf16[4,2,512,128]{3,2,1,0:T(8,128)(2,1)} custom-call(bf16[64,72,128]{2,1,0:T(8,128)(2,1)S(1)} %all-to-all-done.1.parcel_ref, bf16[4,1024,128]{2,1,0:T(8,128)(2,1)S(1)} %pad_maximum_fusion.near_ref, bf16[4,1024,128]{2,1,0:T(8,128)(2,1)S(1)} %collective-permute-done.3.far_ref), custom_call_target="tpu_custom_call" | custom-call | tf_op jit(solution)/shard_map/rotate/pallas_call | solution.py:152
  74.9 3.6 %all-to-all-start.2 = ((bf16[8,512,128]{2,1,0:T(8,128)(2,1)}), bf16[8,512,128]{2,1,0:T(8,128)(2,1)S(1)}, u32[]{:S(2)}, u32[]{:S(2)}) async-start(bf16[8,512,128]{2,1,0:T(8,128)(2,1)} %bitcast.17), calls=%async_computation.2 | async-start | bytes 2097152 | tf_op jit(solution)/shard_map/all_to_all | solution.py:166
  78.5 0.7 dynamic-slice_bitcast_fusion.1
  81.5 26.0 %all-to-all-done.2 = bf16[8,512,128]{2,1,0:T(8,128)(2,1)S(1)} async-done(((bf16[8,512,128]{2,1,0:T(8,128)(2,1)}), bf16[8,512,128]{2,1,0:T(8,128)(2,1)S(1)}, u32[]{:S(2)}, u32[]{:S(2)}) %all-to-all-start.2) | async-done | bytes 1048608 | tf_op jit(solution)/shard_map/all_to_all | solution.py:166
  108.1 10.2 %all_gather.3 = f32[8,2,128]{2,1,0:T(2,128)S(1)} all-gather(f32[1,2,128]{2,1,0:T(2,128)S(1)} %all_gather_reshape.3), channel_id=1, replica_groups=mesh['dp'=8,'tensor'=8,'x'=4,'core'=2] {'x','core'}, dimensions={0}, use_global_device_ids=true | all-gather | bytes 9216 | tf_op jit(solution)/shard_map/all_gather | solution.py:175
  118.4 15.3 %all_to_all.20 = f32[64,2,128]{2,1,0:T(2,128)S(1)} all-to-all(f32[64,2,128]{2,1,0:T(2,128)S(1)} %broadcast_in_dim.29), channel_id=1, replica_groups=mesh['dp'=8,'tensor'=8,'x'=4,'core'=2] {'tensor','dp'}, dimensions={0} | all-to-all | bytes 131072 | tf_op jit(solution)/shard_map/all_to_all | solution.py:21
  133.8 0.7 reshape.51
  (34 shorter events, 4.5 us)
Async XLA Ops:
  0.0 26.6 %collective-permute-start = (bf16[2,1024,128]{2,1,0:T(8,128)(2,1)}, bf16[2,1024,128]{2,1,0:T(8,128)(2,1)S(1)}, u32[]{:S(2)}, u32[]{:S(2)}) collective-permute-start(bf16[2,1024,128]{2,1,0:T(8,128)(2,1)} %param.13), channel_id=1, source_target_pairs={{4,0},{6,2},{0,4},{2,6},{5,1},{7,3},{1,5},{3,7},{12,8},{14,10},{8,... | collective-permute-start | bytes 1572872 | tf_op jit(solution)/shard_map/ppermute | solution.py:107
  7.2 19.7 %copy-start.2 = (bf16[2,2,64,128]{3,2,1,0:T(8,128)(2,1)S(1)}, bf16[2,2,64,128]{3,2,1,0:T(8,128)(2,1)}, u32[]{:S(2)}) copy-start(bf16[2,2,64,128]{3,2,1,0:T(8,128)(2,1)} %param.12) | copy-start | bytes 196612
  7.2 19.3 %all-to-all-start = ((f32[64,4,128]{2,1,0:T(4,128)}), f32[64,4,128]{2,1,0:T(4,128)S(1)}, u32[]{:S(2)}, u32[]{:S(2)}) async-start(f32[64,4,128]{2,1,0:T(4,128)} %get-tuple-element.11), calls=%async_computation | async-start | bytes 262144 | tf_op jit(solution)/shard_map/all_to_all | solution.py:103
  17.4 9.7 %copy-start.1 = (bf16[8,128]{1,0:T(8,128)(2,1)S(1)}, bf16[8,128]{1,0:T(8,128)(2,1)}, u32[]{:S(2)}) copy-start(bf16[8,128]{1,0:T(8,128)(2,1)} %get-tuple-element.15) | copy-start | bytes 6148
  28.3 13.8 %copy-start = (bf16[2,1024,128]{2,1,0:T(8,128)(2,1)S(1)}, bf16[2,1024,128]{2,1,0:T(8,128)(2,1)}, u32[]{:S(2)}) copy-start(bf16[2,1024,128]{2,1,0:T(8,128)(2,1)} %param.13) | copy-start | bytes 1572868
  28.3 44.4 %all-to-all-start.1 = ((bf16[64,72,128]{2,1,0:T(8,128)(2,1)}), bf16[64,72,128]{2,1,0:T(8,128)(2,1)S(1)}, u32[]{:S(2)}, u32[]{:S(2)}) async-start(bf16[64,72,128]{2,1,0:T(8,128)(2,1)} %bitcast.13), calls=%async_computation.1 | async-start | bytes 2359296 | tf_op jit(solution)/shard_map/all_to_all | solution.py:146
  42.2 14.3 %collective-permute-start.2 = (bf16[1024,128]{1,0:T(8,128)(2,1)S(1)}, bf16[1024,128]{1,0:T(8,128)(2,1)S(1)}, u32[]{:S(2)}, u32[]{:S(2)}) collective-permute-start(bf16[1024,128]{1,0:T(8,128)(2,1)S(1)} %get-tuple-element.20), channel_id=1, source_target_pairs={{6,0},{0,2},{2,4},{4,6},{7,1},{1,3},{3,5},{5,7},{14,8},{8,10},{10,... | collective-permute-start | bytes 786440 | tf_op jit(solution)/shard_map/ppermute | solution.py:107
  45.5 13.1 %collective-permute-start.1 = (bf16[1024,128]{1,0:T(8,128)(2,1)S(1)}, bf16[1024,128]{1,0:T(8,128)(2,1)S(1)}, u32[]{:S(2)}, u32[]{:S(2)}) collective-permute-start(bf16[1024,128]{1,0:T(8,128)(2,1)S(1)} %get-tuple-element.20), channel_id=1, source_target_pairs={{2,0},{4,2},{6,4},{0,6},{3,1},{5,3},{7,5},{1,7},{10,8},{12,10},{14... | collective-permute-start | bytes 786440 | tf_op jit(solution)/shard_map/ppermute | solution.py:107
  58.7 6.2 %collective-permute-start.3 = (bf16[4,1024,128]{2,1,0:T(8,128)(2,1)S(1)}, bf16[4,1024,128]{2,1,0:T(8,128)(2,1)S(1)}, u32[]{:S(2)}, u32[]{:S(2)}) collective-permute-start(bf16[4,1024,128]{2,1,0:T(8,128)(2,1)S(1)} %pad_maximum_fusion.near_ref), channel_id=1, source_target_pairs={{0,1},{1,0},{2,3},{3,2},{4,5},{5,4},{6,7},{7,6},{8,9},{9,8},{10,11... | collective-permute-start | bytes 3145736 | tf_op jit(solution)/shard_map/ppermute | solution.py:126
  74.9 32.7 %all-to-all-start.2 = ((bf16[8,512,128]{2,1,0:T(8,128)(2,1)}), bf16[8,512,128]{2,1,0:T(8,128)(2,1)S(1)}, u32[]{:S(2)}, u32[]{:S(2)}) async-start(bf16[8,512,128]{2,1,0:T(8,128)(2,1)} %bitcast.17), calls=%async_computation.2 | async-start | bytes 2097152 | tf_op jit(solution)/shard_map/all_to_all | solution.py:166
  79.2 1.6 %collective-permute-start.4 = (f32[16,128]{1,0:T(8,128)S(1)}, f32[16,128]{1,0:T(8,128)S(1)}, u32[]{:S(2)}, u32[]{:S(2)}) collective-permute-start(f32[16,128]{1,0:T(8,128)S(1)} %dynamic-slice_bitcast_fusion.1), channel_id=1, source_target_pairs={{0,0},{1,1},{2,2},{3,3},{4,4},{5,5},{6,6},{7,7},{9,8},{8,9},{11,10... | collective-permute-start | bytes 24584 | tf_op jit(solution)/shard_map/ppermute | solution.py:91
